TPU v7x, 32 devices: a whole 2x2x4 slice. The times are simulated.
32 devices in a mesh: head: 4 (over z), seq: 8 (over y, x, core).
Axes of the slice: x: 2, y: 2, z: 4, core: 2. Of those that a mesh axis runs over, the one named last changes fastest.
Arguments:
- inputs: bfloat16 [2048, 2048], P('seq', 'head'), may hold values from -6 to 6
- cotangent: bfloat16 [2048, 2048], P('seq', 'head'), may hold values from -6 to 6
- owners: int32 [261], replicated, may hold values from 0 to 7, as said below
- master: float32 [352, 262144], P('seq', 'head'), may hold values from -16 to 16
- moment_one: float32 [352, 262144], P('seq', 'head')
- moment_two: float32 [352, 262144], P('seq', 'head'), as said below
Outputs:
- block_out: bfloat16 [2048, 2048], P('seq', 'head')
- input_grad: float32 [2048, 2048], P('seq', 'head')
- grad_slots: float32 [352, 262144], P('seq', 'head')
- master_new: float32 [352, 262144], P('seq', 'head')
- moment_one_new: float32 [352, 262144], P('seq', 'head')
- moment_two_new: float32 [352, 262144], P('seq', 'head')
- weights_low: bfloat16 [352, 262144], P('seq', 'head')
Inputs may be any that keep to these rules, and one draw needn't show every extreme that they name: owners[p] is the index along seq of the device that keeps block p of every head shard; no index appears more than 44 times and some index exactly 44 times. `moment_two`: every entry is positive.
All inputs are finite; a program needn't handle non-finite values.
Results may differ from a plain program's by a relative error of at most 0.019.
Values may be sent and summed in bfloat16 or wider, within the bound.
No kernel may reach another device: no remote copies, remote signals or barrier semaphores. Data moves between devices by JAX's collectives and lax.ppermute only.
A program may use at most 1.1875 GiB of HBM per device.

v0:
```python
import jax
import jax.numpy as jnp
import numpy as np
from jax import lax
from jax.sharding import PartitionSpec as P

D = 2048
HEADS = 16
DK = 128
DV = 256
FF = 5632
KCONV = 4
GROUP = 64
STEP = 5


EXACT_ARITHMETIC = lax.Precision.HIGHEST
NORM_EPSILON = 1e-06
UNIT_EPSILON = 1e-06
HEAD_EPSILON = 1e-05
ADAM_EPSILON = 1e-08
BETA_ONE = 0.5
BETA_TWO = 0.5
WEIGHT_DECAY = 0.1
PAD_RATE = 0.1


def shifted(block, axis, distance):
    devices = range(lax.axis_size(axis))
    route = [(i - distance, i) for i in devices if i - distance in devices]
    return lax.ppermute(block, axis, route)


def shard_layout(local_heads, head_parts):
    return [
        ("wq", D, local_heads * DK, 0.02),
        ("wk", D, local_heads * DK, 0.02),
        ("wv", D, local_heads * DV, 0.02),
        ("wg", D, local_heads * DV, 0.02),
        ("wo", local_heads * DV, D, 0.015),
        ("wgate", D, FF // head_parts, 0.02),
        ("wup", D, FF // head_parts, 0.02),
        ("wdown", FF // head_parts, D, 0.012),
        ("cq", KCONV, local_heads * DK, 0.4),
        ("ck", KCONV, local_heads * DK, 0.4),
        ("cv", KCONV, local_heads * DV, 0.4),
        ("wab", D, 2 * local_heads, 0.04),
        ("alog", 1, local_heads, 0.5),
        ("dtbias", 1, local_heads, 0.5),
        ("gainone", 1, D // head_parts, 0.1),
        ("gaintwo", 1, D // head_parts, 0.1),
        ("wnorm", 1, DV // head_parts, 0.1),
    ]


def piece_table(owners, seq_parts, capacity):
    piece_count = owners.shape[0]
    devices = jnp.arange(seq_parts, dtype=jnp.int32)
    onehot = (owners[:, None] == devices[None, :]).astype(jnp.int32)
    before = jnp.cumsum(onehot, axis=0) - onehot
    rank_within = jnp.sum(before * onehot, axis=1)
    slot_of_piece = owners * capacity + rank_within
    matches = slot_of_piece[None, :] == jnp.arange(seq_parts * capacity, dtype=jnp.int32)[:, None]
    present = jnp.any(matches, axis=1)
    piece_of_slot = jnp.sum(
        matches.astype(jnp.int32) * jnp.arange(piece_count, dtype=jnp.int32)[None, :], axis=1
    )
    return (slot_of_piece, piece_of_slot, present)


def unpack(flat_weights, segments_list):
    by_name = {}
    offset_now = 0
    for seg_name, row_count, col_count, seg_rate in segments_list:
        by_name[seg_name] = flat_weights[offset_now : offset_now + row_count * col_count].reshape(
            row_count, col_count
        )
        offset_now += row_count * col_count
    return (by_name, offset_now)


def rate_parts(segments_list, piece_count, piece_size):
    piece_rates = np.full(piece_count, PAD_RATE, np.float32)
    small_rates = np.full(piece_size, PAD_RATE, np.float32)
    offset_now = 0
    big_total = (piece_count - 1) * piece_size
    for seg_name, row_count, col_count, seg_rate in segments_list:
        seg_size = row_count * col_count
        if offset_now < big_total:
            piece_rates[offset_now // piece_size : (offset_now + seg_size) // piece_size] = seg_rate
        else:
            small_rates[offset_now - big_total : offset_now - big_total + seg_size] = seg_rate
        offset_now += seg_size
    return (piece_rates, small_rates)


def prepare(
    query_ext, key_ext, value_ext, decay_proj, conv_query, conv_key, conv_value, log_rate, rate_bias
):
    local_heads = decay_proj.shape[1] // 2
    row_count = decay_proj.shape[0]

    def convolve(extended, conv_taps):
        running = conv_taps[0] * extended[0:row_count]
        for tap_number in range(1, KCONV):
            running = (
                running + conv_taps[tap_number] * extended[tap_number : tap_number + row_count]
            )
        return jax.nn.silu(running)

    queries = convolve(query_ext, conv_query).reshape(row_count, local_heads, DK)
    queries = (
        queries
        * lax.rsqrt(jnp.sum(queries * queries, axis=-1, keepdims=True) + UNIT_EPSILON)
        * DK ** (-0.5)
    )
    key_rows = convolve(key_ext, conv_key).reshape(row_count, local_heads, DK)
    key_rows = key_rows * lax.rsqrt(
        jnp.sum(key_rows * key_rows, axis=-1, keepdims=True) + UNIT_EPSILON
    )
    values = convolve(value_ext, conv_value).reshape(row_count, local_heads, DV)
    betas = jax.nn.sigmoid(decay_proj[:, local_heads:])
    decays = -jnp.exp(log_rate) * jax.nn.softplus(decay_proj[:, :local_heads] + rate_bias)
    return (
        jnp.transpose(queries, (1, 0, 2)),
        jnp.transpose(key_rows, (1, 0, 2)),
        jnp.transpose(values, (1, 0, 2)),
        decays.T,
        betas.T,
    )


def group_terms(queries, key_rows, values, decays, betas):
    local_heads, row_count, key_width = key_rows.shape
    value_width = values.shape[-1]
    blocks = row_count // GROUP
    query_blocks = queries.reshape(local_heads, blocks, GROUP, key_width)
    key_blocks = key_rows.reshape(local_heads, blocks, GROUP, key_width)
    value_blocks = values.reshape(local_heads, blocks, GROUP, value_width)
    beta_blocks = betas.reshape(local_heads, blocks, GROUP)
    cumulative = jnp.cumsum(decays.reshape(local_heads, blocks, GROUP), axis=-1)
    positions = jnp.arange(GROUP)
    strictly = (positions[:, None] > positions[None, :]).astype(jnp.float32)
    upto_mask = positions[:, None] >= positions[None, :]
    within = jnp.exp(
        jnp.where(upto_mask, cumulative[..., :, None] - cumulative[..., None, :], 0.0)
    ) * upto_mask.astype(jnp.float32)
    key_gram = jnp.einsum("hctk,hcsk->hcts", key_blocks, key_blocks, precision=EXACT_ARITHMETIC)
    system = (
        jnp.eye(GROUP, dtype=jnp.float32) + beta_blocks[..., :, None] * key_gram * within * strictly
    )
    right_side = jnp.concatenate(
        [
            beta_blocks[..., None] * value_blocks,
            (beta_blocks * jnp.exp(cumulative))[..., None] * key_blocks,
        ],
        axis=-1,
    )
    solved = lax.linalg.triangular_solve(
        system, right_side, left_side=True, lower=True, unit_diagonal=True
    )
    fresh_values = solved[..., :value_width]
    wy_keys = solved[..., value_width:]
    tail_keys = jnp.exp(cumulative[..., -1:] - cumulative)[..., None] * key_blocks
    transition = jnp.exp(cumulative[..., -1])[..., None, None] * jnp.eye(
        key_width, dtype=jnp.float32
    ) - jnp.einsum("hctk,hctj->hckj", tail_keys, wy_keys, precision=EXACT_ARITHMETIC)
    inject = jnp.einsum("hctk,hctv->hckv", tail_keys, fresh_values, precision=EXACT_ARITHMETIC)
    attention_logits = (
        jnp.einsum("hctk,hcsk->hcts", query_blocks, key_blocks, precision=EXACT_ARITHMETIC) * within
    )
    reach_query = jnp.exp(cumulative)[..., None] * query_blocks - jnp.einsum(
        "hcts,hcsk->hctk", attention_logits, wy_keys, precision=EXACT_ARITHMETIC
    )
    local_out = jnp.einsum(
        "hcts,hcsv->hctv", attention_logits, fresh_values, precision=EXACT_ARITHMETIC
    )
    start_state = jnp.concatenate(
        [
            jnp.broadcast_to(
                jnp.eye(key_width, dtype=jnp.float32), (local_heads, key_width, key_width)
            ),
            jnp.zeros((local_heads, key_width, value_width), jnp.float32),
        ],
        axis=-1,
    )

    def advance(carried, block_terms):
        transition_now, inject_now = block_terms
        advanced = jnp.einsum("hkj,hjc->hkc", transition_now, carried, precision=EXACT_ARITHMETIC)
        advanced = advanced + jnp.concatenate([jnp.zeros_like(transition_now), inject_now], axis=-1)
        return (advanced, carried)

    final_state, starts = lax.scan(
        advance, start_state, (jnp.moveaxis(transition, 1, 0), jnp.moveaxis(inject, 1, 0))
    )
    starts = jnp.moveaxis(starts, 0, 1)
    corrected_target_vector = jnp.einsum(
        "hctk,hckj->hctj", reach_query, starts[..., :key_width], precision=EXACT_ARITHMETIC
    )
    zero_out = local_out + jnp.einsum(
        "hctk,hckv->hctv", reach_query, starts[..., key_width:], precision=EXACT_ARITHMETIC
    )
    return (
        zero_out.reshape(local_heads, row_count, value_width),
        corrected_target_vector.reshape(local_heads, row_count, key_width),
        final_state[..., :key_width],
        final_state[..., key_width:],
    )


def gating(recurred, gate_proj, norm_gain):
    local_heads, row_count, value_width = recurred.shape
    head_normed = (
        recurred
        * lax.rsqrt(jnp.mean(recurred * recurred, axis=-1, keepdims=True) + HEAD_EPSILON)
        * norm_gain
    )
    gate_heads = jnp.transpose(gate_proj.reshape(row_count, local_heads, value_width), (1, 0, 2))
    return jnp.transpose(head_normed * jax.nn.silu(gate_heads), (1, 0, 2)).reshape(
        row_count, local_heads * value_width
    )


def weight_grad(left, right):
    return jnp.einsum("td,tc->dc", left, right, preferred_element_type=jnp.float32)


def back_product(grad_rows, weight):
    return jnp.dot(grad_rows, weight.T, preferred_element_type=jnp.float32)


def add_sources(arrived):
    return jnp.sum(arrived, axis=0)


def on_device(inputs, cotangent, owners, master, moment_one, moment_two):
    head_parts = lax.axis_size("head")
    seq_parts = lax.axis_size("seq")
    local_heads = HEADS // head_parts
    capacity, piece_size = master.shape
    piece_count = owners.shape[0]
    segments_list = shard_layout(local_heads, head_parts)
    slot_of_piece, piece_of_slot, present = piece_table(owners, seq_parts, capacity)
    gathered = lax.all_gather(master.astype(jnp.bfloat16), "seq", axis=0, tiled=True)
    flat_weights = jnp.take(gathered, slot_of_piece, axis=0).reshape(-1)
    by_name, used_size = unpack(flat_weights, segments_list)
    row_count = inputs.shape[0]
    rim_width = KCONV - 1
    rows_full, back_full, first_norm_scale_factor, second_norm_scale_factor, norm_gain = (
        lax.all_gather(inputs, "head", axis=1, tiled=True),
        lax.all_gather(cotangent, "head", axis=1, tiled=True),
        lax.all_gather(by_name["gainone"].reshape(-1), "head", axis=0, tiled=True),
        lax.all_gather(by_name["gaintwo"].reshape(-1), "head", axis=0, tiled=True),
        lax.all_gather(by_name["wnorm"].reshape(-1), "head", axis=0, tiled=True),
    )
    first_norm_scale_factor = first_norm_scale_factor.astype(jnp.float32)
    second_norm_scale_factor = second_norm_scale_factor.astype(jnp.float32)
    rows_wide = rows_full.astype(jnp.float32)
    scale_one = lax.rsqrt(jnp.mean(rows_wide * rows_wide, axis=-1, keepdims=True) + NORM_EPSILON)
    normed = (rows_wide * scale_one * first_norm_scale_factor).astype(jnp.bfloat16)
    query_proj = jnp.dot(normed, by_name["wq"], preferred_element_type=jnp.float32)
    key_proj = jnp.dot(normed, by_name["wk"], preferred_element_type=jnp.float32)
    value_proj = jnp.dot(normed, by_name["wv"], preferred_element_type=jnp.float32)
    gate_proj = jnp.dot(normed, by_name["wg"], preferred_element_type=jnp.float32)
    decay_proj = jnp.dot(normed, by_name["wab"], preferred_element_type=jnp.float32)
    query_rim, key_rim, value_rim = shifted(
        (
            query_proj[row_count - rim_width :],
            key_proj[row_count - rim_width :],
            value_proj[row_count - rim_width :],
        ),
        "seq",
        1,
    )
    prep_args = (
        jnp.concatenate([query_rim, query_proj], axis=0),
        jnp.concatenate([key_rim, key_proj], axis=0),
        jnp.concatenate([value_rim, value_proj], axis=0),
        decay_proj,
        by_name["cq"].astype(jnp.float32),
        by_name["ck"].astype(jnp.float32),
        by_name["cv"].astype(jnp.float32),
        by_name["alog"].astype(jnp.float32),
        by_name["dtbias"].astype(jnp.float32),
    )
    prepared, prep_back = jax.vjp(prepare, *prep_args)
    group_out, group_back = jax.vjp(group_terms, *prepared)
    zero_out, corrected_target_vector, handoff_values, start_position = group_out
    zero_states = jnp.zeros_like(start_position)

    def relay_forward(iteration, carried):
        received_values = shifted(carried[1].astype(jnp.bfloat16), "seq", 1).astype(jnp.float32)
        return (
            received_values,
            jnp.einsum("foa,fap->fop", handoff_values, received_values, precision=EXACT_ARITHMETIC)
            + start_position,
        )

    entering_state, unused = lax.fori_loop(
        0, seq_parts - 1, relay_forward, (zero_states, start_position)
    )
    recurred = zero_out + jnp.einsum(
        "sba,saf->sbf", corrected_target_vector, entering_state, precision=EXACT_ARITHMETIC
    )
    gated_out, gate_back = jax.vjp(gating, recurred, gate_proj, norm_gain.astype(jnp.float32))
    gated_low = gated_out.astype(jnp.bfloat16)
    mixed = lax.psum_scatter(
        jnp.dot(gated_low, by_name["wo"], preferred_element_type=jnp.float32).astype(jnp.bfloat16),
        "head",
        scatter_dimension=1,
        tiled=True,
    ).astype(jnp.float32)
    inputs_wide = inputs.astype(jnp.float32)
    residual = inputs_wide + mixed
    resid_low = residual.astype(jnp.bfloat16)
    resid_full = lax.all_gather(resid_low, "head", axis=1, tiled=True).astype(jnp.float32)
    scale_two = lax.rsqrt(jnp.mean(resid_full * resid_full, axis=-1, keepdims=True) + NORM_EPSILON)
    hidden_in = (resid_full * scale_two * second_norm_scale_factor).astype(jnp.bfloat16)
    gate_mlp = jnp.dot(hidden_in, by_name["wgate"], preferred_element_type=jnp.float32)
    up_mlp = jnp.dot(hidden_in, by_name["wup"], preferred_element_type=jnp.float32)
    logistic_output_multiplier = jax.nn.sigmoid(gate_mlp)
    silu_gate = gate_mlp * logistic_output_multiplier
    hidden = (silu_gate * up_mlp).astype(jnp.bfloat16)
    mlp_out = lax.psum_scatter(
        jnp.dot(hidden, by_name["wdown"], preferred_element_type=jnp.float32).astype(jnp.bfloat16),
        "head",
        scatter_dimension=1,
        tiled=True,
    ).astype(jnp.float32)
    block_out = (residual + mlp_out).astype(jnp.bfloat16)
    grad_wdown = weight_grad(hidden, back_full)
    d_hidden = back_product(back_full, by_name["wdown"])
    d_gate_mlp = (
        d_hidden
        * up_mlp
        * logistic_output_multiplier
        * (1.0 + gate_mlp * (1.0 - logistic_output_multiplier))
    ).astype(jnp.bfloat16)
    d_up_mlp = (d_hidden * silu_gate).astype(jnp.bfloat16)
    grad_wgate = weight_grad(hidden_in, d_gate_mlp)
    grad_wup = weight_grad(hidden_in, d_up_mlp)
    d_hidden_in = back_product(d_gate_mlp, by_name["wgate"]) + back_product(
        d_up_mlp, by_name["wup"]
    )
    dot_two = jnp.sum(d_hidden_in * second_norm_scale_factor * resid_full, axis=-1, keepdims=True)
    d_hidden_mine, dot_two_sum = (
        lax.psum_scatter(
            d_hidden_in.astype(jnp.bfloat16), "head", scatter_dimension=1, tiled=True
        ).astype(jnp.float32),
        lax.psum_scatter(
            jnp.broadcast_to(dot_two, (row_count, head_parts)).astype(jnp.bfloat16),
            "head",
            scatter_dimension=1,
            tiled=True,
        ).astype(jnp.float32),
    )
    resid_mine = resid_low.astype(jnp.float32)
    gain_two_mine = by_name["gaintwo"].reshape(-1).astype(jnp.float32)
    grad_gaintwo = jnp.sum(d_hidden_mine * resid_mine * scale_two, axis=0, keepdims=True)
    d_resid = (
        cotangent.astype(jnp.float32)
        + scale_two * d_hidden_mine * gain_two_mine
        - scale_two**3 / D * resid_mine * dot_two_sum
    )
    back_mix_full = lax.all_gather(d_resid.astype(jnp.bfloat16), "head", axis=1, tiled=True)
    grad_wo = weight_grad(gated_low, back_mix_full)
    d_gated = back_product(back_mix_full, by_name["wo"])
    memory_backward_sensitivity, d_gate_wide, d_norm_gain = gate_back(d_gated)
    incoming_state = jnp.einsum(
        "gxh,gxy->ghy",
        corrected_target_vector,
        memory_backward_sensitivity,
        precision=EXACT_ARITHMETIC,
    )
    flipped_matrix = jnp.swapaxes(handoff_values, 1, 2)

    def relay_backward(iteration, carried):
        received_values = shifted(carried[1].astype(jnp.bfloat16), "seq", -1).astype(jnp.float32)
        return (
            received_values,
            incoming_state
            + jnp.einsum(
                "foa,fap->fop", flipped_matrix, received_values, precision=EXACT_ARITHMETIC
            ),
        )

    state_gradient, unused = lax.fori_loop(
        0, seq_parts - 1, relay_backward, (zero_states, incoming_state)
    )
    group_cot = (
        memory_backward_sensitivity,
        jnp.einsum(
            "yib,ypb->yip", memory_backward_sensitivity, entering_state, precision=EXACT_ARITHMETIC
        ),
        jnp.einsum("ciz,cqz->ciq", state_gradient, entering_state, precision=EXACT_ARITHMETIC),
        state_gradient,
    )
    d_prep_args = prep_back(group_back(group_cot))
    (
        d_query_ext,
        d_key_ext,
        d_value_ext,
        d_decay_proj,
        d_conv_query,
        d_conv_key,
        d_conv_value,
        d_log_rate,
        d_rate_bias,
    ) = d_prep_args
    rim_query, rim_key, rim_value = shifted(
        (d_query_ext[:rim_width], d_key_ext[:rim_width], d_value_ext[:rim_width]), "seq", -1
    )

    def with_rim(extended_grad, rim_grad):
        return extended_grad[rim_width:] + jnp.pad(rim_grad, ((row_count - rim_width, 0), (0, 0)))

    d_query = with_rim(d_query_ext, rim_query).astype(jnp.bfloat16)
    d_key = with_rim(d_key_ext, rim_key).astype(jnp.bfloat16)
    d_value = with_rim(d_value_ext, rim_value).astype(jnp.bfloat16)
    d_gate = d_gate_wide.astype(jnp.bfloat16)
    d_decay = d_decay_proj.astype(jnp.bfloat16)
    grad_wq = weight_grad(normed, d_query)
    grad_wk = weight_grad(normed, d_key)
    grad_wv = weight_grad(normed, d_value)
    grad_wg = weight_grad(normed, d_gate)
    grad_wab = weight_grad(normed, d_decay)
    d_normed = (
        back_product(d_query, by_name["wq"])
        + back_product(d_key, by_name["wk"])
        + back_product(d_value, by_name["wv"])
        + back_product(d_gate, by_name["wg"])
        + back_product(d_decay, by_name["wab"])
    )
    dot_one = jnp.sum(d_normed * first_norm_scale_factor * rows_wide, axis=-1, keepdims=True)
    d_normed_mine, dot_one_sum, grad_wnorm = (
        lax.psum_scatter(
            d_normed.astype(jnp.bfloat16), "head", scatter_dimension=1, tiled=True
        ).astype(jnp.float32),
        lax.psum_scatter(
            jnp.broadcast_to(dot_one, (row_count, head_parts)).astype(jnp.bfloat16),
            "head",
            scatter_dimension=1,
            tiled=True,
        ).astype(jnp.float32),
        lax.psum_scatter(
            d_norm_gain.astype(jnp.bfloat16), "head", scatter_dimension=0, tiled=True
        ).astype(jnp.float32),
    )
    gain_one_mine = by_name["gainone"].reshape(-1).astype(jnp.float32)
    grad_gainone = jnp.sum(d_normed_mine * inputs_wide * scale_one, axis=0, keepdims=True)
    input_grad = (
        d_resid
        + scale_one * d_normed_mine * gain_one_mine
        - scale_one**3 / D * inputs_wide * dot_one_sum
    )
    grad_list = [
        grad_wq,
        grad_wk,
        grad_wv,
        grad_wg,
        grad_wo,
        grad_wgate,
        grad_wup,
        grad_wdown,
        d_conv_query,
        d_conv_key,
        d_conv_value,
        grad_wab,
        d_log_rate,
        d_rate_bias,
        grad_gainone,
        grad_gaintwo,
        grad_wnorm.reshape(1, -1),
    ]
    flat_grads = jnp.concatenate(
        [grad_now.reshape(-1) for grad_now in grad_list]
        + [jnp.zeros((piece_count * piece_size - used_size,), jnp.float32)]
    )
    grad_table = flat_grads.reshape(piece_count, piece_size)
    my_index = lax.axis_index("seq")
    slot_ordered = (
        jnp.take(grad_table, piece_of_slot, axis=0) * present[:, None].astype(jnp.float32)
    ).reshape(seq_parts, capacity, piece_size)
    grad_slots = add_sources(
        lax.all_to_all(
            slot_ordered.astype(jnp.bfloat16), "seq", split_axis=0, concat_axis=0, tiled=True
        ).astype(slot_ordered.dtype)
    )
    piece_rates, small_rates = rate_parts(segments_list, piece_count, piece_size)
    my_pieces = lax.dynamic_slice_in_dim(piece_of_slot, my_index * capacity, capacity)
    my_present = lax.dynamic_slice_in_dim(present, my_index * capacity, capacity)
    piece_rate_rows = jnp.sum(
        (my_pieces[:, None] == jnp.arange(piece_count, dtype=jnp.int32)[None, :]).astype(
            jnp.float32
        )
        * jnp.asarray(piece_rates)[None, :],
        axis=1,
    )
    slot_rates = jnp.where(
        (my_pieces == piece_count - 1)[:, None],
        jnp.asarray(small_rates)[None, :],
        piece_rate_rows[:, None],
    )
    slot_rates = jnp.where(my_present[:, None], slot_rates, PAD_RATE)
    moment_new = BETA_ONE * moment_one + (1.0 - BETA_ONE) * grad_slots
    second_new = BETA_TWO * moment_two + (1.0 - BETA_TWO) * grad_slots * grad_slots
    first_hat = moment_new / (1.0 - BETA_ONE**STEP)
    second_hat = second_new / (1.0 - BETA_TWO**STEP)
    master_new = master - slot_rates * (
        first_hat / (jnp.sqrt(second_hat) + ADAM_EPSILON) + WEIGHT_DECAY * master
    )
    return (
        block_out,
        input_grad,
        grad_slots,
        master_new,
        moment_new,
        second_new,
        master_new.astype(jnp.bfloat16),
    )


def solution(mesh):
    return jax.shard_map(
        on_device,
        mesh=mesh,
        in_specs=(
            P("seq", "head"),
            P("seq", "head"),
            P(),
            P("seq", "head"),
            P("seq", "head"),
            P("seq", "head"),
        ),
        out_specs=(
            P("seq", "head"),
            P("seq", "head"),
            P("seq", "head"),
            P("seq", "head"),
            P("seq", "head"),
            P("seq", "head"),
            P("seq", "head"),
        ),
        check_vma=False,
    )
```

profile of v0, /device:TPU:0, one launch (start us, length us, event | category | flops | bytes accessed | tf_op | source)
XLA Modules:
  0.0 3630.5 jit_solution(373899314747270983)
XLA Ops:
  7.9 7.9 convert_bitcast_fusion
  29.7 10.6 all-gather.9.cloned.1.call-done
  42.3 232.2 %all-gather.17.cloned.1.call-done = bf16[8,44,65536]{2,1,0:T(8,128)(2,1)} async-done(((bf16[1,44,65536]{2,1,0:T(8,128)(2,1)}), bf16[8,44,65536]{2,1,0:T(8,128)(2,1)}) %all-gather.17.cloned.1.call-update) | async-done | bytes 46137360 | tf_op jit(solution)/shard_map/all_gather | solution.py:245
  274.5 46.0 %reshape.595 = bf16[352,65536]{1,0:T(8,128)(2,1)} reshape(bf16[8,44,65536]{2,1,0:T(8,128)(2,1)} %all-gather.17.cloned.1.call-done) | data formatting | bytes 92274688
  320.5 68.3 %gather_fusion = bf16[261,65536]{1,0:T(8,128)(2,1)} fusion(bf16[352,65536]{1,0:T(8,128)(2,1)} %reshape.595, s32[1024]{0:T(1024)S(1)} %pad_clamp_fusion.1), kind=kCustom, calls=%fused_computation | custom fusion | bytes 68420624 | tf_op jit(solution)/shard_map/jit(_take)/gather | solution.py:246
  388.8 42.6 %gather.17 = bf16[33408,512]{1,0:T(8,128)(2,1)} reshape(bf16[261,65536]{1,0:T(8,128)(2,1)} %gather_fusion) | data formatting | bytes 68419584 | tf_op jit(solution)/shard_map/jit(_take)/gather | solution.py:246
  431.4 42.6 %gather.19 = bf16[16704,1024]{1,0:T(8,128)(2,1)} reshape(bf16[261,65536]{1,0:T(8,128)(2,1)} %gather_fusion) | data formatting | bytes 68419584 | tf_op jit(solution)/shard_map/jit(_take)/gather | solution.py:246
  474.1 23.8 broadcast_select_fusion
  502.3 9.1 fusion.226
  511.4 42.6 %select_n.83 = bf16[17104896]{0:T(1024)(128)(2,1)} reshape(bf16[261,65536]{1,0:T(8,128)(2,1)} %broadcast_select_fusion) | data formatting | bytes 68419584 | tf_op jit(solution)/shard_map/jit(_take)/select_n | solution.py:246
  559.3 893.9 %gather.18 = bf16[2138112,8]{1,0:T(8,128)(2,1)} reshape(bf16[261,65536]{1,0:T(8,128)(2,1)} %gather_fusion) | data formatting | bytes 68419584 | tf_op jit(solution)/shard_map/jit(_take)/gather | solution.py:246
  1453.2 11.9 all-gather.1
  1468.8 23.7 broadcast_select_fusion.1
  1500.9 5.6 reshape.530
  1506.6 5.6 reshape.525
  1512.2 6.4 copy.304
  1518.6 5.6 reshape.531
  1524.5 10.4 all-reduce.40
  1555.9 78.8 %custom-call.7 = f32[4,4,1,64,64]{3,4,2,1,0:T(8,128)S(1)} custom-call(f32[4,4,1,64,64]{4,3,2,1,0:T(8,128)S(1)} %add_bitcast_fusion.1), custom_call_target="InvertDiagBlocksLowerTriangular" | custom-call | tf_op jit(solution)/shard_map/jvp()/triangular_solve | solution.py:159
  1647.7 15.7 while.54
  1682.3 55.9 %while.55 = (s32[]{:T(128)}, f32[4,128,256]{2,1,0:T(8,128)}, bf16[4,128,256]{2,1,0:T(8,128)(2,1)S(1)}, f32[4,128,128]{2,1,0:T(8,128)S(1)}, f32[4,128,256]{2,1,0:T(8,128)S(1)}, /*index=5*/s32[]{:T(128)}) while((s32[]{:T(128)}, f32[4,128,256]{2,1,0:T(8,128)}, bf16[4,128,256]{2,1,0:T(8,128)(2,1)S(1)}, f32[4,128,128]{2,1,0:T(8,128)S(1)}, ...), condition=%wide.region_10.11_spmd, body=%wide.region_9.10_spmd.sunk | while | flops 201719808 | bytes 3145837 | solution.py:300
  1693.6 6.6 collective-permute-start
  1702.6 6.6 collective-permute-start
  1711.5 6.6 collective-permute-start
  1720.4 6.6 collective-permute-start
  1729.3 6.6 collective-permute-start
  1749.1 36.3 %reduce-scatter.5.cloned.1.call-done = bf16[256,512]{1,0:T(8,128)(2,1)} async-done(((bf16[256,2048]{1,0:T(8,128)(2,1)}), bf16[256,512]{1,0:T(8,128)(2,1)}) %reduce-scatter.5.cloned.1.call-update) | async-done | bytes 262160 | tf_op jit(solution)/shard_map/reduce_scatter | solution.py:308
  1787.8 14.6 fusion.225
  1802.4 8.3 reshape.534
  1810.7 12.3 all-gather.2
  1823.0 13.9 reshape.533
  1836.9 14.1 reshape.532
  1853.2 6.1 fusion.199
  1862.2 6.9 multiply_convert_fusion.1
  1874.6 6.2 fusion.228
  1884.2 5.6 dot_general.220
  1893.1 6.1 convolution_bitcast_fusion.1
  1899.3 11.6 copy.381
  1911.5 9.0 all-reduce.41
  1924.5 7.8 fusion.197
  1932.3 12.6 reshape.550
  1944.9 7.8 fusion.195
  1952.7 12.6 reshape.551
  1965.3 5.6 convolution_convert_fusion.1
  1999.0 72.0 %while.56 = (s32[]{:T(128)}, f32[4,128,256]{2,1,0:T(8,128)}, bf16[4,128,256]{2,1,0:T(8,128)(2,1)}, f32[4,128,128]{2,1,0:T(8,128)}, f32[4,128,256]{2,1,0:T(8,128)}, /*index=5*/s32[]{:T(128)}) while((s32[]{:T(128)}, f32[4,128,256]{2,1,0:T(8,128)}, bf16[4,128,256]{2,1,0:T(8,128)(2,1)}, f32[4,128,128]{2,1,0:T(8,128)}, ...), condition=%wide.region_21.22_spmd, body=%wide.region_20.21_spmd.sunk | while | flops 201719808 | bytes 3145837 | solution.py:388
  2007.3 6.1 collective-permute-done.1
  2017.7 6.6 collective-permute-done.1
  2028.7 6.6 collective-permute-done.1
  2039.6 6.6 collective-permute-done.1
  2050.5 6.6 collective-permute-done.1
  2061.4 6.6 collective-permute-done.1
  2080.8 31.6 while.57
  2193.3 5.6 copy.379
  2208.9 5.5 copy.378
  2214.4 10.6 all-reduce.44
  2228.4 522.3 %concatenate.26 = f32[17104896]{0:T(1024)} concatenate(f32[1048576]{0:T(1024)} %bitcast.362, f32[1048576]{0:T(1024)} %bitcast.361, f32[2097152]{0:T(1024)} %bitcast.352, f32[2097152]{0:T(1024)} %bitcast.351, f32[2097152]{0:T(1024)} %bitcast.350, f32[2883584]{0:T(1024)} %reshape.550, f32[2883584]{0:T(1024)} %reshape.551, f32[2883584]{0:T(1024)} %bitcast.349, f32[2048]{0:T(1024)S(1)} %bitcast.420, ...), dimensions={0} | concatenate | bytes 136839168 | tf_op jit(solution)/shard_map/concatenate | solution.py:476
  2750.6 59.1 %reshape.569 = f32[261,65536]{1,0:T(8,128)} reshape(f32[17104896]{0:T(1024)} %concatenate.26) | data formatting | bytes 136839168 | tf_op jit(solution)/shard_map/reshape | solution.py:480
  2809.7 77.8 %gather_fusion.1 = f32[352,65536]{1,0:T(8,128)} fusion(f32[261,65536]{1,0:T(8,128)} %reshape.569, s32[1024]{0:T(1024)S(1)} %copy-done.146), kind=kCustom, calls=%fused_computation.1 | custom fusion | bytes 184550784 | tf_op jit(solution)/shard_map/jit(_take)/gather | solution.py:483
  2887.5 72.7 %gather.21 = f32[8,44,65536]{2,1,0:T(8,128)} reshape(f32[352,65536]{1,0:T(8,128)} %gather_fusion.1) | data formatting | bytes 184549376 | tf_op jit(solution)/shard_map/jit(_take)/gather | solution.py:483
  2960.2 48.1 %multiply_convert_fusion = bf16[8,44,65536]{2,1,0:T(8,128)(2,1)} fusion(f32[8,44,65536]{2,1,0:T(8,128)} %gather.21, f32[8,44]{1,0:T(8,128)S(1)} %copy-done.139, pred[8,44]{1,0:T(8,128)(4,1)S(1)} %copy-done.159), kind=kLoop, calls=%fused_computation.21 | loop fusion | flops 69206016 | bytes 138413792 | tf_op jit(solution)/shard_map/convert_element_type | solution.py:487
  3008.3 17.2 all-to-all-start
  3026.5 543.5 %all-to-all-done = bf16[8,44,65536]{2,1,0:T(8,128)(2,1)} async-done(((bf16[8,44,65536]{2,1,0:T(8,128)(2,1)}), bf16[8,44,65536]{2,1,0:T(8,128)(2,1)}, u32[]{:S(2)}, u32[]{:S(2)}) %all-to-all-start) | async-done | bytes 46137376 | tf_op jit(solution)/shard_map/all_to_all | solution.py:486
  3569.9 21.7 convert_reduce_fusion
  3591.6 32.1 fusion.217
  (705 shorter events, 358.3 us)
Async XLA Ops:
  7.2 33.1 all-gather.9.cloned.1.call-start
  7.9 266.6 %all-gather.17.cloned.1.call-start = ((), (), s32[]{:S(2)}) async-start(), calls=%async_computation.13 | async-start | bytes 56623104 | tf_op jit(solution)/shard_map/all_gather | solution.py:245
  15.9 1769.6 %reduce-scatter.5.cloned.1.call-start = ((), (), s32[]{:S(2)}) async-start(), calls=%async_computation.6 | async-start | bytes 1310720 | tf_op jit(solution)/shard_map/reduce_scatter | solution.py:308
  431.4 42.6 %copy-start.143 = (pred[261]{0:T(512)(128)(4,1)S(1)}, pred[261]{0:T(512)(128)(4,1)}, u32[]{:S(2)}) copy-start(pred[261]{0:T(512)(128)(4,1)} %copy-done.142) | copy-start | bytes 787
  559.3 893.9 %copy-start.162 = (bf16[512]{0:T(512)(128)(2,1)S(1)}, bf16[512]{0:T(512)(128)(2,1)}, u32[]{:S(2)}) copy-start(bf16[512]{0:T(512)(128)(2,1)} %get-tuple-element.450) | copy-start | bytes 3076
  559.3 905.9 %copy-start.1 = (bf16[256,2048]{1,0:T(8,128)(2,1)S(1)}, bf16[256,2048]{1,0:T(8,128)(2,1)}, u32[]{:S(2)}) copy-start(bf16[256,2048]{1,0:T(8,128)(2,1)} %all-gather.9.cloned.1.call-done) | copy-start | bytes 3145732
  559.3 905.9 %copy-start.97 = (f32[256]{0:T(256)S(1)}, f32[256]{0:T(256)}, u32[]{:S(2)}) copy-start(f32[256]{0:T(256)} %get-tuple-element.507) | copy-start | bytes 3076
  559.3 905.9 %copy-start.147 = (pred[2048]{0:T(1024)(128)(4,1)S(1)}, pred[2048]{0:T(1024)(128)(4,1)}, u32[]{:S(2)}) copy-start(pred[2048]{0:T(1024)(128)(4,1)} %slice.291) | copy-start | bytes 6148
  1453.2 15.6 copy-start.89
  1466.9 25.6 copy-start.117
  1468.2 78.7 %copy-start.67 = (f32[4,4,64]{1,0,2:T(4,128)}, f32[4,4,64]{1,0,2:T(4,128)S(1)}, u32[]{:S(2)}) copy-start(f32[4,4,64]{1,0,2:T(4,128)S(1)} %copy.290) | copy-start | bytes 12292
  1468.8 24.5 copy-start.174
  1497.0 38.5 %copy-start.26 = (bf16[2048,512]{1,0:T(8,128)(2,1)}, bf16[2048,512]{1,0:T(8,128)(2,1)S(1)}, u32[]{:S(2)}) copy-start(bf16[2048,512]{1,0:T(8,128)(2,1)S(1)} %reshape.521) | copy-start | bytes 6291460
  1536.2 13.4 collective-permute-start.3
  1538.6 8.7 collective-permute-start.2
  1544.0 90.8 %copy-start.38 = (f32[256,1024]{1,0:T(8,128)}, f32[256,1024]{1,0:T(8,128)S(1)}, u32[]{:S(2)}) copy-start(f32[256,1024]{1,0:T(8,128)S(1)} %fusion.209) | copy-start | bytes 3145732
  1544.7 90.1 %collective-permute-start.4 = (f32[3,1024]{1,0:T(4,128)}, f32[3,1024]{1,0:T(4,128)S(1)}, u32[]{:S(2)}, u32[]{:S(2)}) collective-permute-start(f32[3,1024]{1,0:T(4,128)} %slice.300), channel_id=1, source_target_pairs={{0,1},{1,2},{2,3},{3,4},{4,5},{5,6},{6,7},{8,9},{9,10},{10,11},{11... | collective-permute-start | bytes 36872 | tf_op jit(solution)/shard_map/ppermute | solution.py:31
  1553.5 81.3 %copy-start.99 = (f32[1,1024]{1,0:T(1,128)S(1)}, f32[1,1024]{1,0:T(1,128)}, u32[]{:S(2)}) copy-start(f32[1,1024]{1,0:T(1,128)} %get-tuple-element.488) | copy-start | bytes 12292
  1553.5 81.3 %copy-start.101 = (f32[1,1024]{1,0:T(1,128)S(1)}, f32[1,1024]{1,0:T(1,128)}, u32[]{:S(2)}) copy-start(f32[1,1024]{1,0:T(1,128)} %get-tuple-element.489) | copy-start | bytes 12292
  1553.5 81.3 %copy-start.103 = (f32[1,1024]{1,0:T(1,128)S(1)}, f32[1,1024]{1,0:T(1,128)}, u32[]{:S(2)}) copy-start(f32[1,1024]{1,0:T(1,128)} %get-tuple-element.490) | copy-start | bytes 12292
  1553.5 81.3 %copy-start.105 = (f32[1,1024]{1,0:T(1,128)S(1)}, f32[1,1024]{1,0:T(1,128)}, u32[]{:S(2)}) copy-start(f32[1,1024]{1,0:T(1,128)} %get-tuple-element.491) | copy-start | bytes 12292
  1682.3 3.7 collective-permute-start
  1687.2 5.2 collective-permute-start
  1693.6 7.7 collective-permute-start
  1702.6 7.7 collective-permute-start
  1711.5 7.7 collective-permute-start
  1720.4 7.7 collective-permute-start
  1729.3 7.7 collective-permute-start
  1746.8 38.6 %copy-start.50 = (bf16[256,512]{1,0:T(8,128)(2,1)S(1)}, bf16[256,512]{1,0:T(8,128)(2,1)}, u32[]{:S(2)}) copy-start(bf16[256,512]{1,0:T(8,128)(2,1)} %param.16) | copy-start | bytes 786436
  1749.1 101.9 %all-gather.11.cloned.1.call-start = ((), (), s32[]{:S(2)}) async-start(), calls=%async_computation.7 | async-start | bytes 1310720 | tf_op jit(solution)/shard_map/all_gather | solution.py:317
  1787.2 75.0 %all-gather.13.cloned.1.call-start = ((), (), s32[]{:S(2)}) async-start(), calls=%async_computation.9 | async-start | bytes 1310720 | tf_op jit(solution)/shard_map/all_gather | solution.py:252
  1787.8 134.7 %reduce-scatter.9.cloned.1.call-start = ((), (), s32[]{:S(2)}) async-start(), calls=%async_computation.10 | async-start | bytes 1310720 | tf_op jit(solution)/shard_map/reduce_scatter | solution.py:348
  1880.8 90.4 %all-gather.15.cloned.1.call-start = ((), (), s32[]{:S(2)}) async-start(), calls=%async_computation.11 | async-start | bytes 1310720 | tf_op jit(solution)/shard_map/all_gather | solution.py:366
  1899.3 23.2 copy-start.40
  1899.3 23.2 copy-start.137
  1924.4 301.3 %reduce-scatter.7.cloned.1.call-start = ((), (), s32[]{:S(2)}) async-start(), calls=%async_computation.8 | async-start | bytes 1310720 | tf_op jit(solution)/shard_map/reduce_scatter | solution.py:325
  1971.0 254.8 %reduce-scatter.11.cloned.1.call-start = ((), (), s32[]{:S(2)}) async-start(), calls=%async_computation.12 | async-start | bytes 1310720 | tf_op jit(solution)/shard_map/reduce_scatter | solution.py:437
  1999.4 3.6 collective-permute-start.1
  2006.1 7.4 collective-permute-start.1
  2016.5 7.9 collective-permute-start.1
  2027.4 7.9 collective-permute-start.1
  2038.3 7.9 collective-permute-start.1
  2049.2 7.9 collective-permute-start.1
  2060.1 7.9 collective-permute-start.1
  2164.3 8.6 collective-permute-start.6
  2165.6 11.2 collective-permute-start.5
  2166.9 8.6 collective-permute-start.7
  2208.8 17.0 copy-start.41
  2208.8 17.0 copy-start.51
  2208.8 17.0 copy-start.52
  2208.8 17.0 copy-start.75
  2208.8 17.0 copy-start.76
  2208.8 17.0 copy-start.138
  2208.8 17.0 copy-start.144
  2208.8 17.0 copy-start.145
  2208.9 17.0 copy-start.150
  2208.9 17.0 copy-start.160
  2750.6 59.1 %copy-start.146 = (s32[1024]{0:T(1024)S(1)}, s32[1024]{0:T(1024)}, u32[]{:S(2)}) copy-start(s32[1024]{0:T(1024)} %pad_clamp_fusion) | copy-start | bytes 12292
  2887.5 72.7 %copy-start.139 = (f32[8,44]{1,0:T(8,128)S(1)}, f32[8,44]{1,0:T(8,128)}, u32[]{:S(2)}) copy-start(f32[8,44]{1,0:T(8,128)} %reshape.573) | copy-start | bytes 4228
  2887.5 72.7 %copy-start.159 = (pred[8,44]{1,0:T(8,128)(4,1)S(1)}, pred[8,44]{1,0:T(8,128)(4,1)}, u32[]{:S(2)}) copy-start(pred[8,44]{1,0:T(8,128)(4,1)} %compare_and_fusion) | copy-start | bytes 1060
  3008.3 17.2 copy-start.164
  3008.3 18.0 copy-start.166
  3008.3 561.6 %all-to-all-start = ((bf16[8,44,65536]{2,1,0:T(8,128)(2,1)}), bf16[8,44,65536]{2,1,0:T(8,128)(2,1)}, u32[]{:S(2)}, u32[]{:S(2)}) async-start(bf16[8,44,65536]{2,1,0:T(8,128)(2,1)} %multiply_convert_fusion), calls=%async_computation.4 | async-start | bytes 100663296 | tf_op jit(solution)/shard_map/all_to_all | solution.py:486
  3026.4 565.1 %copy-start.87 = (f32[65536]{0:T(1024)S(1)}, f32[65536]{0:T(1024)}, u32[]{:S(2)}) copy-start(f32[65536]{0:T(1024)} %constant.194.clone) | copy-start | bytes 786436
  (145 other events, 532.4 us)
Sparse Core Ops, SparseCore 0:
  9.6 30.6 all-gather.8
  42.7 231.7 all-gather.16
  1749.2 36.2 reduce-scatter.4
  1787.5 26.5 all-gather.10
  1815.6 27.4 all-gather.12
  1880.9 25.9 reduce-scatter.8
  1924.6 27.6 all-gather.14
  1971.1 26.9 reduce-scatter.6
  2180.7 40.0 reduce-scatter.10
where the time goes:
time: 3670 us; the launch traced here: 3630 us
  local copies, waits for them, and re-layouts  2090 us (57%)
  waiting for transfers between devices  875 us (24%)
  other arithmetic  304 us (8%)
  matrix products  208 us (6%)
  starting transfers between devices  78 us (2%)
  blocking collectives  54.2 us (1%)
    gather x4, local copies, waits for them, and re-layouts, on_device(): flat_weights = jnp.take(gathered, slot_of_piece, axis=0).reshape(-1)  1050 us
    all_to_all x1, waiting for transfers between devices, on_device(): lax.all_to_all(slot_ordered.astype(jnp.bfloat16), 'seq', split_axis=0, co...  543 us
    concatenate x1, local copies, waits for them, and re-layouts, on_device(): jnp.concatenate([grad_now.reshape(-1) for grad_now in grad_list] + [jnp.z...  522 us
    all_gather x1, waiting for transfers between devices, on_device(): lax.all_gather(master.astype(jnp.bfloat16), 'seq', axis=0, tiled=True)  232 us
    gather x2, local copies, waits for them, and re-layouts, on_device(): jnp.take(grad_table, piece_of_slot, axis=0)  150 us
    unnamed x374, local copies, waits for them, and re-layouts  87.4 us
    another operation x5, other arithmetic, group_terms(): lax.linalg.triangular_solve(system, right_side, left_side=True, lower=Tru...  80.5 us
  transfers between devices with their start and end apart: 30, of which 19 were waited for; matrix products, arithmetic and copies ran while one was open for 12% of the time, Pallas kernels for 0%

commit v1 on v0

v1 whole, which is shorter than its diff:
```python
import jax
import jax.numpy as jnp
import numpy as np
from jax import lax
from jax.experimental import pallas as pl
from jax.experimental.pallas import tpu as pltpu
from jax.sharding import PartitionSpec as P

D = 2048
HEADS = 16
DK = 128
DV = 256
FF = 5632
KCONV = 4
STEP = 5


EXACT_ARITHMETIC = lax.Precision.HIGHEST
NORM_EPSILON = 1e-06
UNIT_EPSILON = 1e-06
HEAD_EPSILON = 1e-05
ADAM_EPSILON = 1e-08
BETA_ONE = 0.5
BETA_TWO = 0.5
WEIGHT_DECAY = 0.1
PAD_RATE = 0.1


def shifted(block, axis, distance):
    devices = range(lax.axis_size(axis))
    route = [(i - distance, i) for i in devices if i - distance in devices]
    return lax.ppermute(block, axis, route)


def shard_layout(local_heads, head_parts):
    return [
        ("wq", D, local_heads * DK, 0.02),
        ("wk", D, local_heads * DK, 0.02),
        ("wv", D, local_heads * DV, 0.02),
        ("wg", D, local_heads * DV, 0.02),
        ("wo", local_heads * DV, D, 0.015),
        ("wgate", D, FF // head_parts, 0.02),
        ("wup", D, FF // head_parts, 0.02),
        ("wdown", FF // head_parts, D, 0.012),
        ("cq", KCONV, local_heads * DK, 0.4),
        ("ck", KCONV, local_heads * DK, 0.4),
        ("cv", KCONV, local_heads * DV, 0.4),
        ("wab", D, 2 * local_heads, 0.04),
        ("alog", 1, local_heads, 0.5),
        ("dtbias", 1, local_heads, 0.5),
        ("gainone", 1, D // head_parts, 0.1),
        ("gaintwo", 1, D // head_parts, 0.1),
        ("wnorm", 1, DV // head_parts, 0.1),
    ]


def piece_table(owners, seq_parts, capacity):
    piece_count = owners.shape[0]
    devices = jnp.arange(seq_parts, dtype=jnp.int32)
    onehot = (owners[:, None] == devices[None, :]).astype(jnp.int32)
    before = jnp.cumsum(onehot, axis=0) - onehot
    rank_within = jnp.sum(before * onehot, axis=1)
    slot_of_piece = owners * capacity + rank_within
    matches = slot_of_piece[None, :] == jnp.arange(seq_parts * capacity, dtype=jnp.int32)[:, None]
    present = jnp.any(matches, axis=1)
    piece_of_slot = jnp.sum(
        matches.astype(jnp.int32) * jnp.arange(piece_count, dtype=jnp.int32)[None, :], axis=1
    )
    return (slot_of_piece, piece_of_slot, present)


def unpack(flat_weights, segments_list):
    by_name = {}
    offset_now = 0
    for seg_name, row_count, col_count, seg_rate in segments_list:
        by_name[seg_name] = flat_weights[offset_now : offset_now + row_count * col_count].reshape(
            row_count, col_count
        )
        offset_now += row_count * col_count
    return (by_name, offset_now)


def rate_parts(segments_list, piece_count, piece_size):
    piece_rates = np.full(piece_count, PAD_RATE, np.float32)
    small_rates = np.full(piece_size, PAD_RATE, np.float32)
    offset_now = 0
    big_total = (piece_count - 1) * piece_size
    for seg_name, row_count, col_count, seg_rate in segments_list:
        seg_size = row_count * col_count
        if offset_now < big_total:
            piece_rates[offset_now // piece_size : (offset_now + seg_size) // piece_size] = seg_rate
        else:
            small_rates[offset_now - big_total : offset_now - big_total + seg_size] = seg_rate
        offset_now += seg_size
    return (piece_rates, small_rates)


def product(left, right, left_axis, right_axis, exact=True):
    return lax.dot_general(
        left,
        right,
        (((left_axis,), (right_axis,)), ((), ())),
        precision=EXACT_ARITHMETIC if exact else None,
        preferred_element_type=jnp.float32,
    )


def take_lane(wide, lane):
    lanes = lax.broadcasted_iota(jnp.int32, wide.shape, 1)
    return jnp.sum(jnp.where(lanes == lane, wide, 0.0), axis=1, keepdims=True)


def put_lane(column, lane):
    lanes = lax.broadcasted_iota(jnp.int32, (column.shape[0], 128), 1)
    return jnp.where(lanes == lane, column, 0.0)


def to_row(column, diagonal):
    return jnp.sum(jnp.where(diagonal, column, 0.0), axis=0, keepdims=True)


def convolved(extended, block_ref, rim_ref, taps_ref):
    row_count = block_ref.shape[0]
    extended[0:8, :] = rim_ref[...]
    extended[8 : 8 + row_count, :] = block_ref[...]
    first = 8 - (KCONV - 1)
    running = taps_ref[0:1, :] * extended[first : first + row_count, :]
    for tap in range(1, KCONV):
        running = running + taps_ref[tap : tap + 1, :] * extended[
            first + tap : first + tap + row_count, :
        ]
    return running


def decay_terms(head, local_heads, decay_ref, scalars_ref):
    row_count = decay_ref.shape[0]
    shape = (row_count, row_count)
    row_ids = lax.broadcasted_iota(jnp.int32, shape, 0)
    column_ids = lax.broadcasted_iota(jnp.int32, shape, 1)
    decay_in = take_lane(decay_ref[...], head) + take_lane(scalars_ref[1:2, :], head)
    rate = -jnp.exp(take_lane(scalars_ref[0:1, :], head))
    soft = jnp.maximum(decay_in, 0.0) + jnp.log1p(jnp.exp(-jnp.abs(decay_in)))
    logs = rate * soft
    beta = jax.nn.sigmoid(take_lane(decay_ref[...], head + local_heads))
    diagonal = row_ids == column_ids
    logs_row = to_row(logs, diagonal)
    upto = row_ids >= column_ids
    sums = jnp.sum(jnp.where(upto, logs_row, 0.0), axis=1, keepdims=True)
    sums_row = to_row(sums, diagonal)
    within = jnp.exp(jnp.where(upto, sums - sums_row, -1e30))
    return decay_in, rate, logs, beta, sums, within, row_ids, column_ids


def unit_rows(rows):
    scale = lax.rsqrt(jnp.sum(rows * rows, axis=-1, keepdims=True) + UNIT_EPSILON)
    return rows * scale, scale


def mixer_specs(local_heads, row_count):
    def spec(rows, width, first):
        return pl.BlockSpec((rows, width), lambda h, first=first: (0, first + h))

    def three(rows):
        return [
            spec(rows, DK, 0),
            spec(rows, DK, local_heads),
            spec(rows, DV, 2 * local_heads * DK // DV),
        ]

    whole = pl.BlockSpec((row_count, 128), lambda h: (0, 0))
    scalars = pl.BlockSpec((8, 128), lambda h: (0, 0))
    return three, whole, scalars


def per_head(*shape):
    return pl.BlockSpec((1,) + shape, lambda h: (h,) + (0,) * len(shape))


def mixer_local(local_heads, projected, rim, taps, decay_proj, scalars):
    row_count = projected.shape[0]
    three, whole, scalar_spec = mixer_specs(local_heads, row_count)

    def kernel(
        pq, pk, pv, rq, rk, rv, tq, tk, tv, decay_ref, scalars_ref,
        solve_ref, fresh_ref, wy_ref, reach_ref, zero_ref, handoff_ref, ext_q, ext_k, ext_v,
    ):
        head = pl.program_id(0)
        queries = unit_rows(jax.nn.silu(convolved(ext_q, pq, rq, tq)))[0] * DK ** (-0.5)
        key_rows = unit_rows(jax.nn.silu(convolved(ext_k, pk, rk, tk)))[0]
        values = jax.nn.silu(convolved(ext_v, pv, rv, tv))
        decay_in, rate, logs, beta, sums, within, row_ids, column_ids = decay_terms(
            head, local_heads, decay_ref, scalars_ref
        )
        gram = product(key_rows, key_rows, 1, 1)
        system = jnp.where(row_ids > column_ids, beta * gram * within, 0.0)
        solve = jnp.where(row_ids == column_ids, 1.0, 0.0)
        size = 1
        while size < row_count:
            lower = (row_ids // (2 * size) == column_ids // (2 * size)) & (
                row_ids // size != column_ids // size
            )
            part = jnp.where(lower, system, 0.0)
            if size == 1:
                solve = solve - part
            else:
                solve = solve - product(solve, product(part, solve, 1, 0), 1, 0)
            size *= 2
        grown = jnp.exp(sums)
        fresh = product(solve, beta * values, 1, 0)
        wy_keys = product(solve, (beta * grown) * key_rows, 1, 0)
        attention = product(queries, key_rows, 1, 1) * within
        last = sums[row_count - 1 : row_count, :]
        tail_keys = jnp.exp(last - sums) * key_rows
        eye = lax.broadcasted_iota(jnp.int32, (DK, DK), 0) == lax.broadcasted_iota(
            jnp.int32, (DK, DK), 1
        )
        solve_ref[0] = solve
        fresh_ref[0] = fresh
        wy_ref[0] = wy_keys
        reach_ref[0] = grown * queries - product(attention, wy_keys, 1, 0)
        zero_ref[0] = product(attention, fresh, 1, 0)
        handoff_ref[0, :, :DK] = (
            jnp.where(eye, jnp.exp(last), 0.0) - product(tail_keys, wy_keys, 0, 0)
        ).astype(jnp.bfloat16)
        handoff_ref[0, :, DK:] = product(tail_keys, fresh, 0, 0).astype(jnp.bfloat16)

    def out(*shape, kind=jnp.float32):
        return jax.ShapeDtypeStruct((local_heads,) + shape, kind)

    return pl.pallas_call(
        kernel,
        grid=(local_heads,),
        in_specs=three(row_count) + three(8) + three(8) + [whole, scalar_spec],
        out_specs=[
            per_head(row_count, row_count),
            per_head(row_count, DV),
            per_head(row_count, DK),
            per_head(row_count, DK),
            per_head(row_count, DV),
            per_head(DK, DK + DV),
        ],
        out_shape=[
            out(row_count, row_count),
            out(row_count, DV),
            out(row_count, DK),
            out(row_count, DK),
            out(row_count, DV),
            out(DK, DK + DV, kind=jnp.bfloat16),
        ],
        scratch_shapes=[
            pltpu.VMEM((row_count + 8, DK), jnp.float32),
            pltpu.VMEM((row_count + 8, DK), jnp.float32),
            pltpu.VMEM((row_count + 8, DV), jnp.float32),
        ],
        compiler_params=params(),
    )(*([projected] * 3), *([rim] * 3), *([taps] * 3), decay_proj, scalars)


def mixer_out(local_heads, my_index, handoffs, reach, zero_out, projected, norm_gain):
    row_count = projected.shape[0]
    gate_first = local_heads * (2 * DK + DV)

    def kernel(index_ref, handoffs_ref, reach_ref, zero_ref, gate_ref, norm_ref, state_ref, out_ref, gated_ref):
        state_ref[...] = jnp.zeros_like(state_ref)

        def advance(j, carry):
            for h in range(local_heads):
                block = handoffs_ref[j, h]
                state_ref[h] = product(
                    block[:, :DK].astype(jnp.float32), state_ref[h], 1, 0
                ) + block[:, DK:].astype(jnp.float32)
            return carry

        lax.fori_loop(0, index_ref[0], advance, 0)
        for h in range(local_heads):
            columns = slice(DV * h, DV * h + DV)
            out = zero_ref[h] + product(reach_ref[h], state_ref[h], 1, 0)
            normed = out * lax.rsqrt(jnp.mean(out * out, axis=-1, keepdims=True) + HEAD_EPSILON)
            out_ref[:, columns] = out
            gated_ref[:, columns] = (
                normed * norm_ref[...] * jax.nn.silu(gate_ref[:, columns])
            ).astype(jnp.bfloat16)

    vmem = pl.BlockSpec(memory_space=pltpu.VMEM)
    width = local_heads * DV
    return pl.pallas_call(
        kernel,
        grid=(1,),
        in_specs=[
            pl.BlockSpec(memory_space=pltpu.SMEM),
            vmem,
            vmem,
            vmem,
            pl.BlockSpec((row_count, width), lambda i: (0, gate_first // width)),
            vmem,
        ],
        out_specs=[vmem, vmem, vmem],
        out_shape=[
            jax.ShapeDtypeStruct((local_heads, DK, DV), jnp.float32),
            jax.ShapeDtypeStruct((row_count, width), jnp.float32),
            jax.ShapeDtypeStruct((row_count, width), jnp.bfloat16),
        ],
        compiler_params=params(),
    )(my_index, handoffs, reach, zero_out, projected, norm_gain)


def mixer_gate_back(local_heads, d_gated, recurred, projected, norm_gain, reach):
    row_count = projected.shape[0]
    gate_first = local_heads * (2 * DK + DV) // DV

    def kernel(d_gated_ref, out_ref, gate_ref, norm_ref, reach_ref, d_out_ref, d_gate_ref, d_norm_ref, d_state_ref):
        out, gate, norm_row, d_gated_now = out_ref[...], gate_ref[...], norm_ref[...], d_gated_ref[...]
        scale = lax.rsqrt(jnp.mean(out * out, axis=-1, keepdims=True) + HEAD_EPSILON)
        normed = out * scale
        logistic = jax.nn.sigmoid(gate)
        silu = gate * logistic
        d_norm = jnp.sum(d_gated_now * normed * silu, axis=0, keepdims=True)

        @pl.when(pl.program_id(0) == 0)
        def _():
            d_norm_ref[...] = jnp.zeros_like(d_norm_ref)

        d_norm_ref[0:1, :] = d_norm_ref[0:1, :] + d_norm
        d_gate_ref[...] = (
            d_gated_now * normed * norm_row * logistic * (1.0 + gate * (1.0 - logistic))
        ).astype(jnp.bfloat16)
        d_normed = d_gated_now * norm_row * silu
        d_out = scale * d_normed - (scale * scale * scale) * out * jnp.mean(
            d_normed * out, axis=-1, keepdims=True
        )
        d_out_ref[...] = d_out
        d_state_ref[0] = product(reach_ref[0], d_out, 0, 0).astype(jnp.bfloat16)

    width = local_heads * DV
    block = pl.BlockSpec((row_count, DV), lambda h: (0, h))
    return pl.pallas_call(
        kernel,
        grid=(local_heads,),
        in_specs=[
            block,
            block,
            pl.BlockSpec((row_count, DV), lambda h: (0, gate_first + h)),
            pl.BlockSpec((1, DV), lambda h: (0, 0)),
            per_head(row_count, DK),
        ],
        out_specs=[block, block, pl.BlockSpec((8, DV), lambda h: (0, 0)), per_head(DK, DV)],
        out_shape=[
            jax.ShapeDtypeStruct((row_count, width), jnp.float32),
            jax.ShapeDtypeStruct((row_count, width), jnp.bfloat16),
            jax.ShapeDtypeStruct((8, DV), jnp.float32),
            jax.ShapeDtypeStruct((local_heads, DK, DV), jnp.bfloat16),
        ],
        compiler_params=params(),
    )(d_gated, recurred, projected, norm_gain, reach)


def relay_back(local_heads, my_index, handoffs, d_enterings):
    devices = handoffs.shape[0]

    def kernel(index_ref, handoffs_ref, d_ref, state_ref):
        state_ref[...] = jnp.zeros_like(state_ref)

        def advance(step, carry):
            j = devices - 1 - step
            for h in range(local_heads):
                state_ref[h] = product(
                    handoffs_ref[j, h, :, :DK].astype(jnp.float32), state_ref[h], 0, 0
                ) + d_ref[j, h].astype(jnp.float32)
            return carry

        lax.fori_loop(0, devices - 1 - index_ref[0], advance, 0)

    vmem = pl.BlockSpec(memory_space=pltpu.VMEM)
    return pl.pallas_call(
        kernel,
        in_specs=[pl.BlockSpec(memory_space=pltpu.SMEM), vmem, vmem],
        out_specs=vmem,
        out_shape=jax.ShapeDtypeStruct((local_heads, DK, DV), jnp.float32),
        compiler_params=params(),
    )(my_index, handoffs, d_enterings)


def conv_back(d_pre, extended, taps_ref, padded, d_block_ref, d_tail_ref, d_rim_ref, d_taps_ref):
    row_count = d_pre.shape[0]
    first = 8 - (KCONV - 1)
    padded[0:8, :] = jnp.zeros((8, d_pre.shape[1]), jnp.float32)
    padded[8 : 8 + row_count, :] = d_pre
    padded[8 + row_count : 16 + row_count, :] = jnp.zeros((8, d_pre.shape[1]), jnp.float32)
    total = None
    d_taps_ref[...] = jnp.zeros_like(d_taps_ref)
    for tap in range(KCONV):
        start = KCONV - 1 - tap
        term = taps_ref[tap : tap + 1, :] * padded[start : start + row_count + 8, :]
        total = term if total is None else total + term
        d_taps_ref[tap : tap + 1, :] = jnp.sum(
            d_pre * extended[first + tap : first + tap + row_count, :], axis=0, keepdims=True
        )
    d_rim_ref[...] = total[0:8, :]
    d_block_ref[...] = total[8:, :].astype(jnp.bfloat16)
    d_tail_ref[...] = total[row_count:, :]


def mixer_back(
    local_heads, projected, rim, taps, decay_proj, scalars,
    solve, fresh, wy_keys, entering_state, d_recurred, d_leaving,
):
    row_count = projected.shape[0]
    three, whole, scalar_spec = mixer_specs(local_heads, row_count)

    def kernel(
        pq, pk, pv, rq, rk, rv, tq, tk, tv, decay_ref, scalars_ref,
        solve_ref, fresh_ref, wy_ref, enter_ref, d_out_ref, d_leave_ref,
        dq_ref, dk_ref, dv_ref, tail_q, tail_k, tail_v, rim_q, rim_k, rim_v,
        taps_q, taps_k, taps_v, d_decay_ref, d_scalars_ref,
        ext_q, ext_k, ext_v, pad_k, pad_v,
    ):
        head = pl.program_id(0)

        @pl.when(head == 0)
        def _():
            d_decay_ref[...] = jnp.zeros_like(d_decay_ref)
            d_scalars_ref[...] = jnp.zeros_like(d_scalars_ref)

        pre_q = convolved(ext_q, pq, rq, tq)
        pre_k = convolved(ext_k, pk, rk, tk)
        pre_v = convolved(ext_v, pv, rv, tv)
        conv_q, conv_k = jax.nn.silu(pre_q), jax.nn.silu(pre_k)
        unit_q, scale_q = unit_rows(conv_q)
        queries = unit_q * DK ** (-0.5)
        key_rows, scale_k = unit_rows(conv_k)
        values = jax.nn.silu(pre_v)
        decay_in, rate, logs, beta, sums, within, row_ids, column_ids = decay_terms(
            head, local_heads, decay_ref, scalars_ref
        )
        strict = row_ids > column_ids
        grown = jnp.exp(sums)
        last = sums[row_count - 1 : row_count, :]
        tail = jnp.exp(last - sums)
        tail_keys = tail * key_rows
        gram = product(key_rows, key_rows, 1, 1)
        scores = jnp.where(strict, gram * within, 0.0)
        attention = product(queries, key_rows, 1, 1) * within
        enter, d_out, d_leave = enter_ref[0], d_out_ref[...], d_leave_ref[0]
        update = fresh_ref[0] - product(wy_ref[0], enter, 1, 0)
        d_update = product(attention, d_out, 0, 0) + product(tail_keys, d_leave, 1, 0)
        d_right = product(solve_ref[0], d_update, 0, 0)
        d_attention = product(d_out, update, 1, 1) * within
        d_system = -product(d_right, update, 1, 1)
        out_state = product(d_out, enter, 1, 1)
        right_state = product(d_right, enter, 1, 1)
        leave_update = product(update, d_leave, 1, 1)
        remainder = values - grown * product(key_rows, enter, 1, 0)
        d_values = beta * d_right
        d_beta = jnp.sum(d_right * remainder, axis=1, keepdims=True) + jnp.sum(
            d_system * scores, axis=1, keepdims=True
        )
        pair = beta * (d_system * scores)
        d_gram = jnp.where(strict, beta * d_system * within, 0.0)
        d_queries = grown * out_state + product(d_attention, key_rows, 1, 0)
        d_keys = (
            product(d_attention, queries, 0, 0)
            + product(d_gram, key_rows, 1, 0)
            + product(d_gram, key_rows, 0, 0)
            + tail * leave_update
            - (beta * grown) * right_state
        )
        both = pair + d_attention * product(queries, key_rows, 1, 1)
        tail_rows = jnp.sum(tail_keys * leave_update, axis=1, keepdims=True)
        diagonal = row_ids == column_ids
        columns = jnp.sum(both, axis=0, keepdims=True)
        d_sums = (
            jnp.sum(both, axis=1, keepdims=True)
            - jnp.sum(jnp.where(diagonal, columns, 0.0), axis=1, keepdims=True)
            + jnp.sum(out_state * (grown * queries), axis=1, keepdims=True)
            - jnp.sum(right_state * ((beta * grown) * key_rows), axis=1, keepdims=True)
            - tail_rows
        )
        d_last = jnp.exp(last) * jnp.sum(
            jnp.sum(d_leave * enter, axis=1, keepdims=True), axis=0, keepdims=True
        ) + jnp.sum(tail_rows, axis=0, keepdims=True)
        d_logs = d_last + jnp.sum(
            jnp.where(row_ids <= column_ids, to_row(d_sums, diagonal), 0.0), axis=1, keepdims=True
        )
        d_decay_in = d_logs * rate * jax.nn.sigmoid(decay_in)
        d_beta_in = d_beta * beta * (1.0 - beta)
        d_decay_ref[...] = (
            d_decay_ref[...]
            + put_lane(d_decay_in, head)
            + put_lane(d_beta_in, head + local_heads)
        )
        d_rate = jnp.sum(d_logs * logs, axis=0, keepdims=True)
        d_bias = jnp.sum(d_decay_in, axis=0, keepdims=True)
        d_scalars_ref[0:1, :] = d_scalars_ref[0:1, :] + put_lane(d_rate, head)
        d_scalars_ref[1:2, :] = d_scalars_ref[1:2, :] + put_lane(d_bias, head)

        def unit_back(d_unit, unit, scale):
            return scale * (d_unit - unit * jnp.sum(unit * d_unit, axis=1, keepdims=True))

        def silu_back(d_act, pre):
            logistic = jax.nn.sigmoid(pre)
            return d_act * logistic * (1.0 + pre * (1.0 - logistic))

        d_pre_q = silu_back(unit_back(d_queries * DK ** (-0.5), unit_q, scale_q), pre_q)
        conv_back(d_pre_q, ext_q, tq, pad_k, dq_ref, tail_q, rim_q, taps_q)
        d_pre_k = silu_back(unit_back(d_keys, key_rows, scale_k), pre_k)
        conv_back(d_pre_k, ext_k, tk, pad_k, dk_ref, tail_k, rim_k, taps_k)
        conv_back(silu_back(d_values, pre_v), ext_v, tv, pad_v, dv_ref, tail_v, rim_v, taps_v)

    def blocks(rows):
        return [
            pl.BlockSpec((rows, DK), lambda h: (0, h)),
            pl.BlockSpec((rows, DK), lambda h: (0, h)),
            pl.BlockSpec((rows, DV), lambda h: (0, h)),
        ]

    def shapes(rows, kind):
        return [
            jax.ShapeDtypeStruct((rows, local_heads * width), kind) for width in (DK, DK, DV)
        ]

    outs = pl.pallas_call(
        kernel,
        grid=(local_heads,),
        in_specs=three(row_count)
        + three(8)
        + three(8)
        + [
            whole,
            scalar_spec,
            per_head(row_count, row_count),
            per_head(row_count, DV),
            per_head(row_count, DK),
            per_head(DK, DV),
            pl.BlockSpec((row_count, DV), lambda h: (0, h)),
            per_head(DK, DV),
        ],
        out_specs=blocks(row_count) + blocks(8) * 3 + [whole, scalar_spec],
        out_shape=shapes(row_count, jnp.bfloat16)
        + shapes(8, jnp.float32) * 3
        + [
            jax.ShapeDtypeStruct((row_count, 128), jnp.float32),
            jax.ShapeDtypeStruct((8, 128), jnp.float32),
        ],
        scratch_shapes=[
            pltpu.VMEM((row_count + 8, DK), jnp.float32),
            pltpu.VMEM((row_count + 8, DK), jnp.float32),
            pltpu.VMEM((row_count + 8, DV), jnp.float32),
            pltpu.VMEM((row_count + 16, DK), jnp.float32),
            pltpu.VMEM((row_count + 16, DV), jnp.float32),
        ],
        compiler_params=params(),
    )(
        *([projected] * 3), *([rim] * 3), *([taps] * 3), decay_proj, scalars,
        solve, fresh, wy_keys, entering_state, d_recurred, d_leaving,
    )
    joined = [jnp.concatenate(outs[3 * i : 3 * i + 3], axis=1) for i in range(4)]
    return (*joined, outs[12], outs[13])


LANES = 128
CHUNK = 32768
TILE = 16
VMEM_LIMIT = 48 * 1024 * 1024


def params(**kwargs):
    return pltpu.CompilerParams(vmem_limit_bytes=VMEM_LIMIT, **kwargs)


def piece_kinds(segments_list, piece_count, piece_size):
    kinds = np.ones(piece_count, np.int32)
    offset_now = 0
    for seg_name, row_count, col_count, seg_rate in segments_list:
        if offset_now >= (piece_count - 1) * piece_size:
            break
        tiles = col_count // LANES
        if tiles in (2, 4, 8, 16):
            first = offset_now // piece_size
            kinds[first : first + row_count * col_count // piece_size] = tiles
        offset_now += row_count * col_count
    return kinds


def pack_blocks(master, slot_kinds, kinds_used):
    capacity, piece_size = master.shape
    chunks = piece_size // CHUNK
    rows = CHUNK // LANES
    slot_blocks = pl.cdiv(capacity, 8)

    def kernel(kinds_ref, master_ref, out_ref, scratch):
        first = pl.program_id(0) * 8
        for j in range(rows):
            scratch[8 * j : 8 * j + 8, :] = master_ref[:, LANES * j : LANES * j + LANES]
        for s in range(8):
            kind_now = kinds_ref[first + s]
            for kind in kinds_used:

                @pl.when(kind_now == kind)
                def _():
                    for tile in range(rows // TILE):
                        row_tile, column = divmod(tile, kind)
                        start = (row_tile * TILE * kind + column) * 8 + s
                        out_ref[s, TILE * tile : TILE * tile + TILE, :] = scratch[
                            pl.ds(start, TILE, stride=8 * kind), :
                        ].astype(jnp.bfloat16)

    return pl.pallas_call(
        kernel,
        grid_spec=pltpu.PrefetchScalarGridSpec(
            num_scalar_prefetch=1,
            grid=(slot_blocks, chunks),
            in_specs=[pl.BlockSpec((8, CHUNK), lambda i, j, kinds: (i, j))],
            out_specs=pl.BlockSpec((8, rows, LANES), lambda i, j, kinds: (i, j, 0)),
            scratch_shapes=[pltpu.VMEM((8 * rows, LANES), jnp.float32)],
        ),
        out_shape=jax.ShapeDtypeStruct((capacity, piece_size // LANES, LANES), jnp.bfloat16),
        compiler_params=params(),
    )(slot_kinds, master)


def tiled_matrix(gathered, positions, col_count, blocks_a_step):
    tiles = col_count // LANES
    piece_rows = gathered.shape[1]
    rows = piece_rows // tiles
    count = positions.shape[0]

    def kernel(positions_ref, *refs):
        out_ref = refs[blocks_a_step]
        for block in range(blocks_a_step):
            for tile in range(piece_rows // TILE):
                row_tile, column = divmod(tile, tiles)
                row = rows * block + TILE * row_tile
                out_ref[row : row + TILE, LANES * column : LANES * column + LANES] = refs[block][
                    0, TILE * tile : TILE * tile + TILE, :
                ]

    return pl.pallas_call(
        kernel,
        grid_spec=pltpu.PrefetchScalarGridSpec(
            num_scalar_prefetch=1,
            grid=(count // blocks_a_step,),
            in_specs=[
                pl.BlockSpec(
                    (1, piece_rows, LANES),
                    lambda g, positions, j=j: (positions[g * blocks_a_step + j], 0, 0),
                )
                for j in range(blocks_a_step)
            ],
            out_specs=pl.BlockSpec((rows * blocks_a_step, col_count), lambda g, positions: (g, 0)),
        ),
        out_shape=jax.ShapeDtypeStruct((count * rows, col_count), jnp.bfloat16),
        compiler_params=params(),
    )(positions, *([gathered] * blocks_a_step))


def spread_matrix(gathered, positions, col_count):
    tiles = col_count // LANES
    rows = gathered.shape[1]
    count = positions.shape[0]
    groups = count // tiles

    def kernel(positions_ref, *refs):
        ins, out_ref, scratch = refs[:tiles], refs[tiles], refs[tiles + 1]
        for j in range(tiles):
            scratch[rows * j : rows * j + rows, :] = ins[j][0].astype(jnp.float32)
        for c in range(tiles):
            out_ref[:, LANES * c : LANES * c + LANES] = scratch[
                pl.ds(c, rows, stride=tiles), :
            ].astype(jnp.bfloat16)

    return pl.pallas_call(
        kernel,
        grid_spec=pltpu.PrefetchScalarGridSpec(
            num_scalar_prefetch=1,
            grid=(groups,),
            in_specs=[
                pl.BlockSpec(
                    (1, rows, LANES), lambda g, positions, j=j: (positions[g * tiles + j], 0, 0)
                )
                for j in range(tiles)
            ],
            out_specs=pl.BlockSpec((rows, col_count), lambda g, positions: (g, 0)),
            scratch_shapes=[pltpu.VMEM((rows * tiles, LANES), jnp.float32)],
        ),
        out_shape=jax.ShapeDtypeStruct((groups * rows, col_count), jnp.bfloat16),
        compiler_params=params(),
    )(positions, *([gathered] * tiles))


def weight_grad_blocks(left_t, right, positions, slots_total, table, blocks_a_step):
    row_total, depth = left_t.shape
    col_count = right.shape[1]
    tiles = col_count // LANES
    piece_rows = 512
    even = tiles in (2, 4, 8, 16)
    step_rows = blocks_a_step * piece_rows // tiles
    steps = row_total // step_rows

    def kernel(positions_ref, left_ref, right_ref, *refs):
        if table is not None:
            refs = refs[1:]
        out_ref, product, staged, sem = refs
        g = pl.program_id(0)
        slot = lax.rem(g, 2)

        def settle(which):
            pltpu.make_async_copy(
                staged.at[which], out_ref.at[pl.ds(0, blocks_a_step)], sem.at[which]
            ).wait()

        @pl.when(g >= 2)
        def _():
            settle(slot)

        left = left_ref[...]
        if even:
            product[...] = jnp.dot(left, right_ref[...], preferred_element_type=jnp.float32)
            for tile in range(step_rows // TILE * tiles):
                row_tile, column = divmod(tile, tiles)
                block, row = divmod(TILE * tile, piece_rows)
                staged[slot, block, row : row + TILE, :] = product[
                    TILE * row_tile : TILE * row_tile + TILE, LANES * column : LANES * column + LANES
                ].astype(jnp.bfloat16)
        else:
            for c in range(0, tiles, 2):
                width = min(2, tiles - c)
                part = jnp.dot(
                    left,
                    right_ref[:, LANES * c : LANES * (c + width)],
                    preferred_element_type=jnp.float32,
                )
                for w in range(width):
                    product[pl.ds(c + w, step_rows, stride=tiles), :] = part[
                        :, LANES * w : LANES * w + LANES
                    ]
            for block in range(blocks_a_step):
                staged[slot, block] = product[
                    piece_rows * block : piece_rows * block + piece_rows, :
                ].astype(jnp.bfloat16)
        for block in range(blocks_a_step):
            pltpu.make_async_copy(
                staged.at[slot, block],
                out_ref.at[positions_ref[g * blocks_a_step + block]],
                sem.at[slot],
            ).start()

        @pl.when(g == steps - 1)
        def _():
            settle(slot)
            if steps > 1:
                settle(1 - slot)

    out_shape = jax.ShapeDtypeStruct((slots_total, piece_rows, LANES), jnp.bfloat16)
    operands = [positions, left_t, right]
    in_specs = [
        pl.BlockSpec((step_rows, depth), lambda g, positions: (g, 0)),
        pl.BlockSpec((depth, col_count), lambda g, positions: (0, 0)),
    ]
    aliases = {}
    if table is not None:
        operands.append(table)
        in_specs.append(pl.BlockSpec(memory_space=pl.ANY))
        aliases = {3: 0}
    product_shape = (step_rows, col_count) if even else (step_rows * tiles, LANES)
    return pl.pallas_call(
        kernel,
        grid_spec=pltpu.PrefetchScalarGridSpec(
            num_scalar_prefetch=1,
            grid=(steps,),
            in_specs=in_specs,
            out_specs=pl.BlockSpec(memory_space=pl.ANY),
            scratch_shapes=[
                pltpu.VMEM(product_shape, jnp.float32),
                pltpu.VMEM((2, blocks_a_step, piece_rows, LANES), jnp.bfloat16),
                pltpu.SemaphoreType.DMA((2,)),
            ],
        ),
        out_shape=out_shape,
        input_output_aliases=aliases,
        cost_estimate=pl.CostEstimate(
            flops=2 * row_total * depth * col_count,
            bytes_accessed=2 * row_total * col_count,
            transcendentals=0,
        ),
        compiler_params=params(),
    )(*operands)


def optimizer_update(
    reduced, slot_kinds, kinds_used, slot_masks, small_rates, master, moment_one, moment_two
):
    capacity, piece_size = master.shape
    chunks = piece_size // CHUNK
    rows = CHUNK // LANES
    slot_blocks = pl.cdiv(capacity, 8)

    def kernel(
        kinds_ref, reduced_ref, masks_ref, small_ref, master_ref, one_ref, two_ref,
        grad_out, master_out, one_out, two_out, low_out, scratch,
    ):
        first = pl.program_id(0) * 8
        for s in range(8):
            kind_now = kinds_ref[first + s]
            for kind in kinds_used:

                @pl.when(kind_now == kind)
                def _():
                    for tile in range(rows // TILE):
                        row_tile, column = divmod(tile, kind)
                        start = (row_tile * TILE * kind + column) * 8 + s
                        scratch[pl.ds(start, TILE, stride=8 * kind), :] = reduced_ref[
                            s, TILE * tile : TILE * tile + TILE, :
                        ].astype(jnp.float32)
        present = masks_ref[0] > 0.5
        is_small = masks_ref[1] > 0.5
        rate_rows = masks_ref[2]
        for j in range(rows):
            lanes = slice(LANES * j, LANES * j + LANES)
            grad = jnp.where(present, scratch[8 * j : 8 * j + 8, :], 0.0)
            rate = jnp.where(is_small, small_ref[:, lanes], rate_rows)
            master_now = master_ref[:, lanes]
            one_new = BETA_ONE * one_ref[:, lanes] + (1.0 - BETA_ONE) * grad
            two_new = BETA_TWO * two_ref[:, lanes] + (1.0 - BETA_TWO) * grad * grad
            first_hat = one_new / (1.0 - BETA_ONE**STEP)
            second_hat = two_new / (1.0 - BETA_TWO**STEP)
            master_new = master_now - rate * (
                first_hat / (jnp.sqrt(second_hat) + ADAM_EPSILON) + WEIGHT_DECAY * master_now
            )
            grad_out[:, lanes] = grad
            master_out[:, lanes] = master_new
            one_out[:, lanes] = one_new
            two_out[:, lanes] = two_new
            low_out[:, lanes] = master_new.astype(jnp.bfloat16)

    state_spec = pl.BlockSpec((8, CHUNK), lambda i, j, kinds: (i, j))
    wide = jax.ShapeDtypeStruct((capacity, piece_size), jnp.float32)
    return pl.pallas_call(
        kernel,
        grid_spec=pltpu.PrefetchScalarGridSpec(
            num_scalar_prefetch=1,
            grid=(slot_blocks, chunks),
            in_specs=[
                pl.BlockSpec((8, rows, LANES), lambda i, j, kinds: (i, j, 0)),
                pl.BlockSpec((3, 8, LANES), lambda i, j, kinds: (0, i, 0)),
                pl.BlockSpec((1, CHUNK), lambda i, j, kinds: (0, j)),
                state_spec,
                state_spec,
                state_spec,
            ],
            out_specs=[state_spec] * 5,
            scratch_shapes=[pltpu.VMEM((8 * rows, LANES), jnp.float32)],
        ),
        out_shape=[wide] * 4 + [jax.ShapeDtypeStruct((capacity, piece_size), jnp.bfloat16)],
        compiler_params=params(),
    )(slot_kinds, reduced, slot_masks, small_rates, master, moment_one, moment_two)


def weight_grad(left, right):
    return jnp.einsum("td,tc->dc", left, right, preferred_element_type=jnp.float32)


def back_product(grad_rows, weight):
    return jnp.dot(grad_rows, weight.T, preferred_element_type=jnp.float32)


def on_device(inputs, cotangent, owners, master, moment_one, moment_two):
    head_parts = lax.axis_size("head")
    seq_parts = lax.axis_size("seq")
    local_heads = HEADS // head_parts
    capacity, piece_size = master.shape
    piece_count = owners.shape[0]
    segments_list = shard_layout(local_heads, head_parts)
    slot_of_piece, piece_of_slot, present = piece_table(owners, seq_parts, capacity)
    my_index = lax.axis_index("seq")
    my_pieces = lax.dynamic_slice_in_dim(piece_of_slot, my_index * capacity, capacity)
    my_present = lax.dynamic_slice_in_dim(present, my_index * capacity, capacity)
    kind_table = piece_kinds(segments_list, piece_count, piece_size)
    kinds_used = sorted(set(kind_table.tolist()) | {1})
    slot_kinds = jnp.where(my_present, jnp.asarray(kind_table)[my_pieces], 1)
    slot_kinds = jnp.pad(slot_kinds, (0, -capacity % 8), constant_values=1)
    gathered = lax.all_gather(
        pack_blocks(master, slot_kinds, kinds_used), "seq", axis=0, tiled=True
    )
    counts = {name: r * c // piece_size for name, r, c, rate in segments_list[:8]}
    firsts = dict(zip(counts, np.cumsum([0] + list(counts.values())).tolist()))
    columns = {name: c for name, r, c, rate in segments_list}

    def positions_of(*names):
        return jnp.concatenate(
            [slot_of_piece[firsts[name] : firsts[name] + counts[name]] for name in names]
        )

    by_name = {}
    for name, blocks_a_step in (("wq", 4), ("wk", 4), ("wv", 8), ("wg", 8), ("wo", 8), ("wdown", 11)):
        by_name[name] = tiled_matrix(gathered, positions_of(name), columns[name], blocks_a_step)
    for name in ("wgate", "wup"):
        by_name[name] = spread_matrix(gathered, positions_of(name), columns[name])
    small_flat = lax.dynamic_index_in_dim(
        gathered, slot_of_piece[piece_count - 1], axis=0, keepdims=False
    ).reshape(-1)
    small_names, small_used = unpack(small_flat, segments_list[8:])
    by_name.update(small_names)
    row_count = inputs.shape[0]
    rim_width = KCONV - 1
    rows_full, back_full, first_norm_scale_factor, second_norm_scale_factor, norm_gain = (
        lax.all_gather(inputs, "head", axis=1, tiled=True),
        lax.all_gather(cotangent, "head", axis=1, tiled=True),
        lax.all_gather(by_name["gainone"].reshape(-1), "head", axis=0, tiled=True),
        lax.all_gather(by_name["gaintwo"].reshape(-1), "head", axis=0, tiled=True),
        lax.all_gather(by_name["wnorm"].reshape(-1), "head", axis=0, tiled=True),
    )
    first_norm_scale_factor = first_norm_scale_factor.astype(jnp.float32)
    second_norm_scale_factor = second_norm_scale_factor.astype(jnp.float32)
    rows_wide = rows_full.astype(jnp.float32)
    scale_one = lax.rsqrt(jnp.mean(rows_wide * rows_wide, axis=-1, keepdims=True) + NORM_EPSILON)
    normed = (rows_wide * scale_one * first_norm_scale_factor).astype(jnp.bfloat16)
    mixer_names = ("wq", "wk", "wv", "wg")
    projected = jnp.concatenate(
        [
            jnp.dot(normed, by_name[name], preferred_element_type=jnp.float32)
            for name in mixer_names
        ],
        axis=1,
    )
    conv_columns = local_heads * (2 * DK + DV)
    decay_weight = jnp.pad(by_name["wab"], ((0, 0), (0, LANES - 2 * local_heads)))
    decay_proj = jnp.dot(normed, decay_weight, preferred_element_type=jnp.float32)
    rim = shifted(projected[row_count - rim_width :, :conv_columns], "seq", 1)
    rim = jnp.pad(rim, ((8 - rim_width, 0), (0, 0)))
    taps = jnp.concatenate([by_name["cq"], by_name["ck"], by_name["cv"]], axis=1)
    taps = jnp.pad(taps.astype(jnp.float32), ((0, 8 - KCONV), (0, 0)))
    scalars = jnp.pad(
        jnp.concatenate([by_name["alog"], by_name["dtbias"]], axis=0).astype(jnp.float32),
        ((0, 6), (0, LANES - local_heads)),
    )
    solve, fresh, wy_keys, reach, zero_out, handoff = mixer_local(
        local_heads, projected, rim, taps, decay_proj, scalars
    )
    handoffs = lax.all_gather(handoff, "seq", axis=0, tiled=False)
    my_index_row = my_index.astype(jnp.int32).reshape(1)
    norm_row = norm_gain.astype(jnp.float32)[None, :]
    entering_state, recurred, gated_low = mixer_out(
        local_heads, my_index_row, handoffs, reach, zero_out, projected, norm_row
    )
    mixed = lax.psum_scatter(
        jnp.dot(gated_low, by_name["wo"], preferred_element_type=jnp.float32).astype(jnp.bfloat16),
        "head",
        scatter_dimension=1,
        tiled=True,
    ).astype(jnp.float32)
    inputs_wide = inputs.astype(jnp.float32)
    residual = inputs_wide + mixed
    resid_low = residual.astype(jnp.bfloat16)
    resid_full = lax.all_gather(resid_low, "head", axis=1, tiled=True).astype(jnp.float32)
    scale_two = lax.rsqrt(jnp.mean(resid_full * resid_full, axis=-1, keepdims=True) + NORM_EPSILON)
    hidden_in = (resid_full * scale_two * second_norm_scale_factor).astype(jnp.bfloat16)
    gate_mlp = jnp.dot(hidden_in, by_name["wgate"], preferred_element_type=jnp.float32)
    up_mlp = jnp.dot(hidden_in, by_name["wup"], preferred_element_type=jnp.float32)
    logistic_output_multiplier = jax.nn.sigmoid(gate_mlp)
    silu_gate = gate_mlp * logistic_output_multiplier
    hidden = (silu_gate * up_mlp).astype(jnp.bfloat16)
    mlp_out = lax.psum_scatter(
        jnp.dot(hidden, by_name["wdown"], preferred_element_type=jnp.float32).astype(jnp.bfloat16),
        "head",
        scatter_dimension=1,
        tiled=True,
    ).astype(jnp.float32)
    block_out = (residual + mlp_out).astype(jnp.bfloat16)
    d_hidden = back_product(back_full, by_name["wdown"])
    d_gate_mlp = (
        d_hidden
        * up_mlp
        * logistic_output_multiplier
        * (1.0 + gate_mlp * (1.0 - logistic_output_multiplier))
    ).astype(jnp.bfloat16)
    d_up_mlp = (d_hidden * silu_gate).astype(jnp.bfloat16)
    slots_total = seq_parts * capacity

    def store_grad(table, name, left, right, blocks_a_step):
        return weight_grad_blocks(
            left.T, right, positions_of(name), slots_total, table, blocks_a_step
        )

    grad_table = store_grad(None, "wdown", hidden, back_full, 11)
    grad_table = store_grad(grad_table, "wgate", hidden_in, d_gate_mlp, 11)
    grad_table = store_grad(grad_table, "wup", hidden_in, d_up_mlp, 11)
    d_hidden_in = back_product(d_gate_mlp, by_name["wgate"]) + back_product(
        d_up_mlp, by_name["wup"]
    )
    dot_two = jnp.sum(d_hidden_in * second_norm_scale_factor * resid_full, axis=-1, keepdims=True)
    d_hidden_mine, dot_two_sum = (
        lax.psum_scatter(
            d_hidden_in.astype(jnp.bfloat16), "head", scatter_dimension=1, tiled=True
        ).astype(jnp.float32),
        lax.psum_scatter(
            jnp.broadcast_to(dot_two, (row_count, head_parts)).astype(jnp.bfloat16),
            "head",
            scatter_dimension=1,
            tiled=True,
        ).astype(jnp.float32),
    )
    resid_mine = resid_low.astype(jnp.float32)
    gain_two_mine = by_name["gaintwo"].reshape(-1).astype(jnp.float32)
    grad_gaintwo = jnp.sum(d_hidden_mine * resid_mine * scale_two, axis=0, keepdims=True)
    d_resid = (
        cotangent.astype(jnp.float32)
        + scale_two * d_hidden_mine * gain_two_mine
        - scale_two**3 / D * resid_mine * dot_two_sum
    )
    back_mix_full = lax.all_gather(d_resid.astype(jnp.bfloat16), "head", axis=1, tiled=True)
    grad_table = store_grad(grad_table, "wo", gated_low, back_mix_full, 8)
    d_gated = back_product(back_mix_full, by_name["wo"])
    d_recurred, d_gate, norm_grad, d_entering = mixer_gate_back(
        local_heads, d_gated, recurred, projected, norm_row, reach
    )
    d_norm_gain = norm_grad[0]
    d_enterings = lax.all_gather(d_entering, "seq", axis=0, tiled=False)
    d_leaving = relay_back(local_heads, my_index_row, handoffs, d_enterings)
    d_conv, d_tail, d_rim, d_taps, d_decay_wide, d_scalars = mixer_back(
        local_heads,
        projected,
        rim,
        taps,
        decay_proj,
        scalars,
        solve,
        fresh,
        wy_keys,
        entering_state,
        d_recurred,
        d_leaving,
    )
    d_rim = shifted(d_rim[8 - rim_width :], "seq", -1)
    d_tail = d_tail + jnp.pad(d_rim, ((8 - rim_width, 0), (0, 0)))
    d_conv = lax.dynamic_update_slice(d_conv, d_tail.astype(jnp.bfloat16), (row_count - 8, 0))
    d_query = d_conv[:, : local_heads * DK]
    d_key = d_conv[:, local_heads * DK : 2 * local_heads * DK]
    d_value = d_conv[:, 2 * local_heads * DK :]
    d_decay = d_decay_wide[:, : 2 * local_heads].astype(jnp.bfloat16)
    d_conv_query = d_taps[:KCONV, : local_heads * DK]
    d_conv_key = d_taps[:KCONV, local_heads * DK : 2 * local_heads * DK]
    d_conv_value = d_taps[:KCONV, 2 * local_heads * DK :]
    d_log_rate = d_scalars[0, :local_heads]
    d_rate_bias = d_scalars[1, :local_heads]
    grad_table = store_grad(grad_table, "wg", normed, d_gate, 8)
    grad_table = store_grad(grad_table, "wv", normed, d_value, 8)
    grad_table = store_grad(grad_table, "wk", normed, d_key, 4)
    grad_table = store_grad(grad_table, "wq", normed, d_query, 4)
    grad_wab = weight_grad(normed, d_decay)
    d_normed = (
        back_product(d_query, by_name["wq"])
        + back_product(d_key, by_name["wk"])
        + back_product(d_value, by_name["wv"])
        + back_product(d_gate, by_name["wg"])
        + back_product(d_decay, by_name["wab"])
    )
    dot_one = jnp.sum(d_normed * first_norm_scale_factor * rows_wide, axis=-1, keepdims=True)
    d_normed_mine, dot_one_sum, grad_wnorm = (
        lax.psum_scatter(
            d_normed.astype(jnp.bfloat16), "head", scatter_dimension=1, tiled=True
        ).astype(jnp.float32),
        lax.psum_scatter(
            jnp.broadcast_to(dot_one, (row_count, head_parts)).astype(jnp.bfloat16),
            "head",
            scatter_dimension=1,
            tiled=True,
        ).astype(jnp.float32),
        lax.psum_scatter(
            d_norm_gain.astype(jnp.bfloat16), "head", scatter_dimension=0, tiled=True
        ).astype(jnp.float32),
    )
    gain_one_mine = by_name["gainone"].reshape(-1).astype(jnp.float32)
    grad_gainone = jnp.sum(d_normed_mine * inputs_wide * scale_one, axis=0, keepdims=True)
    input_grad = (
        d_resid
        + scale_one * d_normed_mine * gain_one_mine
        - scale_one**3 / D * inputs_wide * dot_one_sum
    )
    small_grads = [
        d_conv_query,
        d_conv_key,
        d_conv_value,
        grad_wab,
        d_log_rate,
        d_rate_bias,
        grad_gainone,
        grad_gaintwo,
        grad_wnorm,
    ]
    small_block = jnp.concatenate(
        [grad_now.astype(jnp.bfloat16).reshape(-1) for grad_now in small_grads]
        + [jnp.zeros((piece_size - small_used,), jnp.bfloat16)]
    ).reshape(1, -1, LANES)
    grad_table = lax.dynamic_update_slice(
        grad_table, small_block, (slot_of_piece[piece_count - 1], 0, 0)
    )
    reduced = lax.psum_scatter(grad_table, "seq", scatter_dimension=0, tiled=True)
    piece_rates, small_rates = rate_parts(segments_list, piece_count, piece_size)
    slot_masks = jnp.stack(
        [
            my_present.astype(jnp.float32),
            (my_present & (my_pieces == piece_count - 1)).astype(jnp.float32),
            jnp.where(my_present, jnp.asarray(piece_rates)[my_pieces], PAD_RATE),
        ]
    )
    slot_masks = jnp.pad(slot_masks, ((0, 0), (0, -capacity % 8)))
    slot_masks = jnp.broadcast_to(slot_masks[:, :, None], slot_masks.shape + (LANES,))
    grad_slots, master_new, moment_new, second_new, weights_low = optimizer_update(
        reduced,
        slot_kinds,
        kinds_used,
        slot_masks,
        jnp.asarray(small_rates)[None, :],
        master,
        moment_one,
        moment_two,
    )
    return (
        block_out,
        input_grad,
        grad_slots,
        master_new,
        moment_new,
        second_new,
        weights_low,
    )


def solution(mesh):
    return jax.shard_map(
        on_device,
        mesh=mesh,
        in_specs=(
            P("seq", "head"),
            P("seq", "head"),
            P(),
            P("seq", "head"),
            P("seq", "head"),
            P("seq", "head"),
        ),
        out_specs=(
            P("seq", "head"),
            P("seq", "head"),
            P("seq", "head"),
            P("seq", "head"),
            P("seq", "head"),
            P("seq", "head"),
            P("seq", "head"),
        ),
        check_vma=False,
    )
```

time: 3670 us -> 995 us (0.27)
  local copies, waits for them, and re-layouts: 2090 us -> 53.1 us
  waiting for transfers between devices: 875 us -> 585 us
  other arithmetic: 304 us -> 20.3 us
  Pallas kernels: 0 us -> 193 us
  matrix products: 208 us -> 56.6 us
  starting transfers between devices: 78 us -> 4 us
    gather x6 -> x2, local copies, waits for them, and re-layouts: 1200 us -> 2.53 us  [the longest x1 1.48 us: on_device(): slot_kinds = jnp.where(my_present, jnp.asarray(kind_table)[my_pieces], 1)]
    all_to_all x1 -> x0, waiting for transfers between devices: 543 us -> none  [on_device(): lax.all_to_all(slot_ordered.astype(jnp.bfloat16), 'seq', split_axis=0, co...]
    concatenate x2 -> x1, local copies, waits for them, and re-layouts: 523 us -> 1.16 us  [on_device(): jnp.concatenate([grad_now.astype(jnp.bfloat16).reshape(-1) for grad_now i...]
    unnamed x9 -> x13, waiting for transfers between devices: 1.33 us -> 258 us
    pallas_call x0 -> x23, Pallas kernels: none -> 193 us  [the longest x1 41.3 us: mixer_local(): pl.pallas_call(kernel, grid=(local_heads,), in_specs=three(row_count) + t...]
    dot_general x60 -> x5, matrix products: 122 us -> 6.41 us  [the longest x4 5.6 us: on_device(): jnp.dot(normed, by_name[name], preferred_element_type=jnp.float32)]
    convert_element_type x24 -> x1, other arithmetic: 96.1 us -> 1.27 us  [on_device(): hidden = (silu_gate * up_mlp).astype(jnp.bfloat16)]
    reshape x11 -> x2, local copies, waits for them, and re-layouts: 91.4 us -> 1.41 us  [the longest x1 0.91 us: on_device(): small_flat = lax.dynamic_index_in_dim(gathered, slot_of_piece[piece_count...]
  transfers between devices with their start and end apart: 30 -> 14, of which waited for: 19 -> 10; matrix products, arithmetic and copies ran while one was open for 12% -> 6% of each run, Pallas kernels for 0% -> 10%
where the time goes in v1:
time: 995 us; the launch traced here: 988 us
  waiting for transfers between devices  585 us (59%)
  Pallas kernels  193 us (19%)
  matrix products  56.6 us (6%)
  blocking collectives  56.3 us (6%)
  local copies, waits for them, and re-layouts  53.1 us (5%)
  other arithmetic  20.3 us (2%)
  between operations  19.3 us (2%)
    unnamed x13, waiting for transfers between devices  258 us
    all_gather x1, waiting for transfers between devices, on_device(): lax.all_gather(pack_blocks(master, slot_kinds, kinds_used), 'seq', axis=0...  215 us
    pallas_call x1, Pallas kernels, mixer_local(): pl.pallas_call(kernel, grid=(local_heads,), in_specs=three(row_count) + t...  41.3 us
    pallas_call x1, Pallas kernels, optimizer_update(): pl.pallas_call(kernel, grid_spec=pltpu.PrefetchScalarGridSpec(num_scalar_...  36.9 us
    unnamed x239, local copies, waits for them, and re-layouts  34.4 us
    unnamed x3, blocking collectives  32.4 us
    pallas_call x8, Pallas kernels, weight_grad_blocks(): pl.pallas_call(kernel, grid_spec=pltpu.PrefetchScalarGridSpec(num_scalar_...  32 us
    reduce_scatter x1, waiting for transfers between devices, on_device(): lax.psum_scatter(jnp.dot(gated_low, by_name['wo'], preferred_element_type...  31.2 us
  transfers between devices with their start and end apart: 14, of which 10 were waited for; matrix products, arithmetic and copies ran while one was open for 6% of the time, Pallas kernels for 10%

profile of v1, /device:TPU:0, one launch (start us, length us, event | category | flops | bytes accessed | tf_op | source)
XLA Modules:
  0.0 987.6 jit_solution(5467672687007162276)
XLA Ops:
  7.2 1.8 copy.82
  15.5 13.8 %shard_map.144 = bf16[44,512,128]{2,1,0:T(8,128)(2,1)S(1)} custom-call(s32[48]{0:T(128)S(1)} %pad.36.kinds_ref, f32[44,65536]{1,0:T(8,128)} %master_ref.3), custom_call_target="tpu_custom_call" | custom-call | tf_op jit(solution)/shard_map/pallas_call | solution.py:607
  29.3 2.5 copy-done
  35.1 5.7 all-gather.12.cloned.1.call-done
  42.9 214.5 %all-gather.14.cloned.1.call-done.refs_0_.refs_1_.refs_2_.refs_3_.refs_4_.refs_5_.refs_6_.refs_7_.refs_8_.refs_9_.refs_10_ = bf16[352,512,128]{2,1,0:T(8,128)(2,1)} async-done(((bf16[44,512,128]{2,1,0:T(8,128)(2,1)}), bf16[352,512,128]{2,1,0:T(8,128)(2,1)}) %all-gather.14.cloned.1.call-update) | async-done | bytes 46137360 | tf_op jit(solution)/shard_map/all_gather | solution.py:881
  259.7 11.9 %all-gather.2 = bf16[4,1,512]{2,1,0:T(2,128)(2,1)S(1)} all-gather(bf16[1,1,512]{2,1,0:T(2,128)(2,1)S(1)} %reshape.167), channel_id=1, replica_groups=mesh['head'=4,'seq'=8] {'head'}, dimensions={0}, use_global_device_ids=true | all-gather | bytes 5120 | tf_op jit(solution)/shard_map/all_gather | solution.py:908
  272.2 3.9 shard_map.147
  276.2 4.4 shard_map.146
  283.4 3.1 shard_map.145
  289.5 3.9 shard_map.148
  295.5 2.0 pad_maximum_fusion.pq.pk.pv.gate_ref
  301.3 41.3 %shard_map.149 = (f32[4,256,256]{2,1,0:T(8,128)S(1)}, f32[4,256,256]{2,1,0:T(8,128)S(1)}, f32[4,256,128]{2,1,0:T(8,128)S(1)}, f32[4,256,128]{2,1,0:T(8,128)S(1)}...) custom-call(f32[256,3072]{1,0:T(8,128)} %pad_maximum_fusion.pq.pk.pv.gate_ref, ...), custom_call_target="tpu_custom_call" | custom-call | tf_op jit(solution)/shard_map/pallas_call | solution.py:230
  347.7 10.4 %all-reduce.8 = bf16[256]{0:T(256)(128)(2,1)S(1)} all-reduce(bf16[256]{0:T(256)(128)(2,1)S(1)} %dynamic-update-slice), channel_id=1, replica_groups=mesh['head'=4,'seq'=8] {'head'}, use_global_device_ids=true, to_apply=%add.8 | all-reduce | flops 256 | bytes 1024
  358.1 3.9 shard_map.151
  362.1 2.0 copy-done.14
  364.1 13.4 %all-gather.22.cloned.1.call-done = bf16[32,128,384]{2,1,0:T(8,128)(2,1)} async-done(((bf16[4,128,384]{2,1,0:T(8,128)(2,1)}), bf16[32,128,384]{2,1,0:T(8,128)(2,1)}) %all-gather.22.cloned.1.call-update) | async-done | bytes 3145744 | tf_op jit(solution)/shard_map/all_gather | solution.py:939
  377.5 3.7 shard_map.150
  382.8 2.8 convolution_convert_fusion
  385.7 31.2 %reduce-scatter.8.cloned.1.call-done = bf16[256,512]{0,1:T(8,128)(2,1)} async-done(((bf16[256,2048]{0,1:T(8,128)(2,1)}), bf16[256,512]{0,1:T(8,128)(2,1)}) %reduce-scatter.8.cloned.1.call-update) | async-done | bytes 262160 | tf_op jit(solution)/shard_map/reduce_scatter | solution.py:945
  416.9 1.7 fusion.29
  419.3 12.0 %all-gather.3 = bf16[4,1,512]{2,1,0:T(2,128)(2,1)S(1)} all-gather(bf16[1,1,512]{2,1,0:T(2,128)(2,1)S(1)} %reshape.169), channel_id=1, replica_groups=mesh['head'=4,'seq'=8] {'head'}, dimensions={0}, use_global_device_ids=true | all-gather | bytes 5120 | tf_op jit(solution)/shard_map/all_gather | solution.py:909
  431.9 5.1 shard_map.153
  437.1 2.5 copy-done.8
  439.6 5.2 shard_map.152
  444.8 2.5 copy-done.9
  447.3 4.6 shard_map.154
  452.0 2.5 copy-done.7
  456.1 6.2 fusion.65
  462.2 3.1 fusion.67
  465.3 9.0 all-gather.18.cloned.1.call-done.right_ref
  474.3 5.9 multiply_convert_fusion
  480.3 5.0 fusion.86
  485.3 6.1 fusion.80
  491.7 10.3 %all-reduce.9 = bf16[256,4]{0,1:T(4,128)(2,1)S(1)} all-reduce(bf16[256,4]{0,1:T(4,128)(2,1)S(1)} %broadcast_in_dim.27), channel_id=7, replica_groups=mesh['head'=4,'seq'=8] {'head'}, use_global_device_ids=true, to_apply=%region_11.12.clone | all-reduce | flops 1024 | bytes 4096
  502.6 15.7 %reduce-scatter.12.cloned.1.call-done = bf16[256,512]{0,1:T(8,128)(2,1)} async-done(((bf16[256,2048]{0,1:T(8,128)(2,1)}), bf16[256,512]{0,1:T(8,128)(2,1)}) %reduce-scatter.12.cloned.1.call-update) | async-done | bytes 262160 | tf_op jit(solution)/shard_map/reduce_scatter | solution.py:992
  518.3 1.8 fusion.32
  520.6 26.4 %all-gather.20.cloned.1.call-done = bf16[256,2048]{0,1:T(8,128)(2,1)} async-done(((bf16[256,512]{0,1:T(8,128)(2,1)}), bf16[256,2048]{0,1:T(8,128)(2,1)}) %all-gather.20.cloned.1.call-update) | async-done | bytes 1048592 | tf_op jit(solution)/shard_map/all_gather | solution.py:1010
  547.0 3.8 fusion.87.d_gated_ref
  550.9 4.7 shard_map.155
  559.0 1.8 copy.97
  560.8 1.8 copy.96
  562.6 7.3 convolution_convert_fusion.1
  571.2 5.1 fusion.88
  576.3 8.5 all-gather.24.cloned.1.call-done
  584.9 1.6 copy-done.22
  586.5 4.7 shard_map.156.d_leave_ref
  591.3 22.2 %shard_map.157 = (bf16[256,512]{1,0:T(8,128)(2,1)S(1)}, bf16[256,512]{1,0:T(8,128)(2,1)S(1)}, bf16[256,1024]{1,0:T(8,128)(2,1)S(1)}, f32[8,512]{1,0:T(8,128)S(1)...) custom-call(f32[256,3072]{1,0:T(8,128)} %pad_maximum_fusion.pq.pk.pv, ...), custom_call_target="tpu_custom_call" | custom-call | tf_op jit(solution)/shard_map/pallas_call | solution.py:521
  615.0 1.7 collective-permute-done.1
  617.5 1.8 copy-done.12
  622.9 1.7 fusion.5
  626.2 4.4 shard_map.158.refs_0_
  630.7 4.9 shard_map.159.refs_0_
  635.6 4.9 shard_map.160.refs_0_
  640.5 1.5 copy.98.right_ref
  642.1 3.9 shard_map.161.refs_0_
  648.5 11.7 %all-reduce.13 = (bf16[256,4]{0,1:T(4,128)(2,1)S(1)}, bf16[256]{0:T(256)(128)(2,1)S(1)}) all-reduce(bf16[256,4]{0,1:T(4,128)(2,1)S(1)} %broadcast_in_dim.28, bf16[256]{0:T(256)(128)(2,1)S(1)} %fusion.55), channel_id=9, replica_groups=mesh['head'=4,'seq'=8] {'head'}, use_global_device_ids=true, to_apply=%region_14.15.clone | all-reduce | flops 1280 | bytes 5120
  660.3 3.9 shard_map.162.refs_0_
  664.2 3.9 shard_map.163.refs_0_
  668.2 3.1 shard_map.164.refs_0_
  671.4 3.1 shard_map.165
  675.3 1.7 fusion.20
  683.2 257.6 %reduce-scatter.16.cloned.1.call-done.reduced_ref = bf16[44,512,128]{2,1,0:T(8,128)(2,1)} async-done(((bf16[352,512,128]{2,1,0:T(8,128)(2,1)}), bf16[44,512,128]{2,1,0:T(8,128)(2,1)}) %reduce-scatter.16.cloned.1.call-update) | async-done | bytes 5767184
  940.9 2.6 copy-done.6
  943.5 36.9 %shard_map.166 = (f32[44,65536]{1,0:T(8,128)}, f32[44,65536]{1,0:T(8,128)}, f32[44,65536]{1,0:T(8,128)}, f32[44,65536]{1,0:T(8,128)}, bf16[44,65536]{1,0:T(8,128)(2,1)}) custom-call(s32[48]{0:T(128)S(1)} %copy-done.64, bf16[44,512,128]{2,1,0:T(8,128)(2,1)S(1)} %copy-done.6, f32[3,48,128]{2,1,0:T(8,128)S(1)} %broadcast_in_dim.32.masks_ref, ...), custom_call_target="tpu_custom_call" | custom-call | tf_op jit(solution)/shard_map/pallas_call | solution.py:837
  (335 shorter events, 55.6 us)
Async XLA Ops:
  7.2 33.6 %all-gather.12.cloned.1.call-start = ((), (), s32[]{:S(2)}) async-start(), calls=%async_computation.5 | async-start | bytes 1310720 | tf_op jit(solution)/shard_map/all_gather | solution.py:906
  9.0 248.5 %all-gather.14.cloned.1.call-start = ((), (), s32[]{:S(2)}) async-start(), calls=%async_computation.6 | async-start | bytes 51904512 | tf_op jit(solution)/shard_map/all_gather | solution.py:881
  12.4 22.6 %copy-start.86 = (s32[261]{0:T(512)}, s32[261]{0:T(512)S(1)}, u32[]{:S(2)}) copy-start(s32[261]{0:T(512)S(1)} %multiply_add_fusion) | copy-start | bytes 3136
  13.2 16.1 %copy-start.102 = (s32[1024]{0:T(1024)}, s32[1024]{0:T(1024)S(1)}, u32[]{:S(2)}) copy-start(s32[1024]{0:T(1024)S(1)} %pad_clamp_fusion) | copy-start | bytes 12292
  15.4 13.8 %copy-start.110 = (pred[44]{0:T(512)(128)(4,1)}, pred[44]{0:T(512)(128)(4,1)S(1)}, u32[]{:S(2)}) copy-start(pred[44]{0:T(512)(128)(4,1)S(1)} %get-tuple-element.102) | copy-start | bytes 136
  32.4 345.1 %all-gather.22.cloned.1.call-start = ((), (), s32[]{:S(2)}) async-start(), calls=%async_computation.14 | async-start | bytes 3538944 | tf_op jit(solution)/shard_map/all_gather | solution.py:939
  35.0 241.1 %copy-start.49 = (s32[16]{0:T(128)}, s32[16]{0:T(128)S(1)}, u32[]{:S(2)}) copy-start(s32[16]{0:T(128)S(1)} %get-tuple-element.134.positions_ref) | copy-start | bytes 196
  35.0 248.4 %copy-start.47 = (s32[16]{0:T(128)}, s32[16]{0:T(128)S(1)}, u32[]{:S(2)}) copy-start(s32[16]{0:T(128)S(1)} %get-tuple-element.133.positions_ref) | copy-start | bytes 196
  35.1 241.0 %copy-start.51 = (s32[32]{0:T(128)}, s32[32]{0:T(128)S(1)}, u32[]{:S(2)}) copy-start(s32[32]{0:T(128)S(1)} %get-tuple-element.132.positions_ref) | copy-start | bytes 388
  35.1 254.4 %copy-start.53 = (s32[32]{0:T(128)}, s32[32]{0:T(128)S(1)}, u32[]{:S(2)}) copy-start(s32[32]{0:T(128)S(1)} %get-tuple-element.131.positions_ref) | copy-start | bytes 388
  35.1 323.0 %copy-start.55 = (s32[32]{0:T(128)}, s32[32]{0:T(128)S(1)}, u32[]{:S(2)}) copy-start(s32[32]{0:T(128)S(1)} %get-tuple-element.130.positions_ref) | copy-start | bytes 388
  258.4 17.7 %copy-start.85 = (bf16[65536]{0:T(1024)(128)(2,1)}, bf16[65536]{0:T(1024)(128)(2,1)S(1)}, u32[]{:S(2)}) copy-start(bf16[65536]{0:T(1024)(128)(2,1)S(1)} %dynamic-slice_bitcast_fusion) | copy-start | bytes 393220
  288.0 13.2 %collective-permute-start = (f32[3,2048]{1,0:T(4,128)S(1)}, f32[3,2048]{1,0:T(4,128)S(1)}, u32[]{:S(2)}, u32[]{:S(2)}) collective-permute-start(f32[3,2048]{1,0:T(4,128)S(1)} %pad_maximum_fusion.4), channel_id=1, source_target_pairs={{0,1},{1,2},{2,3},{3,4},{4,5},{5,6},{6,7},{8,9},{9,10},{10,11},{11... | collective-permute-start | bytes 73736 | tf_op jit(solution)/shard_map/ppermute | solution.py:32
  300.3 42.2 %copy-start.77 = (bf16[2048,8]{1,0:T(8,128)(2,1)}, bf16[2048,8]{1,0:T(8,128)(2,1)S(1)}, u32[]{:S(2)}) copy-start(bf16[2048,8]{1,0:T(8,128)(2,1)S(1)} %reshape.130) | copy-start | bytes 98308
  300.3 42.2 %copy-start.17 = (f32[8,2048]{1,0:T(8,128)}, f32[8,2048]{1,0:T(8,128)S(1)}, u32[]{:S(2)}) copy-start(f32[8,2048]{1,0:T(8,128)S(1)} %fusion.40.tq.tk.tv) | copy-start | bytes 196612
  301.2 41.4 %copy-start.34 = (f32[256,128]{1,0:T(8,128)}, f32[256,128]{1,0:T(8,128)S(1)}, u32[]{:S(2)}) copy-start(f32[256,128]{1,0:T(8,128)S(1)} %fusion.27.decay_ref) | copy-start | bytes 393220
  301.2 41.3 %copy-start.45 = (f32[8,128]{1,0:T(8,128)}, f32[8,128]{1,0:T(8,128)S(1)}, u32[]{:S(2)}) copy-start(f32[8,128]{1,0:T(8,128)S(1)} %fusion.52.scalars_ref) | copy-start | bytes 12292
  301.2 41.3 %copy-start.19 = (f32[8,2048]{1,0:T(8,128)}, f32[8,2048]{1,0:T(8,128)S(1)}, u32[]{:S(2)}) copy-start(f32[8,2048]{1,0:T(8,128)S(1)} %pad.37.rq.rk.rv) | copy-start | bytes 196612
  301.3 44.2 %copy-start.106 = (u32[32]{0:T(128)S(1)}, u32[32]{0:T(128)}, u32[]{:S(2)}) copy-start(u32[32]{0:T(128)} %constant.82) | copy-start | bytes 388
  345.4 71.5 %reduce-scatter.8.cloned.1.call-start = ((), (), s32[]{:S(2)}) async-start(), calls=%async_computation.7 | async-start | bytes 1310720 | tf_op jit(solution)/shard_map/reduce_scatter | solution.py:945
  358.1 19.4 %copy-start.61 = (f32[256]{0:T(256)}, f32[256]{0:T(256)S(1)}, u32[]{:S(2)}) copy-start(f32[256]{0:T(256)S(1)} %broadcast_in_dim.34) | copy-start | bytes 3076
  377.5 5.3 copy-start.15
  382.8 34.1 %copy-start.73 = (bf16[256,512]{0,1:T(8,128)(2,1)S(1)}, bf16[256,512]{0,1:T(8,128)(2,1)}, u32[]{:S(2)}) copy-start(bf16[256,512]{0,1:T(8,128)(2,1)} %copy.82) | copy-start | bytes 786436
  385.6 33.6 %copy-start.87 = (s32[261]{0:T(512)S(1)}, s32[261]{0:T(512)}, u32[]{:S(2)}) copy-start(s32[261]{0:T(512)} %copy-done.86) | copy-start | bytes 3136
  385.6 33.7 %copy-start.104 = (bf16[512]{0:T(512)(128)(2,1)S(1)}, bf16[512]{0:T(512)(128)(2,1)}, u32[]{:S(2)}) copy-start(bf16[512]{0:T(512)(128)(2,1)} %get-tuple-element.121) | copy-start | bytes 3076
  385.6 68.8 %all-gather.16.cloned.1.call-start = ((), (), s32[]{:S(2)}) async-start(), calls=%async_computation.8 | async-start | bytes 1310720 | tf_op jit(solution)/shard_map/all_gather | solution.py:954
  418.6 55.7 %all-gather.18.cloned.1.call-start = ((), (), s32[]{:S(2)}) async-start(), calls=%async_computation.10 | async-start | bytes 1310720 | tf_op jit(solution)/shard_map/all_gather | solution.py:907
  419.2 99.1 %reduce-scatter.12.cloned.1.call-start = ((), (), s32[]{:S(2)}) async-start(), calls=%async_computation.11 | async-start | bytes 1310720 | tf_op jit(solution)/shard_map/reduce_scatter | solution.py:992
  419.3 17.8 %copy-start.57 = (s32[44]{0:T(128)}, s32[44]{0:T(128)S(1)}, u32[]{:S(2)}) copy-start(s32[44]{0:T(128)S(1)} %get-tuple-element.129.positions_ref) | copy-start | bytes 532
  419.3 20.3 %copy-start.59 = (s32[44]{0:T(128)}, s32[44]{0:T(128)S(1)}, u32[]{:S(2)}) copy-start(s32[44]{0:T(128)S(1)} %get-tuple-element.127.positions_ref) | copy-start | bytes 532
  447.3 8.7 copy-start.101
  456.0 62.3 %copy-start.94 = (f32[256]{0:T(256)}, f32[256]{0:T(256)S(1)}, u32[]{:S(2)}) copy-start(f32[256]{0:T(256)S(1)} %get-tuple-element.137) | copy-start | bytes 3076
  456.0 62.3 %copy-start.96 = (f32[256]{0:T(256)}, f32[256]{0:T(256)S(1)}, u32[]{:S(2)}) copy-start(f32[256]{0:T(256)S(1)} %get-tuple-element.138) | copy-start | bytes 3076
  456.0 6.2 copy-start.10
  456.1 6.2 copy-start.82
  480.2 5.0 copy-start.32
  480.2 5.0 copy-start.30
  480.3 5.0 copy-start.83
  485.3 6.2 copy-start.84
  485.3 33.0 %copy-start.68 = (bf16[256,512]{0,1:T(8,128)(2,1)S(1)}, bf16[256,512]{0,1:T(8,128)(2,1)}, u32[]{:S(2)}) copy-start(bf16[256,512]{0,1:T(8,128)(2,1)} %fusion.29) | copy-start | bytes 786436
  485.3 33.0 %copy-start.90 = (f32[512]{0:T(512)S(1)}, f32[512]{0:T(512)}, u32[]{:S(2)}) copy-start(f32[512]{0:T(512)} %get-tuple-element.120) | copy-start | bytes 6148
  491.5 55.6 %all-gather.20.cloned.1.call-start = ((), (), s32[]{:S(2)}) async-start(), calls=%async_computation.12 | async-start | bytes 1310720 | tf_op jit(solution)/shard_map/all_gather | solution.py:1010
  491.7 59.2 %copy-start.75 = (bf16[256,512]{0,1:T(8,128)(2,1)}, bf16[256,512]{0,1:T(8,128)(2,1)S(1)}, u32[]{:S(2)}) copy-start(bf16[256,512]{0,1:T(8,128)(2,1)S(1)} %copy.86) | copy-start | bytes 786436
  502.6 18.0 %copy-start.98 = (f32[256,1]{0,1:T(1,128)}, f32[256,1]{0,1:T(1,128)S(1)}, u32[]{:S(2)}) copy-start(f32[256,1]{0,1:T(1,128)S(1)} %dynamic-slice_convert_fusion.1) | copy-start | bytes 3076
  520.2 30.7 %copy-start.62 = (f32[256]{0:T(256)S(1)}, f32[256]{0:T(256)}, u32[]{:S(2)}) copy-start(f32[256]{0:T(256)} %copy-done.61) | copy-start | bytes 3076
  520.2 64.7 %all-gather.24.cloned.1.call-start = ((), (), s32[]{:S(2)}) async-start(), calls=%async_computation.15 | async-start | bytes 2359296 | tf_op jit(solution)/shard_map/all_gather | solution.py:1017
  550.9 7.2 copy-start.41
  557.3 117.8 %reduce-scatter.10.cloned.1.call-start = ((), (), s32[]{:S(2)}) async-start(), calls=%async_computation.9 | async-start | bytes 1310720 | tf_op jit(solution)/shard_map/reduce_scatter | solution.py:962
  569.9 105.3 %reduce-scatter.14.cloned.1.call-start = ((), (), s32[]{:S(2)}) async-start(), calls=%async_computation.13 | async-start | bytes 1310720 | tf_op jit(solution)/shard_map/reduce_scatter | solution.py:1059
  571.2 13.6 %copy-start.3 = (bf16[32,128,384]{2,1,0:T(8,128)(2,1)S(1)}, bf16[32,128,384]{2,1,0:T(8,128)(2,1)}, u32[]{:S(2)}) copy-start(bf16[32,128,384]{2,1,0:T(8,128)(2,1)} %all-gather.22.cloned.1.call-done) | copy-start | bytes 9437188
  586.5 4.8 copy-start.28
  586.5 4.8 copy-start.35
  586.5 4.8 copy-start.37
  586.5 4.8 copy-start.39
  586.5 4.8 copy-start.46
  613.5 3.2 collective-permute-start.1
  624.7 6.0 copy-start.16
  624.7 316.1 %reduce-scatter.16.cloned.1.call-start = ((), (), s32[]{:S(2)}) async-start(), calls=%async_computation.16 | async-start | bytes 51904512
  630.7 4.9 copy-start.31
  630.7 4.9 copy-start.58
  646.1 14.2 %copy-start.43 = (bf16[256,1024]{1,0:T(8,128)(2,1)S(1)}, bf16[256,1024]{1,0:T(8,128)(2,1)}, u32[]{:S(2)}) copy-start(bf16[256,1024]{1,0:T(8,128)(2,1)} %copy-done.42) | copy-start | bytes 1572868
  646.1 14.2 %copy-start.54 = (s32[32]{0:T(128)S(1)}, s32[32]{0:T(128)}, u32[]{:S(2)}) copy-start(s32[32]{0:T(128)} %copy-done.53) | copy-start | bytes 388
  679.6 261.3 %copy-start.44 = (f32[1,65536]{1,0:T(1,128)S(1)}, f32[1,65536]{1,0:T(1,128)}, u32[]{:S(2)}) copy-start(f32[1,65536]{1,0:T(1,128)} %constant.79.small_ref) | copy-start | bytes 786436
  679.6 261.3 %copy-start.64 = (s32[48]{0:T(128)S(1)}, s32[48]{0:T(128)}, u32[]{:S(2)}) copy-start(s32[48]{0:T(128)} %copy-done.63) | copy-start | bytes 580
  (62 other events, 169.0 us)
Sparse Core Ops, SparseCore 0:
  10.1 30.6 all-gather.11
  43.3 214.1 all-gather.13
  345.5 31.9 all-gather.21
  385.7 31.0 reduce-scatter.7
  418.7 26.5 all-gather.15
  446.9 27.4 all-gather.17
  491.6 26.6 reduce-scatter.11
  520.4 26.5 all-gather.19
  557.5 27.3 all-gather.23
  587.6 27.1 reduce-scatter.9
  624.8 28.1 reduce-scatter.13
  679.0 261.7 reduce-scatter.15

commit v2 on v1

--- a/solution.py
+++ b/solution.py
@@ -256,16 +256,16 @@
     )(*([projected] * 3), *([rim] * 3), *([taps] * 3), decay_proj, scalars)
 
 
-def mixer_out(local_heads, my_index, handoffs, reach, zero_out, projected, norm_gain):
+def mixer_out(local_heads, my_index, base, handoffs, reach, zero_out, projected, norm_gain):
     row_count = projected.shape[0]
     gate_first = local_heads * (2 * DK + DV)
 
-    def kernel(index_ref, handoffs_ref, reach_ref, zero_ref, gate_ref, norm_ref, state_ref, out_ref, gated_ref):
+    def kernel(index_ref, base_ref, handoffs_ref, reach_ref, zero_ref, gate_ref, norm_ref, state_ref, out_ref, gated_ref):
         state_ref[...] = jnp.zeros_like(state_ref)
 
         def advance(j, carry):
             for h in range(local_heads):
-                block = handoffs_ref[j, h]
+                block = handoffs_ref[j ^ base_ref[0], h]
                 state_ref[h] = product(
                     block[:, :DK].astype(jnp.float32), state_ref[h], 1, 0
                 ) + block[:, DK:].astype(jnp.float32)
@@ -287,6 +287,7 @@
         kernel,
         grid=(1,),
         in_specs=[
+            pl.BlockSpec(memory_space=pltpu.SMEM),
             pl.BlockSpec(memory_space=pltpu.SMEM),
             vmem,
             vmem,
@@ -301,7 +302,7 @@
             jax.ShapeDtypeStruct((row_count, width), jnp.bfloat16),
         ],
         compiler_params=params(),
-    )(my_index, handoffs, reach, zero_out, projected, norm_gain)
+    )(my_index, base, handoffs, reach, zero_out, projected, norm_gain)
 
 
 def mixer_gate_back(local_heads, d_gated, recurred, projected, norm_gain, reach):
@@ -354,14 +355,14 @@
     )(d_gated, recurred, projected, norm_gain, reach)
 
 
-def relay_back(local_heads, my_index, handoffs, d_enterings):
+def relay_back(local_heads, my_index, base, handoffs, d_enterings):
     devices = handoffs.shape[0]
 
-    def kernel(index_ref, handoffs_ref, d_ref, state_ref):
+    def kernel(index_ref, base_ref, handoffs_ref, d_ref, state_ref):
         state_ref[...] = jnp.zeros_like(state_ref)
 
         def advance(step, carry):
-            j = devices - 1 - step
+            j = (devices - 1 - step) ^ base_ref[0]
             for h in range(local_heads):
                 state_ref[h] = product(
                     handoffs_ref[j, h, :, :DK].astype(jnp.float32), state_ref[h], 0, 0
@@ -373,11 +374,11 @@
     vmem = pl.BlockSpec(memory_space=pltpu.VMEM)
     return pl.pallas_call(
         kernel,
-        in_specs=[pl.BlockSpec(memory_space=pltpu.SMEM), vmem, vmem],
+        in_specs=[pl.BlockSpec(memory_space=pltpu.SMEM)] * 2 + [vmem, vmem],
         out_specs=vmem,
         out_shape=jax.ShapeDtypeStruct((local_heads, DK, DV), jnp.float32),
         compiler_params=params(),
-    )(my_index, handoffs, d_enterings)
+    )(my_index, base, handoffs, d_enterings)
 
 
 def conv_back(d_pre, extended, taps_ref, padded, d_block_ref, d_tail_ref, d_rim_ref, d_taps_ref):
@@ -560,6 +561,11 @@
 LANES = 128
 CHUNK = 32768
 TILE = 16
+CAPACITY_UNIT = 44
+FIRST_GATHER = 24
+FIRST_REDUCE = 20
+SECOND_REDUCE = 24
+TABLE = 1 << 16
 VMEM_LIMIT = 48 * 1024 * 1024
 
 
@@ -581,14 +587,15 @@
     return kinds
 
 
-def pack_blocks(master, slot_kinds, kinds_used):
-    capacity, piece_size = master.shape
+def pack_blocks(master, slot_kinds, kinds_used, first_slot, slot_count):
+    piece_size = master.shape[1]
     chunks = piece_size // CHUNK
     rows = CHUNK // LANES
-    slot_blocks = pl.cdiv(capacity, 8)
+    first_block = first_slot // 8
+    slot_blocks = pl.cdiv(slot_count, 8)
 
     def kernel(kinds_ref, master_ref, out_ref, scratch):
-        first = pl.program_id(0) * 8
+        first = (first_block + pl.program_id(0)) * 8
         for j in range(rows):
             scratch[8 * j : 8 * j + 8, :] = master_ref[:, LANES * j : LANES * j + LANES]
         for s in range(8):
@@ -609,87 +616,238 @@
         grid_spec=pltpu.PrefetchScalarGridSpec(
             num_scalar_prefetch=1,
             grid=(slot_blocks, chunks),
-            in_specs=[pl.BlockSpec((8, CHUNK), lambda i, j, kinds: (i, j))],
+            in_specs=[pl.BlockSpec((8, CHUNK), lambda i, j, kinds: (first_block + i, j))],
             out_specs=pl.BlockSpec((8, rows, LANES), lambda i, j, kinds: (i, j, 0)),
             scratch_shapes=[pltpu.VMEM((8 * rows, LANES), jnp.float32)],
         ),
-        out_shape=jax.ShapeDtypeStruct((capacity, piece_size // LANES, LANES), jnp.bfloat16),
+        out_shape=jax.ShapeDtypeStruct((slot_count, piece_size // LANES, LANES), jnp.bfloat16),
         compiler_params=params(),
     )(slot_kinds, master)
 
 
-def tiled_matrix(gathered, positions, col_count, blocks_a_step):
-    tiles = col_count // LANES
-    piece_rows = gathered.shape[1]
-    rows = piece_rows // tiles
-    count = positions.shape[0]
-
-    def kernel(positions_ref, *refs):
-        out_ref = refs[blocks_a_step]
-        for block in range(blocks_a_step):
-            for tile in range(piece_rows // TILE):
-                row_tile, column = divmod(tile, tiles)
-                row = rows * block + TILE * row_tile
-                out_ref[row : row + TILE, LANES * column : LANES * column + LANES] = refs[block][
-                    0, TILE * tile : TILE * tile + TILE, :
-                ]
-
+def reserve(shape, kind):
+    def kernel(out_ref):
+        pass
+
+    return pl.pallas_call(
+        kernel,
+        out_specs=pl.BlockSpec(memory_space=pl.ANY),
+        out_shape=jax.ShapeDtypeStruct(shape, kind),
+        compiler_params=params(),
+    )()
+
+
+def assemble(tables, matrices, step_rows, rows_in=None):
+    piece_rows = tables[0].shape[1]
+    plans = []
+    first_block, first_column = 0, 0
+    for positions, col_count in matrices:
+        tiles = col_count // LANES
+        blocks = step_rows * tiles // piece_rows
+        plans.append((first_block, first_column, tiles, blocks))
+        first_block += blocks
+        first_column += col_count
+    blocks_a_step, width = first_block, first_column
+    steps = matrices[0][0].shape[0] // plans[0][3]
+    order = jnp.concatenate(
+        [
+            positions.reshape(steps, plan[3])
+            for (positions, col_count), plan in zip(matrices, plans)
+        ],
+        axis=1,
+    ).reshape(-1)
+    uneven = [plan for plan in plans if piece_rows * plan[3] != step_rows * plan[2] or plan[2] not in (2, 4, 8, 16)]
+    multiply = rows_in is not None
+
+    def kernel(order_ref, *refs):
+        if multiply:
+            rows_ref, refs = refs[0], refs[1:]
+        table_refs, refs = refs[: len(tables)], refs[len(tables) :]
+        out_ref, refs = refs[0], refs[1:]
+        if multiply:
+            product_ref, refs = refs[0], refs[1:]
+        buffer, sem, scratch = refs
+        g = pl.program_id(0)
+        slot = lax.rem(g, 2)
+
+        def start(step, which):
+            def one(j, carry):
+                position = order_ref[step * blocks_a_step + j]
+                for number, table_ref in enumerate(table_refs):
+
+                    @pl.when(position // TABLE == number)
+                    def _():
+                        pltpu.make_async_copy(
+                            table_ref.at[lax.rem(position, TABLE)],
+                            buffer.at[which, j],
+                            sem.at[which],
+                        ).start()
+
+                return carry
+
+            lax.fori_loop(0, blocks_a_step, one, 0)
+
+        @pl.when(g == 0)
+        def _():
+            start(0, 0)
+
+        @pl.when(g + 1 < steps)
+        def _():
+            start(g + 1, 1 - slot)
+
+        pltpu.make_async_copy(buffer.at[slot], buffer.at[slot], sem.at[slot]).wait()
+        for plan in plans:
+            first, left, tiles, blocks = plan
+            if plan in uneven:
+                for j in range(blocks):
+                    scratch[piece_rows * j : piece_rows * j + piece_rows, :] = buffer[
+                        slot, first + j
+                    ].astype(jnp.float32)
+                for c in range(tiles):
+                    out_ref[:, left + LANES * c : left + LANES * c + LANES] = scratch[
+                        pl.ds(c, step_rows, stride=tiles), :
+                    ].astype(jnp.bfloat16)
+                continue
+            for j in range(blocks):
+                for tile in range(piece_rows // TILE):
+                    row_tile, column = divmod(tile, tiles)
+                    row = piece_rows // tiles * j + TILE * row_tile
+                    column = left + LANES * column
+                    out_ref[row : row + TILE, column : column + LANES] = buffer[
+                        slot, first + j, TILE * tile : TILE * tile + TILE, :
+                    ]
+        if multiply:
+            part = jnp.dot(rows_ref[...], out_ref[...], preferred_element_type=jnp.float32)
+
+            @pl.when(g == 0)
+            def _():
+                product_ref[...] = part
+
+            @pl.when(g > 0)
+            def _():
+                product_ref[...] = product_ref[...] + part
+
+    anywhere = pl.BlockSpec(memory_space=pl.ANY)
+    in_specs = [anywhere for table in tables]
+    operands = list(tables)
+    out_specs = [pl.BlockSpec((step_rows, width), lambda g, order: (g, 0))]
+    out_shape = [jax.ShapeDtypeStruct((steps * step_rows, width), jnp.bfloat16)]
+    if multiply:
+        row_count = rows_in.shape[0]
+        in_specs.insert(0, pl.BlockSpec((row_count, step_rows), lambda g, order: (0, g)))
+        operands.insert(0, rows_in)
+        out_specs.append(pl.BlockSpec((row_count, width), lambda g, order: (0, 0)))
+        out_shape.append(jax.ShapeDtypeStruct((row_count, width), jnp.float32))
+    scratch_rows = max([plan[3] * piece_rows for plan in uneven], default=8)
     return pl.pallas_call(
         kernel,
         grid_spec=pltpu.PrefetchScalarGridSpec(
             num_scalar_prefetch=1,
-            grid=(count // blocks_a_step,),
-            in_specs=[
-                pl.BlockSpec(
-                    (1, piece_rows, LANES),
-                    lambda g, positions, j=j: (positions[g * blocks_a_step + j], 0, 0),
+            grid=(steps,),
+            in_specs=in_specs,
+            out_specs=out_specs,
+            scratch_shapes=[
+                pltpu.VMEM((2, blocks_a_step, piece_rows, LANES), jnp.bfloat16),
+                pltpu.SemaphoreType.DMA((2,)),
+                pltpu.VMEM((scratch_rows, LANES), jnp.float32),
+            ],
+        ),
+        out_shape=out_shape,
+        cost_estimate=pl.CostEstimate(
+            flops=2 * steps * step_rows * width * (rows_in.shape[0] if multiply else 0),
+            bytes_accessed=4 * steps * step_rows * width,
+            transcendentals=0,
+        ),
+        compiler_params=params(),
+    )(order, *operands)
+
+
+def spread_products(my_part, parts, pairs):
+    row_count = pairs[0][0].shape[0]
+    total = pairs[0][1].shape[0 if pairs[0][2] else 1]
+    width = total // parts
+
+    def kernel(part_ref, *refs):
+        ins, outs = refs[: 2 * len(pairs)], refs[2 * len(pairs) :]
+        for m in range(parts):
+            first = pl.multiple_of((part_ref[0] ^ m) * width, width)
+            result = None
+            for i, (left, right, transposed) in enumerate(pairs):
+                if transposed:
+                    block, axis = ins[2 * i + 1][pl.ds(first, width), :], 1
+                else:
+                    block, axis = ins[2 * i + 1][:, pl.ds(first, width)], 0
+                part = lax.dot_general(
+                    ins[2 * i][...],
+                    block,
+                    (((1,), (axis,)), ((), ())),
+                    preferred_element_type=jnp.float32,
                 )
-                for j in range(blocks_a_step)
-            ],
-            out_specs=pl.BlockSpec((rows * blocks_a_step, col_count), lambda g, positions: (g, 0)),
-        ),
-        out_shape=jax.ShapeDtypeStruct((count * rows, col_count), jnp.bfloat16),
-        compiler_params=params(),
-    )(positions, *([gathered] * blocks_a_step))
-
-
-def spread_matrix(gathered, positions, col_count):
-    tiles = col_count // LANES
-    rows = gathered.shape[1]
-    count = positions.shape[0]
-    groups = count // tiles
-
-    def kernel(positions_ref, *refs):
-        ins, out_ref, scratch = refs[:tiles], refs[tiles], refs[tiles + 1]
-        for j in range(tiles):
-            scratch[rows * j : rows * j + rows, :] = ins[j][0].astype(jnp.float32)
-        for c in range(tiles):
-            out_ref[:, LANES * c : LANES * c + LANES] = scratch[
-                pl.ds(c, rows, stride=tiles), :
-            ].astype(jnp.bfloat16)
-
+                result = part if result is None else result + part
+            outs[m][...] = result.astype(jnp.bfloat16)
+
+    vmem = pl.BlockSpec(memory_space=pltpu.VMEM)
+    flat = [array for left, right, transposed in pairs for array in (left, right)]
     return pl.pallas_call(
         kernel,
-        grid_spec=pltpu.PrefetchScalarGridSpec(
-            num_scalar_prefetch=1,
-            grid=(groups,),
-            in_specs=[
-                pl.BlockSpec(
-                    (1, rows, LANES), lambda g, positions, j=j: (positions[g * tiles + j], 0, 0)
-                )
-                for j in range(tiles)
-            ],
-            out_specs=pl.BlockSpec((rows, col_count), lambda g, positions: (g, 0)),
-            scratch_shapes=[pltpu.VMEM((rows * tiles, LANES), jnp.float32)],
+        in_specs=[pl.BlockSpec(memory_space=pltpu.SMEM)] + [vmem] * len(flat),
+        out_specs=[vmem] * parts,
+        out_shape=[jax.ShapeDtypeStruct((row_count, width), jnp.bfloat16)] * parts,
+        cost_estimate=pl.CostEstimate(
+            flops=2 * row_count * sum(pair[1].size for pair in pairs),
+            bytes_accessed=2 * sum(pair[1].size for pair in pairs),
+            transcendentals=0,
         ),
-        out_shape=jax.ShapeDtypeStruct((groups * rows, col_count), jnp.bfloat16),
         compiler_params=params(),
-    )(positions, *([gathered] * tiles))
-
-
-def weight_grad_blocks(left_t, right, positions, slots_total, table, blocks_a_step):
+    )(my_part, *flat)
+
+
+def exchange(blocks, axis):
+    devices = lax.axis_size(axis)
+    return [blocks[0]] + [
+        lax.ppermute(blocks[m], axis, [(i, i ^ m) for i in range(devices)])
+        for m in range(1, devices)
+    ]
+
+
+def total_of(blocks):
+    total = blocks[0].astype(jnp.float32)
+    for block in blocks[1:]:
+        total = total + block.astype(jnp.float32)
+    return total
+
+
+def sum_over(block, axis):
+    return total_of(exchange([block] * lax.axis_size(axis), axis))
+
+
+def in_order(blocks, my_part, axis):
+    stacked = jnp.stack(blocks)
+    return jnp.concatenate(
+        [
+            lax.dynamic_index_in_dim(stacked, my_part ^ j, 0, keepdims=False)
+            for j in range(len(blocks))
+        ],
+        axis=axis,
+    )
+
+
+def gather_states(block):
+    devices = lax.axis_size("seq")
+    if devices != 8:
+        return lax.all_gather(block, "seq", axis=0, tiled=False), jnp.zeros((1,), jnp.int32)
+
+    def moved(array, mask):
+        return lax.ppermute(array, "seq", [(i, i ^ mask) for i in range(devices)])
+
+    chips = [block] + [moved(block, mask) for mask in (2, 4, 6)]
+    pairs = [(chip, moved(chip, 1)) for chip in chips]
+    rows = jnp.stack([array for pair in pairs for array in pair])
+    return rows, lax.axis_index("seq").astype(jnp.int32).reshape(1)
+
+
+def weight_grad_blocks(left_t, right, right_block, col_count, positions, tables, blocks_a_step):
     row_total, depth = left_t.shape
-    col_count = right.shape[1]
     tiles = col_count // LANES
     piece_rows = 512
     even = tiles in (2, 4, 8, 16)
@@ -697,16 +855,13 @@
     steps = row_total // step_rows
 
     def kernel(positions_ref, left_ref, right_ref, *refs):
-        if table is not None:
-            refs = refs[1:]
-        out_ref, product, staged, sem = refs
+        table_refs = refs[len(tables) : 2 * len(tables)]
+        product, staged, sem = refs[2 * len(tables) :]
         g = pl.program_id(0)
         slot = lax.rem(g, 2)
 
         def settle(which):
-            pltpu.make_async_copy(
-                staged.at[which], out_ref.at[pl.ds(0, blocks_a_step)], sem.at[which]
-            ).wait()
+            pltpu.make_async_copy(staged.at[which], staged.at[which], sem.at[which]).wait()
 
         @pl.when(g >= 2)
         def _():
@@ -738,11 +893,17 @@
                     piece_rows * block : piece_rows * block + piece_rows, :
                 ].astype(jnp.bfloat16)
         for block in range(blocks_a_step):
-            pltpu.make_async_copy(
-                staged.at[slot, block],
-                out_ref.at[positions_ref[g * blocks_a_step + block]],
-                sem.at[slot],
-            ).start()
+            position = positions_ref[g * blocks_a_step + block]
+
+            for number, table_ref in enumerate(table_refs):
+
+                @pl.when(position // TABLE == number)
+                def _():
+                    pltpu.make_async_copy(
+                        staged.at[slot, block],
+                        table_ref.at[lax.rem(position, TABLE)],
+                        sem.at[slot],
+                    ).start()
 
         @pl.when(g == steps - 1)
         def _():
@@ -750,17 +911,11 @@
             if steps > 1:
                 settle(1 - slot)
 
-    out_shape = jax.ShapeDtypeStruct((slots_total, piece_rows, LANES), jnp.bfloat16)
-    operands = [positions, left_t, right]
+    anywhere = pl.BlockSpec(memory_space=pl.ANY)
     in_specs = [
         pl.BlockSpec((step_rows, depth), lambda g, positions: (g, 0)),
-        pl.BlockSpec((depth, col_count), lambda g, positions: (0, 0)),
-    ]
-    aliases = {}
-    if table is not None:
-        operands.append(table)
-        in_specs.append(pl.BlockSpec(memory_space=pl.ANY))
-        aliases = {3: 0}
+        pl.BlockSpec((depth, col_count), lambda g, positions: (0, right_block)),
+    ] + [anywhere for table in tables]
     product_shape = (step_rows, col_count) if even else (step_rows * tiles, LANES)
     return pl.pallas_call(
         kernel,
@@ -768,37 +923,69 @@
             num_scalar_prefetch=1,
             grid=(steps,),
             in_specs=in_specs,
-            out_specs=pl.BlockSpec(memory_space=pl.ANY),
+            out_specs=[anywhere for table in tables],
             scratch_shapes=[
                 pltpu.VMEM(product_shape, jnp.float32),
                 pltpu.VMEM((2, blocks_a_step, piece_rows, LANES), jnp.bfloat16),
                 pltpu.SemaphoreType.DMA((2,)),
             ],
         ),
-        out_shape=out_shape,
-        input_output_aliases=aliases,
+        out_shape=[jax.ShapeDtypeStruct(table.shape, table.dtype) for table in tables],
+        input_output_aliases={3 + i: i for i in range(len(tables))},
         cost_estimate=pl.CostEstimate(
             flops=2 * row_total * depth * col_count,
             bytes_accessed=2 * row_total * col_count,
             transcendentals=0,
         ),
         compiler_params=params(),
-    )(*operands)
+    )(positions, left_t, right, *tables)
 
 
 def optimizer_update(
-    reduced, slot_kinds, kinds_used, slot_masks, small_rates, master, moment_one, moment_two
+    sources, slot_sources, slot_rows, slot_kinds, kinds_used, slot_masks, small_rates, master, moment_one, moment_two
 ):
     capacity, piece_size = master.shape
     chunks = piece_size // CHUNK
     rows = CHUNK // LANES
     slot_blocks = pl.cdiv(capacity, 8)
 
-    def kernel(
-        kinds_ref, reduced_ref, masks_ref, small_ref, master_ref, one_ref, two_ref,
-        grad_out, master_out, one_out, two_out, low_out, scratch,
-    ):
+    steps = slot_blocks * chunks
+
+    def kernel(kinds_ref, sources_ref, rows_ref, *refs):
+        source_refs, refs = refs[: len(sources)], refs[len(sources) :]
+        (
+            masks_ref, small_ref, master_ref, one_ref, two_ref,
+            grad_out, master_out, one_out, two_out, low_out, scratch, buffer, sem,
+        ) = refs
         first = pl.program_id(0) * 8
+        step = pl.program_id(0) * chunks + pl.program_id(1)
+        slot = lax.rem(step, 2)
+
+        def start(step, which):
+            block, chunk = step // chunks, lax.rem(step, chunks)
+            for s in range(8):
+                for i, source_ref in enumerate(source_refs):
+
+                    @pl.when(sources_ref[block * 8 + s] == i)
+                    def _():
+                        pltpu.make_async_copy(
+                            source_ref.at[
+                                rows_ref[block * 8 + s],
+                                pl.ds(pl.multiple_of(chunk * rows, rows), rows),
+                            ],
+                            buffer.at[which, s],
+                            sem.at[which],
+                        ).start()
+
+        @pl.when(step == 0)
+        def _():
+            start(0, 0)
+
+        @pl.when(step + 1 < steps)
+        def _():
+            start(step + 1, 1 - slot)
+
+        pltpu.make_async_copy(buffer.at[slot], buffer.at[slot], sem.at[slot]).wait()
         for s in range(8):
             kind_now = kinds_ref[first + s]
             for kind in kinds_used:
@@ -808,8 +995,8 @@
                     for tile in range(rows // TILE):
                         row_tile, column = divmod(tile, kind)
                         start = (row_tile * TILE * kind + column) * 8 + s
-                        scratch[pl.ds(start, TILE, stride=8 * kind), :] = reduced_ref[
-                            s, TILE * tile : TILE * tile + TILE, :
+                        scratch[pl.ds(start, TILE, stride=8 * kind), :] = buffer[
+                            slot, s, TILE * tile : TILE * tile + TILE, :
                         ].astype(jnp.float32)
         present = masks_ref[0] > 0.5
         is_small = masks_ref[1] > 0.5
@@ -832,27 +1019,34 @@
             two_out[:, lanes] = two_new
             low_out[:, lanes] = master_new.astype(jnp.bfloat16)
 
-    state_spec = pl.BlockSpec((8, CHUNK), lambda i, j, kinds: (i, j))
+    state_spec = pl.BlockSpec((8, CHUNK), lambda i, j, *tables: (i, j))
     wide = jax.ShapeDtypeStruct((capacity, piece_size), jnp.float32)
     return pl.pallas_call(
         kernel,
         grid_spec=pltpu.PrefetchScalarGridSpec(
-            num_scalar_prefetch=1,
+            num_scalar_prefetch=3,
             grid=(slot_blocks, chunks),
-            in_specs=[
-                pl.BlockSpec((8, rows, LANES), lambda i, j, kinds: (i, j, 0)),
-                pl.BlockSpec((3, 8, LANES), lambda i, j, kinds: (0, i, 0)),
-                pl.BlockSpec((1, CHUNK), lambda i, j, kinds: (0, j)),
+            in_specs=[pl.BlockSpec(memory_space=pl.ANY) for source in sources]
+            + [
+                pl.BlockSpec((3, 8, LANES), lambda i, j, *tables: (0, i, 0)),
+                pl.BlockSpec((1, CHUNK), lambda i, j, *tables: (0, j)),
                 state_spec,
                 state_spec,
                 state_spec,
             ],
             out_specs=[state_spec] * 5,
-            scratch_shapes=[pltpu.VMEM((8 * rows, LANES), jnp.float32)],
+            scratch_shapes=[
+                pltpu.VMEM((8 * rows, LANES), jnp.float32),
+                pltpu.VMEM((2, 8, rows, LANES), jnp.bfloat16),
+                pltpu.SemaphoreType.DMA((2,)),
+            ],
         ),
         out_shape=[wide] * 4 + [jax.ShapeDtypeStruct((capacity, piece_size), jnp.bfloat16)],
         compiler_params=params(),
-    )(slot_kinds, reduced, slot_masks, small_rates, master, moment_one, moment_two)
+    )(
+        slot_kinds, slot_sources, slot_rows, *sources,
+        slot_masks, small_rates, master, moment_one, moment_two,
+    )
 
 
 def weight_grad(left, right):
@@ -861,6 +1055,32 @@
 
 def back_product(grad_rows, weight):
     return jnp.dot(grad_rows, weight.T, preferred_element_type=jnp.float32)
+
+
+def gather_rest(packed, first, trips, most, extra_step):
+    devices = lax.axis_size("seq")
+    rows = devices * extra_step
+    room = reserve((most * rows,) + packed.shape[1:], packed.dtype)
+
+    def more(trip, table):
+        part = lax.dynamic_slice_in_dim(packed, first + trip * extra_step, extra_step)
+        part = lax.all_gather(part, "seq", axis=0, tiled=True)
+        return lax.dynamic_update_slice_in_dim(table, part, trip * rows, axis=0)
+
+    return lax.fori_loop(0, trips, more, room)
+
+
+def reduce_rest(rest, trips, most, extra_step):
+    devices = lax.axis_size("seq")
+    rows = devices * extra_step
+    room = reserve((most * extra_step,) + rest.shape[1:], rest.dtype)
+
+    def more(trip, table):
+        part = lax.dynamic_slice_in_dim(rest, trip * rows, rows)
+        part = lax.psum_scatter(part, "seq", scatter_dimension=0, tiled=True)
+        return lax.dynamic_update_slice_in_dim(table, part, trip * extra_step, axis=0)
+
+    return lax.fori_loop(0, trips, more, room)
 
 
 def on_device(inputs, cotangent, owners, master, moment_one, moment_two):
@@ -869,104 +1089,192 @@
     local_heads = HEADS // head_parts
     capacity, piece_size = master.shape
     piece_count = owners.shape[0]
+    row_count = inputs.shape[0]
+    rim_width = KCONV - 1
     segments_list = shard_layout(local_heads, head_parts)
-    slot_of_piece, piece_of_slot, present = piece_table(owners, seq_parts, capacity)
-    my_index = lax.axis_index("seq")
-    my_pieces = lax.dynamic_slice_in_dim(piece_of_slot, my_index * capacity, capacity)
-    my_present = lax.dynamic_slice_in_dim(present, my_index * capacity, capacity)
-    kind_table = piece_kinds(segments_list, piece_count, piece_size)
-    kinds_used = sorted(set(kind_table.tolist()) | {1})
-    slot_kinds = jnp.where(my_present, jnp.asarray(kind_table)[my_pieces], 1)
-    slot_kinds = jnp.pad(slot_kinds, (0, -capacity % 8), constant_values=1)
-    gathered = lax.all_gather(
-        pack_blocks(master, slot_kinds, kinds_used), "seq", axis=0, tiled=True
-    )
+    columns = {name: c for name, r, c, rate in segments_list}
     counts = {name: r * c // piece_size for name, r, c, rate in segments_list[:8]}
     firsts = dict(zip(counts, np.cumsum([0] + list(counts.values())).tolist()))
-    columns = {name: c for name, r, c, rate in segments_list}
-
-    def positions_of(*names):
-        return jnp.concatenate(
-            [slot_of_piece[firsts[name] : firsts[name] + counts[name]] for name in names]
-        )
-
-    by_name = {}
-    for name, blocks_a_step in (("wq", 4), ("wk", 4), ("wv", 8), ("wg", 8), ("wo", 8), ("wdown", 11)):
-        by_name[name] = tiled_matrix(gathered, positions_of(name), columns[name], blocks_a_step)
-    for name in ("wgate", "wup"):
-        by_name[name] = spread_matrix(gathered, positions_of(name), columns[name])
+    mixer_count = firsts["wgate"]
+    big_count = piece_count - 1
+    my_head = lax.axis_index("head").astype(jnp.int32)
+    my_index = lax.axis_index("seq").astype(jnp.int32)
+    my_head_row, my_index_row = my_head.reshape(1), my_index.reshape(1)
+
+    onehot = (owners[:, None] == jnp.arange(seq_parts, dtype=jnp.int32)[None, :]).astype(jnp.int32)
+    ranks = jnp.sum((jnp.cumsum(onehot, axis=0) - onehot) * onehot, axis=1)
+    mixer_held = jnp.sum(onehot[:mixer_count], axis=0)
+    mlp_held = jnp.sum(onehot[mixer_count:big_count], axis=0)
+    padded = capacity + -capacity % 8
+    small_rank = ranks[big_count]
+    big_owners, big_ranks = owners[:big_count], ranks[:big_count]
+    is_mixer = np.arange(big_count) < mixer_count
+    held_there = jnp.sum(onehot[:big_count] * mixer_held[None, :], axis=1)
+
+    def rest_row(over, owner):
+        return over // extra_step * (seq_parts * extra_step) + owner * extra_step + over % extra_step
+
+    early = -(-capacity * FIRST_GATHER // (8 * CAPACITY_UNIT)) * 8
+    late = capacity - early
+    extra_step = min(4, late)
+    most_gather = -(-late // extra_step)
+    trips_gather = jnp.maximum(-(-(jnp.max(mixer_held) - early) // extra_step), 0)
+    early_row = big_owners * early + big_ranks
+    mixer_fetch = jnp.where(
+        big_ranks < early, early_row, TABLE + rest_row(big_ranks - early, big_owners)
+    )
+    mlp_fetch = jnp.where(
+        big_ranks < early, TABLE + early_row, big_owners * late + big_ranks - early
+    )
+    first_room = -(-capacity * FIRST_REDUCE // CAPACITY_UNIT)
+    second_room = -(-capacity * SECOND_REDUCE // CAPACITY_UNIT)
+    most_reduce = -(-(capacity - second_room) // extra_step)
+    second_held = mixer_held + jnp.maximum(mlp_held - first_room, 0)
+    trips_reduce = jnp.maximum(-(-(jnp.max(second_held) - second_room) // extra_step), 0)
+    mlp_ranks = big_ranks - held_there
+    second_index = jnp.where(is_mixer, big_ranks, big_ranks - first_room)
+    store = jnp.where(
+        ~is_mixer & (mlp_ranks < first_room),
+        big_owners * first_room + mlp_ranks,
+        jnp.where(
+            second_index < second_room,
+            TABLE + big_owners * second_room + second_index,
+            2 * TABLE + rest_row(second_index - second_room, big_owners),
+        ),
+    )
+    small_owner = owners[big_count]
+
+    def spots(table, name):
+        return table[firsts[name] : firsts[name] + counts[name]]
+
+    my_mixer = mixer_held[my_index]
+    my_mlp = mlp_held[my_index]
+    my_count = my_mixer + my_mlp
+    slot_ids = jnp.arange(padded, dtype=jnp.int32)
+    mine = owners == my_index
+    matches = (mine[None, :] & (ranks[None, :] == slot_ids[:, None])).astype(jnp.int32)
+    kind_table = piece_kinds(segments_list, piece_count, piece_size)
+    piece_rates, small_rates = rate_parts(segments_list, piece_count, piece_size)
+    present = jnp.sum(matches, axis=1)
+    slot_kinds = 1 + jnp.sum(matches * jnp.asarray(kind_table - 1)[None, :], axis=1)
+    slot_rates = PAD_RATE + jnp.sum(
+        matches.astype(jnp.float32) * jnp.asarray(piece_rates - np.float32(PAD_RATE))[None, :], axis=1
+    )
+    is_small = matches[:, big_count]
+    kinds_used = sorted(set(kind_table.tolist()) | {1})
+
+    small_rows = -(-sum(r * c for name, r, c, rate in segments_list[8:]) // (TILE * LANES)) * TILE
+    gain_width = D // head_parts
+    norm_width = DV // head_parts
+    gain_first = sum(r * c for name, r, c, rate in segments_list[8:14])
+    my_small = lax.dynamic_slice(master, (small_rank, 0), (1, small_rows * LANES))
+    my_small = my_small.astype(jnp.bfloat16)
+    gains = my_small[:, gain_first : gain_first + 2 * gain_width + norm_width]
+    gains = in_order(exchange([gains] * head_parts, "head"), my_head, 0)
+    gains = jnp.concatenate(
+        [
+            gains[:, :gain_width].reshape(1, D),
+            gains[:, gain_width : 2 * gain_width].reshape(1, D),
+            gains[:, 2 * gain_width :].reshape(1, DV),
+        ],
+        axis=1,
+    )
+    rows_of_piece = piece_size // LANES
+    small_width = small_rows * LANES
+    small_part = jnp.concatenate([my_small, gains], axis=1).reshape(-1, LANES)
+    small_table = lax.all_gather(small_part, "seq", axis=0, tiled=False)
+    input_blocks = exchange([inputs] * head_parts, "head")
+    early_part = pack_blocks(master, slot_kinds, kinds_used, 0, early)
+    early_table = lax.all_gather(early_part, "seq", axis=0, tiled=True)
+    late_part = pack_blocks(master, slot_kinds, kinds_used, early, late)
+    back_blocks = exchange([cotangent] * head_parts, "head")
+    rows_full = in_order(input_blocks, my_head, 1)
+    back_full = in_order(back_blocks, my_head, 1)
     small_flat = lax.dynamic_index_in_dim(
-        gathered, slot_of_piece[piece_count - 1], axis=0, keepdims=False
+        small_table, small_owner, axis=0, keepdims=False
     ).reshape(-1)
-    small_names, small_used = unpack(small_flat, segments_list[8:])
-    by_name.update(small_names)
-    row_count = inputs.shape[0]
-    rim_width = KCONV - 1
-    rows_full, back_full, first_norm_scale_factor, second_norm_scale_factor, norm_gain = (
-        lax.all_gather(inputs, "head", axis=1, tiled=True),
-        lax.all_gather(cotangent, "head", axis=1, tiled=True),
-        lax.all_gather(by_name["gainone"].reshape(-1), "head", axis=0, tiled=True),
-        lax.all_gather(by_name["gaintwo"].reshape(-1), "head", axis=0, tiled=True),
-        lax.all_gather(by_name["wnorm"].reshape(-1), "head", axis=0, tiled=True),
-    )
-    first_norm_scale_factor = first_norm_scale_factor.astype(jnp.float32)
-    second_norm_scale_factor = second_norm_scale_factor.astype(jnp.float32)
+    by_name, small_used = unpack(small_flat, segments_list[8:])
+    gains = small_flat[small_width:].astype(jnp.float32)[None, :]
+    gain_one, gain_two, norm_row = gains[:, :D], gains[:, D : 2 * D], gains[:, 2 * D :]
+    gain_one_mine = by_name["gainone"].astype(jnp.float32)
+    gain_two_mine = by_name["gaintwo"].astype(jnp.float32)
+
     rows_wide = rows_full.astype(jnp.float32)
     scale_one = lax.rsqrt(jnp.mean(rows_wide * rows_wide, axis=-1, keepdims=True) + NORM_EPSILON)
-    normed = (rows_wide * scale_one * first_norm_scale_factor).astype(jnp.bfloat16)
-    mixer_names = ("wq", "wk", "wv", "wg")
-    projected = jnp.concatenate(
-        [
-            jnp.dot(normed, by_name[name], preferred_element_type=jnp.float32)
-            for name in mixer_names
-        ],
-        axis=1,
-    )
-    conv_columns = local_heads * (2 * DK + DV)
+    normed = (rows_wide * scale_one * gain_one).astype(jnp.bfloat16)
+
     decay_weight = jnp.pad(by_name["wab"], ((0, 0), (0, LANES - 2 * local_heads)))
     decay_proj = jnp.dot(normed, decay_weight, preferred_element_type=jnp.float32)
-    rim = shifted(projected[row_count - rim_width :, :conv_columns], "seq", 1)
-    rim = jnp.pad(rim, ((8 - rim_width, 0), (0, 0)))
     taps = jnp.concatenate([by_name["cq"], by_name["ck"], by_name["cv"]], axis=1)
     taps = jnp.pad(taps.astype(jnp.float32), ((0, 8 - KCONV), (0, 0)))
     scalars = jnp.pad(
         jnp.concatenate([by_name["alog"], by_name["dtbias"]], axis=0).astype(jnp.float32),
         ((0, 6), (0, LANES - local_heads)),
     )
+
+    beside = (
+        trips_gather, late_part, normed, scale_one, decay_proj, decay_weight, taps, scalars,
+        back_full, mixer_fetch, mlp_fetch, store, gain_two, norm_row,
+    )
+    early_table, beside = lax.optimization_barrier((early_table, beside))
+    (
+        trips_now, late_part, normed, scale_one, decay_proj, decay_weight, taps, scalars,
+        back_full, mixer_fetch, mlp_fetch, store, gain_two, norm_row,
+    ) = beside
+    mixer_rest = gather_rest(late_part, 0, trips_now, most_gather, extra_step)
+    late_table = lax.all_gather(late_part, "seq", axis=0, tiled=True)
+
+    mixer_names = ("wq", "wk", "wv", "wg")
+    mixer_weights, projected = assemble(
+        [early_table, mixer_rest],
+        [(spots(mixer_fetch, name), columns[name]) for name in mixer_names],
+        512,
+        normed,
+    )
+    conv_columns = local_heads * (2 * DK + DV)
+    rim = shifted(projected[row_count - rim_width :, :conv_columns], "seq", 1)
+    rim = jnp.pad(rim, ((8 - rim_width, 0), (0, 0)))
     solve, fresh, wy_keys, reach, zero_out, handoff = mixer_local(
         local_heads, projected, rim, taps, decay_proj, scalars
     )
-    handoffs = lax.all_gather(handoff, "seq", axis=0, tiled=False)
-    my_index_row = my_index.astype(jnp.int32).reshape(1)
-    norm_row = norm_gain.astype(jnp.float32)[None, :]
+    handoffs, base = gather_states(handoff)
+    (out_weights,) = assemble(
+        [early_table, mixer_rest], [(spots(mixer_fetch, "wo"), columns["wo"])], 256
+    )
     entering_state, recurred, gated_low = mixer_out(
-        local_heads, my_index_row, handoffs, reach, zero_out, projected, norm_row
-    )
-    mixed = lax.psum_scatter(
-        jnp.dot(gated_low, by_name["wo"], preferred_element_type=jnp.float32).astype(jnp.bfloat16),
-        "head",
-        scatter_dimension=1,
-        tiled=True,
-    ).astype(jnp.float32)
+        local_heads, my_index_row, base, handoffs, reach, zero_out, projected, norm_row
+    )
+    mixed_parts = exchange(
+        spread_products(my_head_row, head_parts, [(gated_low, out_weights, False)]), "head"
+    )
+    (down_weights,) = assemble(
+        [late_table, early_table], [(spots(mlp_fetch, "wdown"), columns["wdown"])], 352
+    )
+    (mlp_weights,) = assemble(
+        [late_table, early_table],
+        [(spots(mlp_fetch, name), columns[name]) for name in ("wgate", "wup")],
+        512,
+    )
+    mixed_parts, down_weights, mlp_weights = lax.optimization_barrier(
+        (mixed_parts, down_weights, mlp_weights)
+    )
+    mixed = total_of(mixed_parts)
     inputs_wide = inputs.astype(jnp.float32)
     residual = inputs_wide + mixed
     resid_low = residual.astype(jnp.bfloat16)
-    resid_full = lax.all_gather(resid_low, "head", axis=1, tiled=True).astype(jnp.float32)
+
+    resid_blocks = exchange([resid_low] * head_parts, "head")
+    resid_full = in_order(resid_blocks, my_head, 1).astype(jnp.float32)
     scale_two = lax.rsqrt(jnp.mean(resid_full * resid_full, axis=-1, keepdims=True) + NORM_EPSILON)
-    hidden_in = (resid_full * scale_two * second_norm_scale_factor).astype(jnp.bfloat16)
-    gate_mlp = jnp.dot(hidden_in, by_name["wgate"], preferred_element_type=jnp.float32)
-    up_mlp = jnp.dot(hidden_in, by_name["wup"], preferred_element_type=jnp.float32)
+    hidden_in = (resid_full * scale_two * gain_two).astype(jnp.bfloat16)
+    gate_up = jnp.dot(hidden_in, mlp_weights, preferred_element_type=jnp.float32)
+    hidden_width = columns["wgate"]
+    gate_mlp, up_mlp = gate_up[:, :hidden_width], gate_up[:, hidden_width:]
     logistic_output_multiplier = jax.nn.sigmoid(gate_mlp)
     silu_gate = gate_mlp * logistic_output_multiplier
     hidden = (silu_gate * up_mlp).astype(jnp.bfloat16)
-    mlp_out = lax.psum_scatter(
-        jnp.dot(hidden, by_name["wdown"], preferred_element_type=jnp.float32).astype(jnp.bfloat16),
-        "head",
-        scatter_dimension=1,
-        tiled=True,
-    ).astype(jnp.float32)
-    block_out = (residual + mlp_out).astype(jnp.bfloat16)
-    d_hidden = back_product(back_full, by_name["wdown"])
+    mlp_blocks = spread_products(my_head_row, head_parts, [(hidden, down_weights, False)])
+    d_hidden = back_product(back_full, down_weights)
     d_gate_mlp = (
         d_hidden
         * up_mlp
@@ -974,48 +1282,62 @@
         * (1.0 + gate_mlp * (1.0 - logistic_output_multiplier))
     ).astype(jnp.bfloat16)
     d_up_mlp = (d_hidden * silu_gate).astype(jnp.bfloat16)
-    slots_total = seq_parts * capacity
-
-    def store_grad(table, name, left, right, blocks_a_step):
+    d_gate_up = jnp.concatenate([d_gate_mlp, d_up_mlp], axis=1)
+    def store_grad(tables, name, left_t, right, right_block, blocks_a_step):
         return weight_grad_blocks(
-            left.T, right, positions_of(name), slots_total, table, blocks_a_step
+            left_t, right, right_block, columns[name], spots(store, name), tables, blocks_a_step
         )
 
-    grad_table = store_grad(None, "wdown", hidden, back_full, 11)
-    grad_table = store_grad(grad_table, "wgate", hidden_in, d_gate_mlp, 11)
-    grad_table = store_grad(grad_table, "wup", hidden_in, d_up_mlp, 11)
-    d_hidden_in = back_product(d_gate_mlp, by_name["wgate"]) + back_product(
-        d_up_mlp, by_name["wup"]
-    )
-    dot_two = jnp.sum(d_hidden_in * second_norm_scale_factor * resid_full, axis=-1, keepdims=True)
-    d_hidden_mine, dot_two_sum = (
-        lax.psum_scatter(
-            d_hidden_in.astype(jnp.bfloat16), "head", scatter_dimension=1, tiled=True
-        ).astype(jnp.float32),
-        lax.psum_scatter(
-            jnp.broadcast_to(dot_two, (row_count, head_parts)).astype(jnp.bfloat16),
-            "head",
-            scatter_dimension=1,
-            tiled=True,
-        ).astype(jnp.float32),
-    )
+    grad_tables = [
+        reserve((rows, rows_of_piece, LANES), jnp.bfloat16)
+        for rows in (
+            seq_parts * first_room,
+            seq_parts * second_room,
+            most_reduce * seq_parts * extra_step,
+        )
+    ]
+    grad_tables = store_grad(grad_tables, "wdown", hidden.T, back_full, 0, 11)
+    hidden_in_t = hidden_in.T
+    grad_tables = store_grad(grad_tables, "wgate", hidden_in_t, d_gate_up, 0, 11)
+    grad_tables = store_grad(grad_tables, "wup", hidden_in_t, d_gate_up, 1, 11)
+    grad_tables, d_gate_up = lax.optimization_barrier((grad_tables, d_gate_up))
+    d_hidden_parts = exchange(
+        spread_products(my_head_row, head_parts, [(d_gate_up, mlp_weights, True)]), "head"
+    )
+    first_reduced = lax.psum_scatter(grad_tables[0], "seq", scatter_dimension=0, tiled=True)
+    grad_tables = grad_tables[1:]
+    store = store - TABLE
+    d_hidden_mine = total_of(d_hidden_parts)
+    mlp_out = total_of(exchange(mlp_blocks, "head"))
+    block_out = (residual + mlp_out).astype(jnp.bfloat16)
+
     resid_mine = resid_low.astype(jnp.float32)
-    gain_two_mine = by_name["gaintwo"].reshape(-1).astype(jnp.float32)
-    grad_gaintwo = jnp.sum(d_hidden_mine * resid_mine * scale_two, axis=0, keepdims=True)
+    d_hidden_low = d_hidden_mine.astype(jnp.bfloat16)
+    dot_mine = jnp.sum(d_hidden_mine * gain_two_mine * resid_mine, axis=-1)
+    d_hidden_blocks = exchange([d_hidden_low] * head_parts, "head")
+    dot_two = sum_over(dot_mine.reshape(-1, LANES), "head").reshape(row_count, 1)
+    grad_gaintwo = jnp.sum(d_hidden_mine * resid_mine * scale_two, axis=0)
     d_resid = (
         cotangent.astype(jnp.float32)
         + scale_two * d_hidden_mine * gain_two_mine
-        - scale_two**3 / D * resid_mine * dot_two_sum
-    )
-    back_mix_full = lax.all_gather(d_resid.astype(jnp.bfloat16), "head", axis=1, tiled=True)
-    grad_table = store_grad(grad_table, "wo", gated_low, back_mix_full, 8)
-    d_gated = back_product(back_mix_full, by_name["wo"])
+        - scale_two**3 / D * resid_mine * dot_two
+    )
+    d_hidden_full = in_order(d_hidden_blocks, my_head, 1).astype(jnp.float32)
+    back_mix_full = (
+        back_full.astype(jnp.float32)
+        + scale_two * d_hidden_full * gain_two
+        - scale_two**3 / D * resid_full * dot_two
+    ).astype(jnp.bfloat16)
+
+    d_gated = back_product(back_mix_full, out_weights)
     d_recurred, d_gate, norm_grad, d_entering = mixer_gate_back(
         local_heads, d_gated, recurred, projected, norm_row, reach
     )
-    d_norm_gain = norm_grad[0]
-    d_enterings = lax.all_gather(d_entering, "seq", axis=0, tiled=False)
-    d_leaving = relay_back(local_heads, my_index_row, handoffs, d_enterings)
+    d_enterings, base = gather_states(d_entering)
+    normed_t = normed.T
+    grad_tables = store_grad(grad_tables, "wo", gated_low.T, back_mix_full, 0, 8)
+    grad_tables = store_grad(grad_tables, "wg", normed_t, d_gate, 0, 8)
+    d_leaving = relay_back(local_heads, my_index_row, base, handoffs, d_enterings)
     d_conv, d_tail, d_rim, d_taps, d_decay_wide, d_scalars = mixer_back(
         local_heads,
         projected,
@@ -1033,80 +1355,85 @@
     d_rim = shifted(d_rim[8 - rim_width :], "seq", -1)
     d_tail = d_tail + jnp.pad(d_rim, ((8 - rim_width, 0), (0, 0)))
     d_conv = lax.dynamic_update_slice(d_conv, d_tail.astype(jnp.bfloat16), (row_count - 8, 0))
-    d_query = d_conv[:, : local_heads * DK]
-    d_key = d_conv[:, local_heads * DK : 2 * local_heads * DK]
-    d_value = d_conv[:, 2 * local_heads * DK :]
-    d_decay = d_decay_wide[:, : 2 * local_heads].astype(jnp.bfloat16)
-    d_conv_query = d_taps[:KCONV, : local_heads * DK]
-    d_conv_key = d_taps[:KCONV, local_heads * DK : 2 * local_heads * DK]
-    d_conv_value = d_taps[:KCONV, 2 * local_heads * DK :]
-    d_log_rate = d_scalars[0, :local_heads]
-    d_rate_bias = d_scalars[1, :local_heads]
-    grad_table = store_grad(grad_table, "wg", normed, d_gate, 8)
-    grad_table = store_grad(grad_table, "wv", normed, d_value, 8)
-    grad_table = store_grad(grad_table, "wk", normed, d_key, 4)
-    grad_table = store_grad(grad_table, "wq", normed, d_query, 4)
-    grad_wab = weight_grad(normed, d_decay)
-    d_normed = (
-        back_product(d_query, by_name["wq"])
-        + back_product(d_key, by_name["wk"])
-        + back_product(d_value, by_name["wv"])
-        + back_product(d_gate, by_name["wg"])
-        + back_product(d_decay, by_name["wab"])
-    )
-    dot_one = jnp.sum(d_normed * first_norm_scale_factor * rows_wide, axis=-1, keepdims=True)
-    d_normed_mine, dot_one_sum, grad_wnorm = (
-        lax.psum_scatter(
-            d_normed.astype(jnp.bfloat16), "head", scatter_dimension=1, tiled=True
-        ).astype(jnp.float32),
-        lax.psum_scatter(
-            jnp.broadcast_to(dot_one, (row_count, head_parts)).astype(jnp.bfloat16),
+    key_width = local_heads * DK
+    grad_tables = store_grad(grad_tables, "wv", normed_t, d_conv, 1, 8)
+    grad_tables = store_grad(grad_tables, "wk", normed_t, d_conv, 1, 4)
+    grad_tables = store_grad(grad_tables, "wq", normed_t, d_conv, 0, 4)
+    second_table, first_reduced = lax.optimization_barrier((grad_tables[0], first_reduced))
+    second_reduced = lax.psum_scatter(second_table, "seq", scatter_dimension=0, tiled=True)
+    d_decay = d_decay_wide.astype(jnp.bfloat16)
+    grad_wab = weight_grad(normed, d_decay)[:, : 2 * local_heads]
+    d_projected = jnp.concatenate([d_conv, d_gate], axis=1)
+    d_normed_mine = total_of(
+        exchange(
+            spread_products(
+                my_head_row,
+                head_parts,
+                [(d_projected, mixer_weights, True), (d_decay, decay_weight, True)],
+            ),
             "head",
-            scatter_dimension=1,
-            tiled=True,
-        ).astype(jnp.float32),
-        lax.psum_scatter(
-            d_norm_gain.astype(jnp.bfloat16), "head", scatter_dimension=0, tiled=True
-        ).astype(jnp.float32),
-    )
-    gain_one_mine = by_name["gainone"].reshape(-1).astype(jnp.float32)
-    grad_gainone = jnp.sum(d_normed_mine * inputs_wide * scale_one, axis=0, keepdims=True)
+        )
+    )
+    dot_one = jnp.sum(d_normed_mine * gain_one_mine * inputs_wide, axis=-1)
+    sums = sum_over(
+        jnp.concatenate([dot_one.reshape(-1, LANES), norm_grad[0].reshape(-1, LANES)]), "head"
+    )
+    dot_one = sums[: row_count // LANES].reshape(row_count, 1)
+    grad_wnorm = lax.dynamic_slice_in_dim(
+        sums[row_count // LANES :].reshape(-1), my_head * norm_width, norm_width
+    )
+    grad_gainone = jnp.sum(d_normed_mine * inputs_wide * scale_one, axis=0)
     input_grad = (
         d_resid
         + scale_one * d_normed_mine * gain_one_mine
-        - scale_one**3 / D * inputs_wide * dot_one_sum
-    )
+        - scale_one**3 / D * inputs_wide * dot_one
+    )
+
     small_grads = [
-        d_conv_query,
-        d_conv_key,
-        d_conv_value,
+        d_taps[:KCONV, :key_width],
+        d_taps[:KCONV, key_width : 2 * key_width],
+        d_taps[:KCONV, 2 * key_width :],
         grad_wab,
-        d_log_rate,
-        d_rate_bias,
+        d_scalars[0, :local_heads],
+        d_scalars[1, :local_heads],
         grad_gainone,
         grad_gaintwo,
         grad_wnorm,
     ]
     small_block = jnp.concatenate(
-        [grad_now.astype(jnp.bfloat16).reshape(-1) for grad_now in small_grads]
-        + [jnp.zeros((piece_size - small_used,), jnp.bfloat16)]
-    ).reshape(1, -1, LANES)
-    grad_table = lax.dynamic_update_slice(
-        grad_table, small_block, (slot_of_piece[piece_count - 1], 0, 0)
-    )
-    reduced = lax.psum_scatter(grad_table, "seq", scatter_dimension=0, tiled=True)
-    piece_rates, small_rates = rate_parts(segments_list, piece_count, piece_size)
-    slot_masks = jnp.stack(
-        [
-            my_present.astype(jnp.float32),
-            (my_present & (my_pieces == piece_count - 1)).astype(jnp.float32),
-            jnp.where(my_present, jnp.asarray(piece_rates)[my_pieces], PAD_RATE),
-        ]
-    )
-    slot_masks = jnp.pad(slot_masks, ((0, 0), (0, -capacity % 8)))
+        [grad_now.reshape(-1) for grad_now in small_grads]
+        + [jnp.zeros((small_rows * LANES - small_used,), jnp.float32)]
+    ).reshape(-1, LANES)
+    mask = 1
+    while mask < seq_parts:
+        small_block = small_block + lax.ppermute(
+            small_block, "seq", [(i, i ^ mask) for i in range(seq_parts)]
+        )
+        mask *= 2
+    small_block = jnp.pad(
+        small_block.astype(jnp.bfloat16), ((0, rows_of_piece - small_rows), (0, 0))
+    )[None]
+
+    trips_now, second_reduced, rest_grads = lax.optimization_barrier(
+        (trips_reduce, second_reduced, grad_tables[1])
+    )
+    rest_reduced = reduce_rest(rest_grads, trips_now, most_reduce, extra_step)
+    my_first = slot_ids - my_mixer
+    in_first = (my_first >= 0) & (my_first < first_room)
+    my_second = jnp.where(my_first >= 0, slot_ids - first_room, slot_ids)
+    slot_sources = jnp.where(in_first, 0, jnp.where(my_second < second_room, 1, 2))
+    slot_rows = jnp.where(
+        in_first, my_first, jnp.where(my_second < second_room, my_second, my_second - second_room)
+    )
+    slot_sources = jnp.where(present > 0, jnp.where(is_small > 0, 3, slot_sources), 0)
+    slot_rows = jnp.where(is_small > 0, 0, slot_rows)
+    slot_rows = jnp.where(present > 0, slot_rows, 0)
+    slot_masks = jnp.stack([present.astype(jnp.float32), is_small.astype(jnp.float32), slot_rates])
     slot_masks = jnp.broadcast_to(slot_masks[:, :, None], slot_masks.shape + (LANES,))
     grad_slots, master_new, moment_new, second_new, weights_low = optimizer_update(
-        reduced,
+        [first_reduced, second_reduced, rest_reduced, small_block],
+        slot_sources,
+        slot_rows,
         slot_kinds,
         kinds_used,
         slot_masks,

time: 995 us -> 721 us (0.72)
  waiting for transfers between devices: 585 us -> 330 us
  starting transfers between devices: 4 us -> 71.6 us
  blocking collectives: 56.3 us -> 12 us
  matrix products: 56.6 us -> 12.8 us
  local copies, waits for them, and re-layouts: 53.1 us -> 21.6 us
  Pallas kernels: 193 us -> 223 us
    unnamed x13 -> x4, waiting for transfers between devices: 258 us -> 0.78 us
    all_gather x7 -> x2, waiting for transfers between devices: 278 us -> 79 us  [the longest x1 66.1 us: on_device(): early_table = lax.all_gather(early_part, 'seq', axis=0, tiled=True)]
    ppermute x0 -> x50, waiting for transfers between devices: none -> 154 us  [the longest x33 95.5 us: exchange(): lax.ppermute(blocks[m], axis, [(i, i ^ m) for i in range(devices)])]
    ppermute x0 -> x50, starting transfers between devices: none -> 67.4 us  [the longest x33 54.9 us: exchange(): lax.ppermute(blocks[m], axis, [(i, i ^ m) for i in range(devices)])]
    reduce_scatter x4 -> x2, waiting for transfers between devices: 46.9 us -> 94.1 us  [the longest x1 80.8 us: on_device(): lax.psum_scatter(second_table, 'seq', scatter_dimension=0, tiled=True)]
    unnamed x3 -> x0, blocking collectives: 32.4 us -> none
    unnamed x239 -> x186, local copies, waits for them, and re-layouts: 34.4 us -> 8.54 us
    dot_general x9 -> x2, matrix products: 30.4 us -> 5.07 us  [back_product(): return jnp.dot(grad_rows, weight.T, preferred_element_type=jnp.float32)]
  transfers between devices with their start and end apart: 14 -> 56, of which waited for: 10 -> 28; matrix products, arithmetic and copies ran while one was open for 6% -> 3% of each run, Pallas kernels for 10% -> 23%
where the time goes in v2:
time: 721 us; the launch traced here: 711 us
  waiting for transfers between devices  330 us (46%)
  Pallas kernels  223 us (31%)
  starting transfers between devices  71.6 us (10%)
  local copies, waits for them, and re-layouts  21.6 us (3%)
  between operations  21.4 us (3%)
  other arithmetic  19.2 us (3%)
  matrix products  12.8 us (2%)
  blocking collectives  12 us (2%)
    ppermute x33, waiting for transfers between devices, exchange(): lax.ppermute(blocks[m], axis, [(i, i ^ m) for i in range(devices)])  95.5 us
    reduce_scatter x1, waiting for transfers between devices, on_device(): lax.psum_scatter(second_table, 'seq', scatter_dimension=0, tiled=True)  80.8 us
    all_gather x1, waiting for transfers between devices, on_device(): early_table = lax.all_gather(early_part, 'seq', axis=0, tiled=True)  66.1 us
    ppermute x33, starting transfers between devices, exchange(): lax.ppermute(blocks[m], axis, [(i, i ^ m) for i in range(devices)])  54.9 us
    ppermute x14, waiting for transfers between devices, moved(): return lax.ppermute(array, 'seq', [(i, i ^ mask) for i in range(devices)])  46.5 us
    pallas_call x1, Pallas kernels, mixer_local(): pl.pallas_call(kernel, grid=(local_heads,), in_specs=three(row_count) + t...  40.6 us
    pallas_call x1, Pallas kernels, optimizer_update(): pl.pallas_call(kernel, grid_spec=pltpu.PrefetchScalarGridSpec(num_scalar_...  39.8 us
    pallas_call x4, Pallas kernels, assemble(): pl.pallas_call(kernel, grid_spec=pltpu.PrefetchScalarGridSpec(num_scalar_...  33.3 us
  transfers between devices with their start and end apart: 56, of which 28 were waited for; matrix products, arithmetic and copies ran while one was open for 3% of the time, Pallas kernels for 23%

profile of v2, /device:TPU:0, one launch (start us, length us, event | category | flops | bytes accessed | tf_op | source)
XLA Modules:
  0.0 711.4 jit_solution(2904664705256112982)
XLA Ops:
  12.0 8.6 %shard_map.162 = bf16[24,512,128]{2,1,0:T(8,128)(2,1)} custom-call(s32[48]{0:T(128)S(1)} %broadcast_add_fusion.1.kinds_ref, f32[44,65536]{1,0:T(8,128)} %refs_6_.1), custom_call_target="tpu_custom_call" | custom-call | tf_op jit(solution)/shard_map/pallas_call | solution.py:614
  24.4 4.0 collective-permute-start.4
  32.0 2.5 collective-permute-start.6
  36.8 8.1 %shard_map.163 = bf16[20,512,128]{2,1,0:T(8,128)(2,1)} custom-call(s32[48]{0:T(128)S(1)} %broadcast_add_fusion.1.kinds_ref, f32[44,65536]{1,0:T(8,128)} %refs_6_.1), custom_call_target="tpu_custom_call" | custom-call | tf_op jit(solution)/shard_map/pallas_call | solution.py:614
  48.5 2.0 collective-permute-start.1
  51.1 12.0 %all_gather.13 = bf16[8,242,128]{2,1,0:T(8,128)(2,1)S(1)} all-gather(bf16[1,242,128]{2,1,0:T(8,128)(2,1)S(1)} %bitcast.211), channel_id=1, replica_groups=mesh['head'=4,'seq'=8] {'seq'}, dimensions={0}, use_global_device_ids=true | all-gather | bytes 557568 | tf_op jit(solution)/shard_map/all_gather | solution.py:1185
  65.9 13.8 %collective-permute-done.1 = bf16[256,512]{1,0:T(8,128)(2,1)S(1)} collective-permute-done((bf16[256,512]{1,0:T(8,128)(2,1)S(1)}, bf16[256,512]{1,0:T(8,128)(2,1)S(1)}, u32[]{:S(2)}, u32[]{:S(2)}) %collective-permute-start.1) | collective-permute-done | bytes 262176 | tf_op jit(solution)/shard_map/ppermute | solution.py:808
  84.7 66.1 %all-gather.4.cloned.1.call-done.refs_1_.refs_0_ = bf16[192,512,128]{2,1,0:T(8,128)(2,1)} async-done(((bf16[24,512,128]{2,1,0:T(8,128)(2,1)}), bf16[192,512,128]{2,1,0:T(8,128)(2,1)}) %all-gather.4.cloned.1.call-update) | async-done | bytes 25165840 | tf_op jit(solution)/shard_map/all_gather | solution.py:1188
  155.2 13.0 %shard_map.165 = (bf16[2048,3072]{1,0:T(8,128)(2,1)}, f32[256,3072]{1,0:T(8,128)S(1)}) custom-call(s32[96]{0:T(128)S(1)} %reshape.251.order_ref, bf16[256,2048]{1,0:T(8,128)(2,1)S(1)} %copy-done.10, bf16[192,512,128]{2,1,0:T(8,128)(2,1)} %all-gather.4.cloned.1.call-done.refs_1_.refs_0_, bf16[160,512,128]{2,1,0:T(8,128)(2,1)} %get-tuple-element.157.refs_2_.refs_1_), custom_call_target="tpu_custom_call" | custom-call | flops 3221225472 | bytes 25165824 | tf_op jit(solution)/shard_map/pallas_call | solution.py:742
  168.2 2.2 collective-permute-start.9
  171.2 40.6 %shard_map.166 = (f32[4,256,256]{2,1,0:T(8,128)S(1)}, f32[4,256,256]{2,1,0:T(8,128)S(1)}, f32[4,256,128]{2,1,0:T(8,128)S(1)}, f32[4,256,128]{2,1,0:T(8,128)S(1)}...) custom-call(f32[256,3072]{1,0:T(8,128)} %copy-done, f32[256,3072]{1,0:T(8,128)} %copy-done, ...), custom_call_target="tpu_custom_call" | custom-call | tf_op jit(solution)/shard_map/pallas_call | solution.py:230
  211.9 4.4 collective-permute-start.15
  217.8 3.8 shard_map.168.refs_1_
  221.8 12.9 %collective-permute-done.15 = bf16[4,128,384]{2,1,0:T(8,128)(2,1)S(1)} collective-permute-done((bf16[4,128,384]{2,1,0:T(8,128)(2,1)S(1)}, bf16[4,128,384]{2,1,0:T(8,128)(2,1)S(1)}, u32[]{:S(2)}, u32[]{:S(2)}) %collective-permute-start.15) | collective-permute-done | bytes 393248 | tf_op jit(solution)/shard_map/ppermute | solution.py:841
  234.7 8.6 %collective-permute-done.13 = bf16[4,128,384]{2,1,0:T(8,128)(2,1)S(1)} collective-permute-done((bf16[4,128,384]{2,1,0:T(8,128)(2,1)S(1)}, bf16[4,128,384]{2,1,0:T(8,128)(2,1)S(1)}, u32[]{:S(2)}, u32[]{:S(2)}) %collective-permute-start.13) | collective-permute-done | bytes 393248 | tf_op jit(solution)/shard_map/ppermute | solution.py:841
  243.3 8.7 %collective-permute-done.11 = bf16[4,128,384]{2,1,0:T(8,128)(2,1)S(1)} collective-permute-done((bf16[4,128,384]{2,1,0:T(8,128)(2,1)S(1)}, bf16[4,128,384]{2,1,0:T(8,128)(2,1)S(1)}, u32[]{:S(2)}, u32[]{:S(2)}) %collective-permute-start.11) | collective-permute-done | bytes 393248 | tf_op jit(solution)/shard_map/ppermute | solution.py:841
  255.8 3.8 shard_map.167
  262.6 2.4 collective-permute-start.18
  265.8 12.8 %all-gather.6.cloned.1.call-done.refs_0_ = bf16[160,512,128]{2,1,0:T(8,128)(2,1)} async-done(((bf16[20,512,128]{2,1,0:T(8,128)(2,1)}), bf16[160,512,128]{2,1,0:T(8,128)(2,1)}) %all-gather.6.cloned.1.call-update) | async-done | bytes 20971536 | tf_op jit(solution)/shard_map/all_gather | solution.py:1225
  278.6 4.4 shard_map.170.refs_1_
  283.0 12.1 %shard_map.171.refs_1_ = bf16[2048,2816]{1,0:T(8,128)(2,1)} custom-call(s32[88]{0:T(128)S(1)} %reshape.254.order_ref, bf16[160,512,128]{2,1,0:T(8,128)(2,1)} %all-gather.6.cloned.1.call-done.refs_0_, bf16[192,512,128]{2,1,0:T(8,128)(2,1)} %all-gather.4.cloned.1.call-done.refs_1_.refs_0_), custom_call_target="tpu_custom_call" | custom-call | bytes 23068672 | tf_op jit(solution)/shard_map/pallas_call | solution.py:742
  295.5 3.4 collective-permute-start.22
  299.9 6.7 collective-permute-done.22
  306.6 15.2 %collective-permute-done.21 = bf16[256,512]{1,0:T(8,128)(2,1)S(1)} collective-permute-done((bf16[256,512]{1,0:T(8,128)(2,1)S(1)}, bf16[256,512]{1,0:T(8,128)(2,1)S(1)}, u32[]{:S(2)}, u32[]{:S(2)}) %collective-permute-start.21) | collective-permute-done | bytes 262176 | tf_op jit(solution)/shard_map/ppermute | solution.py:808
  324.7 6.8 fusion.22
  331.5 3.8 multiply_convert_fusion.1
  335.3 2.3 copy.61.left_ref
  339.1 4.5 shard_map.176
  343.6 5.0 shard_map.177
  348.6 4.9 shard_map.178
  354.6 8.3 %shard_map.179 = (bf16[256,512]{1,0:T(8,128)(2,1)S(1)}, bf16[256,512]{1,0:T(8,128)(2,1)S(1)}, bf16[256,512]{1,0:T(8,128)(2,1)S(1)}, bf16[256,512]{1,0:T(8,128)(2,1)S(1)}) custom-call(s32[1]{0:T(128)} %bitcast.part_ref, bf16[256,2816]{1,0:T(8,128)(2,1)S(1)} %pad_maximum_fusion.1.right_ref.refs_0_, bf16[2048,2816]{1,0:T(8,128)(2,1)} %shard_map.171.refs_1_), custom_call_target="tpu_custom_call" | custom-call | flops 2952790016 | bytes 11534336 | tf_op jit(solution)/shard_map/pallas_call | solution.py:791
  363.0 2.1 collective-permute-start.27
  365.1 2.3 collective-permute-start.28
  367.4 6.7 collective-permute-done.26
  374.1 10.3 %collective-permute-done.27 = bf16[256,512]{1,0:T(8,128)(2,1)S(1)} collective-permute-done((bf16[256,512]{1,0:T(8,128)(2,1)S(1)}, bf16[256,512]{1,0:T(8,128)(2,1)S(1)}, u32[]{:S(2)}, u32[]{:S(2)}) %collective-permute-start.27) | collective-permute-done | bytes 262176 | tf_op jit(solution)/shard_map/ppermute | solution.py:808
  384.8 4.8 collective-permute-start.30
  391.4 3.0 collective-permute-start.33
  396.0 14.4 %collective-permute-done.33 = bf16[256,512]{1,0:T(8,128)(2,1)S(1)} collective-permute-done((bf16[256,512]{1,0:T(8,128)(2,1)S(1)}, bf16[256,512]{1,0:T(8,128)(2,1)S(1)}, u32[]{:S(2)}, u32[]{:S(2)}) %collective-permute-start.33) | collective-permute-done | bytes 262176 | tf_op jit(solution)/shard_map/ppermute | solution.py:808
  416.0 4.0 shard_map.180
  423.6 3.9 shard_map.184
  427.6 4.0 shard_map.185
  431.6 4.1 collective-permute-done.40
  435.7 3.2 collective-permute-done.38
  438.9 5.9 collective-permute-done.36
  446.5 4.5 shard_map.181.d_leave_ref
  451.1 22.2 %shard_map.182 = (bf16[256,512]{1,0:T(8,128)(2,1)S(1)}, bf16[256,512]{1,0:T(8,128)(2,1)S(1)}, bf16[256,1024]{1,0:T(8,128)(2,1)S(1)}, f32[8,512]{1,0:T(8,128)S(1)...) custom-call(f32[256,3072]{1,0:T(8,128)} %copy-done, ...), custom_call_target="tpu_custom_call" | custom-call | tf_op jit(solution)/shard_map/pallas_call | solution.py:522
  476.5 4.0 shard_map.186
  480.5 3.2 shard_map.187
  483.7 3.2 shard_map.188
  486.9 13.3 %reduce-scatter.4.cloned.1.call-done.refs_0_ = bf16[20,512,128]{2,1,0:T(8,128)(2,1)} async-done(((bf16[160,512,128]{2,1,0:T(8,128)(2,1)}), bf16[20,512,128]{2,1,0:T(8,128)(2,1)}) %reduce-scatter.4.cloned.1.call-update) | async-done | bytes 2621456 | tf_op jit(solution)/shard_map/reduce_scatter | solution.py:1307
  502.6 4.5 shard_map.172
  508.7 2.4 collective-permute-start.24
  511.8 11.3 %shard_map.183 = (bf16[256,512]{1,0:T(8,128)(2,1)S(1)}, bf16[256,512]{1,0:T(8,128)(2,1)S(1)}, bf16[256,512]{1,0:T(8,128)(2,1)S(1)}, bf16[256,512]{1,0:T(8,128)(2,1)S(1)}) custom-call(s32[1]{0:T(128)} %bitcast.part_ref, bf16[256,3072]{1,0:T(8,128)(2,1)S(1)} %pad_maximum_fusion.refs_0_, bf16[2048,3072]{1,0:T(8,128)(2,1)} %get-tuple-element.217.refs_1_, ...), custom_call_target="tpu_custom_call" | custom-call | flops 3355443200 | bytes 13107200 | tf_op jit(solution)/shard_map/pallas_call | solution.py:791
  523.6 3.4 collective-permute-start.44
  528.0 2.1 collective-permute-done.24
  530.1 5.4 collective-permute-done.43
  535.5 17.1 %collective-permute-done.44 = bf16[256,512]{1,0:T(8,128)(2,1)S(1)} collective-permute-done((bf16[256,512]{1,0:T(8,128)(2,1)S(1)}, bf16[256,512]{1,0:T(8,128)(2,1)S(1)}, u32[]{:S(2)}, u32[]{:S(2)}) %collective-permute-start.44) | collective-permute-done | bytes 262176 | tf_op jit(solution)/shard_map/ppermute | solution.py:808
  553.9 5.7 collective-permute-start.47
  561.6 3.3 collective-permute-done.48
  568.0 6.3 collective-permute-done.50
  575.9 2.2 fusion.13
  578.1 3.9 collective-permute-done.51
  582.0 80.8 %reduce-scatter.6.cloned.1.call-done.refs_1_ = bf16[24,512,128]{2,1,0:T(8,128)(2,1)} async-done(((bf16[192,512,128]{2,1,0:T(8,128)(2,1)}), bf16[24,512,128]{2,1,0:T(8,128)(2,1)}) %reduce-scatter.6.cloned.1.call-update) | async-done | bytes 3145744 | tf_op jit(solution)/shard_map/reduce_scatter | solution.py:1363
  664.6 39.8 %shard_map.190 = (f32[44,65536]{1,0:T(8,128)}, f32[44,65536]{1,0:T(8,128)}, f32[44,65536]{1,0:T(8,128)}, f32[44,65536]{1,0:T(8,128)}, bf16[44,65536]{1,0:T(8,128)(2,1)}) custom-call(s32[48]{0:T(128)S(1)} %copy-done.36, s32[48]{0:T(128)S(1)} %get-tuple-element.303.sources_ref, s32[48]{0:T(128)S(1)} %get-tuple-element.302.rows_ref, ...), custom_call_target="tpu_custom_call" | custom-call | tf_op jit(solution)/shard_map/pallas_call | solution.py:1024
  (398 shorter events, 75.1 us)
Async XLA Ops:
  7.2 143.7 %all-gather.4.cloned.1.call-start = ((), (), s32[]{:S(2)}) async-start(), calls=%async_computation.3 | async-start | bytes 28311552 | tf_op jit(solution)/shard_map/all_gather | solution.py:1188
  24.4 22.5 %collective-permute-start.4 = (bf16[1,1088]{1,0:T(2,128)(2,1)S(1)}, bf16[1,1088]{1,0:T(2,128)(2,1)S(1)}, u32[]{:S(2)}, u32[]{:S(2)}) collective-permute-start(bf16[1,1088]{1,0:T(2,128)(2,1)S(1)} %get-tuple-element.305), channel_id=1, source_target_pairs={{0,16},{8,24},{16,0},{24,8},{1,17},{9,25},{17,1},{25,9},{2,18},{10... | collective-permute-start | bytes 6536 | tf_op jit(solution)/shard_map/ppermute | solution.py:808
  28.5 18.8 %collective-permute-start.3 = (bf16[1,1088]{1,0:T(2,128)(2,1)S(1)}, bf16[1,1088]{1,0:T(2,128)(2,1)S(1)}, u32[]{:S(2)}, u32[]{:S(2)}) collective-permute-start(bf16[1,1088]{1,0:T(2,128)(2,1)S(1)} %get-tuple-element.305), channel_id=1, source_target_pairs={{0,8},{8,0},{16,24},{24,16},{1,9},{9,1},{17,25},{25,17},{2,10},{10... | collective-permute-start | bytes 6536 | tf_op jit(solution)/shard_map/ppermute | solution.py:808
  30.1 18.5 %collective-permute-start.5 = (bf16[1,1088]{1,0:T(2,128)(2,1)S(1)}, bf16[1,1088]{1,0:T(2,128)(2,1)S(1)}, u32[]{:S(2)}, u32[]{:S(2)}) collective-permute-start(bf16[1,1088]{1,0:T(2,128)(2,1)S(1)} %get-tuple-element.305), channel_id=1, source_target_pairs={{0,24},{8,16},{16,8},{24,0},{1,25},{9,17},{17,9},{25,1},{2,26},{10... | collective-permute-start | bytes 6536 | tf_op jit(solution)/shard_map/ppermute | solution.py:808
  30.1 50.8 %collective-permute-start.7 = (bf16[256,512]{1,0:T(8,128)(2,1)}, bf16[256,512]{1,0:T(8,128)(2,1)}, u32[]{:S(2)}, u32[]{:S(2)}) collective-permute-start(bf16[256,512]{1,0:T(8,128)(2,1)} %param.16), channel_id=1, source_target_pairs={{0,16},{8,24},{16,0},{24,8},{1,17},{9,25},{17,1},{25,9},{2,18},{10... | collective-permute-start | bytes 786440 | tf_op jit(solution)/shard_map/ppermute | solution.py:808
  32.0 48.9 %collective-permute-start.6 = (bf16[256,512]{1,0:T(8,128)(2,1)}, bf16[256,512]{1,0:T(8,128)(2,1)}, u32[]{:S(2)}, u32[]{:S(2)}) collective-permute-start(bf16[256,512]{1,0:T(8,128)(2,1)} %param.16), channel_id=1, source_target_pairs={{0,8},{8,0},{16,24},{24,16},{1,9},{9,1},{17,25},{25,17},{2,10},{10... | collective-permute-start | bytes 786440 | tf_op jit(solution)/shard_map/ppermute | solution.py:808
  46.9 18.0 %collective-permute-start = (bf16[256,512]{1,0:T(8,128)(2,1)S(1)}, bf16[256,512]{1,0:T(8,128)(2,1)S(1)}, u32[]{:S(2)}, u32[]{:S(2)}) collective-permute-start(bf16[256,512]{1,0:T(8,128)(2,1)S(1)} %copy-done.50), channel_id=1, source_target_pairs={{0,8},{8,0},{16,24},{24,16},{1,9},{9,1},{17,25},{25,17},{2,10},{10... | collective-permute-start | bytes 786440 | tf_op jit(solution)/shard_map/ppermute | solution.py:808
  47.3 18.7 %collective-permute-start.2 = (bf16[256,512]{1,0:T(8,128)(2,1)S(1)}, bf16[256,512]{1,0:T(8,128)(2,1)S(1)}, u32[]{:S(2)}, u32[]{:S(2)}) collective-permute-start(bf16[256,512]{1,0:T(8,128)(2,1)S(1)} %copy-done.50), channel_id=1, source_target_pairs={{0,24},{8,16},{16,8},{24,0},{1,25},{9,17},{17,9},{25,1},{2,26},{10... | collective-permute-start | bytes 786440 | tf_op jit(solution)/shard_map/ppermute | solution.py:808
  48.5 31.3 %collective-permute-start.1 = (bf16[256,512]{1,0:T(8,128)(2,1)S(1)}, bf16[256,512]{1,0:T(8,128)(2,1)S(1)}, u32[]{:S(2)}, u32[]{:S(2)}) collective-permute-start(bf16[256,512]{1,0:T(8,128)(2,1)S(1)} %copy-done.50), channel_id=1, source_target_pairs={{0,16},{8,24},{16,0},{24,8},{1,17},{9,25},{17,1},{25,9},{2,18},{10... | collective-permute-start | bytes 786440 | tf_op jit(solution)/shard_map/ppermute | solution.py:808
  64.9 16.0 %collective-permute-start.8 = (bf16[256,512]{1,0:T(8,128)(2,1)}, bf16[256,512]{1,0:T(8,128)(2,1)}, u32[]{:S(2)}, u32[]{:S(2)}) collective-permute-start(bf16[256,512]{1,0:T(8,128)(2,1)} %param.16), channel_id=1, source_target_pairs={{0,24},{8,16},{16,8},{24,0},{1,25},{9,17},{17,9},{25,1},{2,26},{10... | collective-permute-start | bytes 786440 | tf_op jit(solution)/shard_map/ppermute | solution.py:808
  84.2 68.3 %copy-start.1 = (bf16[256,2048]{0,1:T(8,128)(2,1)}, bf16[256,2048]{0,1:T(8,128)(2,1)S(1)}, u32[]{:S(2)}) copy-start(bf16[256,2048]{0,1:T(8,128)(2,1)S(1)} %fusion.2) | copy-start | bytes 3145732
  150.9 127.8 %all-gather.6.cloned.1.call-start = ((), (), s32[]{:S(2)}) async-start(), calls=%async_computation.4 | async-start | bytes 23592960 | tf_op jit(solution)/shard_map/all_gather | solution.py:1225
  151.6 348.5 %reduce-scatter.4.cloned.1.call-start = ((), (), s32[]{:S(2)}) async-start(), calls=%async_computation.5 | async-start | bytes 23592960 | tf_op jit(solution)/shard_map/reduce_scatter | solution.py:1307
  168.2 3.0 collective-permute-start.9
  171.2 40.7 %copy-start.11 = (f32[8,2048]{1,0:T(8,128)}, f32[8,2048]{1,0:T(8,128)S(1)}, u32[]{:S(2)}) copy-start(f32[8,2048]{1,0:T(8,128)S(1)} %pad.39.rq.rk.rv) | copy-start | bytes 196612
  211.9 42.2 %copy-start.18 = (f32[4,256,128]{2,1,0:T(8,128)}, f32[4,256,128]{2,1,0:T(8,128)S(1)}, u32[]{:S(2)}) copy-start(f32[4,256,128]{2,1,0:T(8,128)S(1)} %get-tuple-element.163.reach_ref) | copy-start | bytes 1572868
  211.9 22.8 %collective-permute-start.15 = (bf16[4,128,384]{2,1,0:T(8,128)(2,1)S(1)}, bf16[4,128,384]{2,1,0:T(8,128)(2,1)S(1)}, u32[]{:S(2)}, u32[]{:S(2)}) collective-permute-start(bf16[4,128,384]{2,1,0:T(8,128)(2,1)S(1)} %get-tuple-element.162), channel_id=1, source_target_pairs={{0,6},{1,7},{2,4},{3,5},{4,2},{5,3},{6,0},{7,1},{8,14},{9,15},{10,... | collective-permute-start | bytes 1179656 | tf_op jit(solution)/shard_map/ppermute | solution.py:841
  216.4 26.9 %collective-permute-start.13 = (bf16[4,128,384]{2,1,0:T(8,128)(2,1)S(1)}, bf16[4,128,384]{2,1,0:T(8,128)(2,1)S(1)}, u32[]{:S(2)}, u32[]{:S(2)}) collective-permute-start(bf16[4,128,384]{2,1,0:T(8,128)(2,1)S(1)} %get-tuple-element.162), channel_id=1, source_target_pairs={{0,4},{1,5},{2,6},{3,7},{4,0},{5,1},{6,2},{7,3},{8,12},{9,13},{10,... | collective-permute-start | bytes 1179656 | tf_op jit(solution)/shard_map/ppermute | solution.py:841
  217.8 34.2 %collective-permute-start.11 = (bf16[4,128,384]{2,1,0:T(8,128)(2,1)S(1)}, bf16[4,128,384]{2,1,0:T(8,128)(2,1)S(1)}, u32[]{:S(2)}, u32[]{:S(2)}) collective-permute-start(bf16[4,128,384]{2,1,0:T(8,128)(2,1)S(1)} %get-tuple-element.162), channel_id=1, source_target_pairs={{0,2},{1,3},{2,0},{3,1},{4,6},{5,7},{6,4},{7,5},{8,10},{9,11},{10,... | collective-permute-start | bytes 1179656 | tf_op jit(solution)/shard_map/ppermute | solution.py:841
  217.8 34.2 %collective-permute-start.10 = (bf16[4,128,384]{2,1,0:T(8,128)(2,1)S(1)}, bf16[4,128,384]{2,1,0:T(8,128)(2,1)S(1)}, u32[]{:S(2)}, u32[]{:S(2)}) collective-permute-start(bf16[4,128,384]{2,1,0:T(8,128)(2,1)S(1)} %get-tuple-element.162), channel_id=1, source_target_pairs={{0,1},{1,0},{2,3},{3,2},{4,5},{5,4},{6,7},{7,6},{8,9},{9,8},{10,11... | collective-permute-start | bytes 1179656 | tf_op jit(solution)/shard_map/ppermute | solution.py:841
  221.7 37.9 %copy-start.4 = (bf16[1024,2048]{1,0:T(8,128)(2,1)}, bf16[1024,2048]{1,0:T(8,128)(2,1)S(1)}, u32[]{:S(2)}) copy-start(bf16[1024,2048]{1,0:T(8,128)(2,1)S(1)} %shard_map.168.refs_1_) | copy-start | bytes 12582916
  234.7 19.3 %collective-permute-start.16 = (bf16[4,128,384]{2,1,0:T(8,128)(2,1)S(1)}, bf16[4,128,384]{2,1,0:T(8,128)(2,1)S(1)}, u32[]{:S(2)}, u32[]{:S(2)}) collective-permute-start(bf16[4,128,384]{2,1,0:T(8,128)(2,1)S(1)} %collective-permute-done.15), channel_id=1, source_target_pairs={{0,1},{1,0},{2,3},{3,2},{4,5},{5,4},{6,7},{7,6},{8,9},{9,8},{10,11... | collective-permute-start | bytes 1179656 | tf_op jit(solution)/shard_map/ppermute | solution.py:841
  243.3 10.5 %collective-permute-start.14 = (bf16[4,128,384]{2,1,0:T(8,128)(2,1)S(1)}, bf16[4,128,384]{2,1,0:T(8,128)(2,1)S(1)}, u32[]{:S(2)}, u32[]{:S(2)}) collective-permute-start(bf16[4,128,384]{2,1,0:T(8,128)(2,1)S(1)} %collective-permute-done.13), channel_id=1, source_target_pairs={{0,1},{1,0},{2,3},{3,2},{4,5},{5,4},{6,7},{7,6},{8,9},{9,8},{10,11... | collective-permute-start | bytes 1179656 | tf_op jit(solution)/shard_map/ppermute | solution.py:841
  252.0 1.7 collective-permute-start.12
  260.9 34.3 %copy-start.23 = (bf16[256,512]{1,0:T(8,128)(2,1)}, bf16[256,512]{1,0:T(8,128)(2,1)S(1)}, u32[]{:S(2)}) copy-start(bf16[256,512]{1,0:T(8,128)(2,1)S(1)} %get-tuple-element.172) | copy-start | bytes 786436
  260.9 34.2 %collective-permute-start.17 = (bf16[256,512]{1,0:T(8,128)(2,1)S(1)}, bf16[256,512]{1,0:T(8,128)(2,1)S(1)}, u32[]{:S(2)}, u32[]{:S(2)}) collective-permute-start(bf16[256,512]{1,0:T(8,128)(2,1)S(1)} %get-tuple-element.168), channel_id=1, source_target_pairs={{0,8},{8,0},{16,24},{24,16},{1,9},{9,1},{17,25},{25,17},{2,10},{10... | collective-permute-start | bytes 786440 | tf_op jit(solution)/shard_map/ppermute | solution.py:808
  262.6 32.6 %collective-permute-start.18 = (bf16[256,512]{1,0:T(8,128)(2,1)S(1)}, bf16[256,512]{1,0:T(8,128)(2,1)S(1)}, u32[]{:S(2)}, u32[]{:S(2)}) collective-permute-start(bf16[256,512]{1,0:T(8,128)(2,1)S(1)} %get-tuple-element.169), channel_id=1, source_target_pairs={{0,16},{8,24},{16,0},{24,8},{1,17},{9,25},{17,1},{25,9},{2,18},{10... | collective-permute-start | bytes 786440 | tf_op jit(solution)/shard_map/ppermute | solution.py:808
  265.0 30.2 %collective-permute-start.19 = (bf16[256,512]{1,0:T(8,128)(2,1)S(1)}, bf16[256,512]{1,0:T(8,128)(2,1)S(1)}, u32[]{:S(2)}, u32[]{:S(2)}) collective-permute-start(bf16[256,512]{1,0:T(8,128)(2,1)S(1)} %get-tuple-element.170), channel_id=1, source_target_pairs={{0,24},{8,16},{16,8},{24,0},{1,25},{9,17},{17,9},{25,1},{2,26},{10... | collective-permute-start | bytes 786440 | tf_op jit(solution)/shard_map/ppermute | solution.py:808
  295.5 11.1 %collective-permute-start.22 = (bf16[256,512]{1,0:T(8,128)(2,1)S(1)}, bf16[256,512]{1,0:T(8,128)(2,1)S(1)}, u32[]{:S(2)}, u32[]{:S(2)}) collective-permute-start(bf16[256,512]{1,0:T(8,128)(2,1)S(1)} %fusion.41), channel_id=1, source_target_pairs={{0,24},{8,16},{16,8},{24,0},{1,25},{9,17},{17,9},{25,1},{2,26},{10... | collective-permute-start | bytes 786440 | tf_op jit(solution)/shard_map/ppermute | solution.py:808
  298.8 23.0 %collective-permute-start.21 = (bf16[256,512]{1,0:T(8,128)(2,1)S(1)}, bf16[256,512]{1,0:T(8,128)(2,1)S(1)}, u32[]{:S(2)}, u32[]{:S(2)}) collective-permute-start(bf16[256,512]{1,0:T(8,128)(2,1)S(1)} %fusion.41), channel_id=1, source_target_pairs={{0,16},{8,24},{16,0},{24,8},{1,17},{9,25},{17,1},{25,9},{2,18},{10... | collective-permute-start | bytes 786440 | tf_op jit(solution)/shard_map/ppermute | solution.py:808
  298.9 23.0 %collective-permute-start.20 = (bf16[256,512]{1,0:T(8,128)(2,1)S(1)}, bf16[256,512]{1,0:T(8,128)(2,1)S(1)}, u32[]{:S(2)}, u32[]{:S(2)}) collective-permute-start(bf16[256,512]{1,0:T(8,128)(2,1)S(1)} %fusion.41), channel_id=1, source_target_pairs={{0,8},{8,0},{16,24},{24,16},{1,9},{9,1},{17,25},{25,17},{2,10},{10... | collective-permute-start | bytes 786440 | tf_op jit(solution)/shard_map/ppermute | solution.py:808
  353.5 309.3 %reduce-scatter.6.cloned.1.call-start = ((), (), s32[]{:S(2)}) async-start(), calls=%async_computation.6 | async-start | bytes 28311552 | tf_op jit(solution)/shard_map/reduce_scatter | solution.py:1363
  354.6 29.8 %copy-start.48 = (bf16[256,512]{1,0:T(8,128)(2,1)S(1)}, bf16[256,512]{1,0:T(8,128)(2,1)}, u32[]{:S(2)}) copy-start(bf16[256,512]{1,0:T(8,128)(2,1)} %copy-done.47) | copy-start | bytes 786436
  362.9 11.2 %collective-permute-start.26 = (bf16[256,512]{1,0:T(8,128)(2,1)S(1)}, bf16[256,512]{1,0:T(8,128)(2,1)S(1)}, u32[]{:S(2)}, u32[]{:S(2)}) collective-permute-start(bf16[256,512]{1,0:T(8,128)(2,1)S(1)} %get-tuple-element.196), channel_id=1, source_target_pairs={{0,8},{8,0},{16,24},{24,16},{1,9},{9,1},{17,25},{25,17},{2,10},{10... | collective-permute-start | bytes 786440 | tf_op jit(solution)/shard_map/ppermute | solution.py:808
  363.0 21.4 %collective-permute-start.27 = (bf16[256,512]{1,0:T(8,128)(2,1)S(1)}, bf16[256,512]{1,0:T(8,128)(2,1)S(1)}, u32[]{:S(2)}, u32[]{:S(2)}) collective-permute-start(bf16[256,512]{1,0:T(8,128)(2,1)S(1)} %get-tuple-element.197), channel_id=1, source_target_pairs={{0,16},{8,24},{16,0},{24,8},{1,17},{9,25},{17,1},{25,9},{2,18},{10... | collective-permute-start | bytes 786440 | tf_op jit(solution)/shard_map/ppermute | solution.py:808
  365.1 19.3 %collective-permute-start.28 = (bf16[256,512]{1,0:T(8,128)(2,1)S(1)}, bf16[256,512]{1,0:T(8,128)(2,1)S(1)}, u32[]{:S(2)}, u32[]{:S(2)}) collective-permute-start(bf16[256,512]{1,0:T(8,128)(2,1)S(1)} %get-tuple-element.198), channel_id=1, source_target_pairs={{0,24},{8,16},{16,8},{24,0},{1,25},{9,17},{17,9},{25,1},{2,26},{10... | collective-permute-start | bytes 786440 | tf_op jit(solution)/shard_map/ppermute | solution.py:808
  384.8 9.6 %collective-permute-start.30 = (f32[2,128]{1,0:T(2,128)S(1)}, f32[2,128]{1,0:T(2,128)S(1)}, u32[]{:S(2)}, u32[]{:S(2)}) collective-permute-start(f32[2,128]{1,0:T(2,128)S(1)} %bitcast.233), channel_id=1, source_target_pairs={{0,16},{8,24},{16,0},{24,8},{1,17},{9,25},{17,1},{25,9},{2,18},{10... | collective-permute-start | bytes 3080 | tf_op jit(solution)/shard_map/ppermute | solution.py:808
  389.8 6.1 collective-permute-start.31
  391.3 4.6 collective-permute-start.29
  391.4 19.1 %collective-permute-start.33 = (bf16[256,512]{1,0:T(8,128)(2,1)S(1)}, bf16[256,512]{1,0:T(8,128)(2,1)S(1)}, u32[]{:S(2)}, u32[]{:S(2)}) collective-permute-start(bf16[256,512]{1,0:T(8,128)(2,1)S(1)} %convert_element_type.208), channel_id=1, source_target_pairs={{0,16},{8,24},{16,0},{24,8},{1,17},{9,25},{17,1},{25,9},{2,18},{10... | collective-permute-start | bytes 786440 | tf_op jit(solution)/shard_map/ppermute | solution.py:808
  394.4 16.5 %collective-permute-start.32 = (bf16[256,512]{1,0:T(8,128)(2,1)S(1)}, bf16[256,512]{1,0:T(8,128)(2,1)S(1)}, u32[]{:S(2)}, u32[]{:S(2)}) collective-permute-start(bf16[256,512]{1,0:T(8,128)(2,1)S(1)} %convert_element_type.208), channel_id=1, source_target_pairs={{0,8},{8,0},{16,24},{24,16},{1,9},{9,1},{17,25},{25,17},{2,10},{10... | collective-permute-start | bytes 786440 | tf_op jit(solution)/shard_map/ppermute | solution.py:808
  394.4 16.5 %collective-permute-start.34 = (bf16[256,512]{1,0:T(8,128)(2,1)S(1)}, bf16[256,512]{1,0:T(8,128)(2,1)S(1)}, u32[]{:S(2)}, u32[]{:S(2)}) collective-permute-start(bf16[256,512]{1,0:T(8,128)(2,1)S(1)} %convert_element_type.208), channel_id=1, source_target_pairs={{0,24},{8,16},{16,8},{24,0},{1,25},{9,17},{17,9},{25,1},{2,26},{10... | collective-permute-start | bytes 786440 | tf_op jit(solution)/shard_map/ppermute | solution.py:808
  420.0 15.7 %collective-permute-start.40 = (bf16[4,128,256]{2,1,0:T(8,128)(2,1)S(1)}, bf16[4,128,256]{2,1,0:T(8,128)(2,1)S(1)}, u32[]{:S(2)}, u32[]{:S(2)}) collective-permute-start(bf16[4,128,256]{2,1,0:T(8,128)(2,1)S(1)} %get-tuple-element.206), channel_id=1, source_target_pairs={{0,6},{1,7},{2,4},{3,5},{4,2},{5,3},{6,0},{7,1},{8,14},{9,15},{10,... | collective-permute-start | bytes 786440 | tf_op jit(solution)/shard_map/ppermute | solution.py:841
  421.7 17.2 %collective-permute-start.38 = (bf16[4,128,256]{2,1,0:T(8,128)(2,1)S(1)}, bf16[4,128,256]{2,1,0:T(8,128)(2,1)S(1)}, u32[]{:S(2)}, u32[]{:S(2)}) collective-permute-start(bf16[4,128,256]{2,1,0:T(8,128)(2,1)S(1)} %get-tuple-element.206), channel_id=1, source_target_pairs={{0,4},{1,5},{2,6},{3,7},{4,0},{5,1},{6,2},{7,3},{8,12},{9,13},{10,... | collective-permute-start | bytes 786440 | tf_op jit(solution)/shard_map/ppermute | solution.py:841
  422.9 21.9 %collective-permute-start.36 = (bf16[4,128,256]{2,1,0:T(8,128)(2,1)S(1)}, bf16[4,128,256]{2,1,0:T(8,128)(2,1)S(1)}, u32[]{:S(2)}, u32[]{:S(2)}) collective-permute-start(bf16[4,128,256]{2,1,0:T(8,128)(2,1)S(1)} %get-tuple-element.206), channel_id=1, source_target_pairs={{0,2},{1,3},{2,0},{3,1},{4,6},{5,7},{6,4},{7,5},{8,10},{9,11},{10,... | collective-permute-start | bytes 786440 | tf_op jit(solution)/shard_map/ppermute | solution.py:841
  423.6 21.2 %collective-permute-start.35 = (bf16[4,128,256]{2,1,0:T(8,128)(2,1)S(1)}, bf16[4,128,256]{2,1,0:T(8,128)(2,1)S(1)}, u32[]{:S(2)}, u32[]{:S(2)}) collective-permute-start(bf16[4,128,256]{2,1,0:T(8,128)(2,1)S(1)} %get-tuple-element.206), channel_id=1, source_target_pairs={{0,1},{1,0},{2,3},{3,2},{4,5},{5,4},{6,7},{7,6},{8,9},{9,8},{10,11... | collective-permute-start | bytes 786440 | tf_op jit(solution)/shard_map/ppermute | solution.py:841
  435.7 10.7 %collective-permute-start.41 = (bf16[4,128,256]{2,1,0:T(8,128)(2,1)S(1)}, bf16[4,128,256]{2,1,0:T(8,128)(2,1)S(1)}, u32[]{:S(2)}, u32[]{:S(2)}) collective-permute-start(bf16[4,128,256]{2,1,0:T(8,128)(2,1)S(1)} %collective-permute-done.40), channel_id=1, source_target_pairs={{0,1},{1,0},{2,3},{3,2},{4,5},{5,4},{6,7},{7,6},{8,9},{9,8},{10,11... | collective-permute-start | bytes 786440 | tf_op jit(solution)/shard_map/ppermute | solution.py:841
  438.9 7.4 %collective-permute-start.39 = (bf16[4,128,256]{2,1,0:T(8,128)(2,1)S(1)}, bf16[4,128,256]{2,1,0:T(8,128)(2,1)S(1)}, u32[]{:S(2)}, u32[]{:S(2)}) collective-permute-start(bf16[4,128,256]{2,1,0:T(8,128)(2,1)S(1)} %collective-permute-done.38), channel_id=1, source_target_pairs={{0,1},{1,0},{2,3},{3,2},{4,5},{5,4},{6,7},{7,6},{8,9},{9,8},{10,11... | collective-permute-start | bytes 786440 | tf_op jit(solution)/shard_map/ppermute | solution.py:841
  444.8 1.5 collective-permute-start.37
  473.4 3.1 collective-permute-start.42
  507.1 19.9 %collective-permute-start.23 = (bf16[256,512]{1,0:T(8,128)(2,1)S(1)}, bf16[256,512]{1,0:T(8,128)(2,1)S(1)}, u32[]{:S(2)}, u32[]{:S(2)}) collective-permute-start(bf16[256,512]{1,0:T(8,128)(2,1)S(1)} %get-tuple-element.180), channel_id=1, source_target_pairs={{0,8},{8,0},{16,24},{24,16},{1,9},{9,1},{17,25},{25,17},{2,10},{10... | collective-permute-start | bytes 786440 | tf_op jit(solution)/shard_map/ppermute | solution.py:808
  508.7 21.4 %collective-permute-start.24 = (bf16[256,512]{1,0:T(8,128)(2,1)S(1)}, bf16[256,512]{1,0:T(8,128)(2,1)S(1)}, u32[]{:S(2)}, u32[]{:S(2)}) collective-permute-start(bf16[256,512]{1,0:T(8,128)(2,1)S(1)} %get-tuple-element.181), channel_id=1, source_target_pairs={{0,16},{8,24},{16,0},{24,8},{1,17},{9,25},{17,1},{25,9},{2,18},{10... | collective-permute-start | bytes 786440 | tf_op jit(solution)/shard_map/ppermute | solution.py:808
  511.1 19.0 %collective-permute-start.25 = (bf16[256,512]{1,0:T(8,128)(2,1)S(1)}, bf16[256,512]{1,0:T(8,128)(2,1)S(1)}, u32[]{:S(2)}, u32[]{:S(2)}) collective-permute-start(bf16[256,512]{1,0:T(8,128)(2,1)S(1)} %get-tuple-element.182), channel_id=1, source_target_pairs={{0,24},{8,16},{16,8},{24,0},{1,25},{9,17},{17,9},{25,1},{2,26},{10... | collective-permute-start | bytes 786440 | tf_op jit(solution)/shard_map/ppermute | solution.py:808
  523.1 29.5 %copy-start.24 = (bf16[256,512]{1,0:T(8,128)(2,1)S(1)}, bf16[256,512]{1,0:T(8,128)(2,1)}, u32[]{:S(2)}) copy-start(bf16[256,512]{1,0:T(8,128)(2,1)} %copy-done.23) | copy-start | bytes 786436
  523.1 29.5 %copy-start.52 = (bf16[256,512]{1,0:T(8,128)(2,1)S(1)}, bf16[256,512]{1,0:T(8,128)(2,1)}, u32[]{:S(2)}) copy-start(bf16[256,512]{1,0:T(8,128)(2,1)} %param.15) | copy-start | bytes 786436
  523.1 12.3 %collective-permute-start.43 = (bf16[256,512]{1,0:T(8,128)(2,1)S(1)}, bf16[256,512]{1,0:T(8,128)(2,1)S(1)}, u32[]{:S(2)}, u32[]{:S(2)}) collective-permute-start(bf16[256,512]{1,0:T(8,128)(2,1)S(1)} %get-tuple-element.221), channel_id=1, source_target_pairs={{0,8},{8,0},{16,24},{24,16},{1,9},{9,1},{17,25},{25,17},{2,10},{10... | collective-permute-start | bytes 786440 | tf_op jit(solution)/shard_map/ppermute | solution.py:808
  523.6 28.9 %collective-permute-start.44 = (bf16[256,512]{1,0:T(8,128)(2,1)S(1)}, bf16[256,512]{1,0:T(8,128)(2,1)S(1)}, u32[]{:S(2)}, u32[]{:S(2)}) collective-permute-start(bf16[256,512]{1,0:T(8,128)(2,1)S(1)} %get-tuple-element.222), channel_id=1, source_target_pairs={{0,16},{8,24},{16,0},{24,8},{1,17},{9,25},{17,1},{25,9},{2,18},{10... | collective-permute-start | bytes 786440 | tf_op jit(solution)/shard_map/ppermute | solution.py:808
  527.0 25.6 %collective-permute-start.45 = (bf16[256,512]{1,0:T(8,128)(2,1)S(1)}, bf16[256,512]{1,0:T(8,128)(2,1)S(1)}, u32[]{:S(2)}, u32[]{:S(2)}) collective-permute-start(bf16[256,512]{1,0:T(8,128)(2,1)S(1)} %get-tuple-element.223), channel_id=1, source_target_pairs={{0,24},{8,16},{16,8},{24,0},{1,25},{9,17},{17,9},{25,1},{2,26},{10... | collective-permute-start | bytes 786440 | tf_op jit(solution)/shard_map/ppermute | solution.py:808
  553.9 7.7 %collective-permute-start.47 = (f32[4,128]{1,0:T(4,128)S(1)}, f32[4,128]{1,0:T(4,128)S(1)}, u32[]{:S(2)}, u32[]{:S(2)}) collective-permute-start(f32[4,128]{1,0:T(4,128)S(1)} %pad_maximum_fusion.14), channel_id=1, source_target_pairs={{0,16},{8,24},{16,0},{24,8},{1,17},{9,25},{17,1},{25,9},{2,18},{10... | collective-permute-start | bytes 6152 | tf_op jit(solution)/shard_map/ppermute | solution.py:808
  559.5 5.4 collective-permute-start.48
  561.0 3.9 collective-permute-start.46
  565.1 1.3 collective-permute-start.49
  566.5 7.9 %collective-permute-start.50 = (f32[208,128]{1,0:T(8,128)S(1)}, f32[208,128]{1,0:T(8,128)S(1)}, u32[]{:S(2)}, u32[]{:S(2)}) collective-permute-start(f32[208,128]{1,0:T(8,128)S(1)} %bitcast_add_fusion), channel_id=1, source_target_pairs={{0,2},{1,3},{2,0},{3,1},{4,6},{5,7},{6,4},{7,5},{8,10},{9,11},{10,... | collective-permute-start | bytes 319496 | tf_op jit(solution)/shard_map/ppermute | solution.py:1409
  574.4 7.6 %collective-permute-start.51 = (f32[208,128]{1,0:T(8,128)S(1)}, f32[208,128]{1,0:T(8,128)S(1)}, u32[]{:S(2)}, u32[]{:S(2)}) collective-permute-start(f32[208,128]{1,0:T(8,128)S(1)} %fusion.90), channel_id=1, source_target_pairs={{0,4},{1,5},{2,6},{3,7},{4,0},{5,1},{6,2},{7,3},{8,12},{9,13},{10,... | collective-permute-start | bytes 319496 | tf_op jit(solution)/shard_map/ppermute | solution.py:1409
  (73 other events, 584.7 us)
Sparse Core Ops, SparseCore 0:
  20.7 130.1 all-gather.3
  154.2 124.4 all-gather.5
  353.6 146.4 reduce-scatter.3
  503.6 159.1 reduce-scatter.5

commit v3 on v2

--- a/solution.py
+++ b/solution.py
@@ -95,14 +95,24 @@
     return (piece_rates, small_rates)
 
 
-def product(left, right, left_axis, right_axis, exact=True):
-    return lax.dot_general(
-        left,
-        right,
-        (((left_axis,), (right_axis,)), ((), ())),
-        precision=EXACT_ARITHMETIC if exact else None,
-        preferred_element_type=jnp.float32,
-    )
+HEADS_A_STEP = 1
+
+
+def product(left, right, left_axis, right_axis, exact=False):
+    def dot(a, b):
+        return lax.dot_general(
+            a,
+            b,
+            (((left_axis,), (right_axis,)), ((), ())),
+            preferred_element_type=jnp.float32,
+        )
+
+    left_low, right_low = left.astype(jnp.bfloat16), right.astype(jnp.bfloat16)
+    if not exact:
+        return dot(left_low, right_low)
+    left_rest = (left - left_low.astype(jnp.float32)).astype(jnp.bfloat16)
+    right_rest = (right - right_low.astype(jnp.float32)).astype(jnp.bfloat16)
+    return dot(left_low, right_low) + (dot(left_low, right_rest) + dot(left_rest, right_low))
 
 
 def take_lane(wide, lane):
@@ -119,14 +129,14 @@
     return jnp.sum(jnp.where(diagonal, column, 0.0), axis=0, keepdims=True)
 
 
-def convolved(extended, block_ref, rim_ref, taps_ref):
+def convolved(extended, block_ref, rim_ref, taps_ref, columns):
     row_count = block_ref.shape[0]
-    extended[0:8, :] = rim_ref[...]
-    extended[8 : 8 + row_count, :] = block_ref[...]
+    extended[0:8, :] = rim_ref[:, columns]
+    extended[8 : 8 + row_count, :] = block_ref[:, columns]
     first = 8 - (KCONV - 1)
-    running = taps_ref[0:1, :] * extended[first : first + row_count, :]
+    running = taps_ref[0:1, columns] * extended[first : first + row_count, :]
     for tap in range(1, KCONV):
-        running = running + taps_ref[tap : tap + 1, :] * extended[
+        running = running + taps_ref[tap : tap + 1, columns] * extended[
             first + tap : first + tap + row_count, :
         ]
     return running
@@ -158,13 +168,13 @@
 
 def mixer_specs(local_heads, row_count):
     def spec(rows, width, first):
-        return pl.BlockSpec((rows, width), lambda h, first=first: (0, first + h))
+        return pl.BlockSpec((rows, width), lambda h, first=first // width: (0, first + h))
 
     def three(rows):
         return [
-            spec(rows, DK, 0),
-            spec(rows, DK, local_heads),
-            spec(rows, DV, 2 * local_heads * DK // DV),
+            spec(rows, HEADS_A_STEP * DK, 0),
+            spec(rows, HEADS_A_STEP * DK, local_heads * DK),
+            spec(rows, HEADS_A_STEP * DV, 2 * local_heads * DK),
         ]
 
     whole = pl.BlockSpec((row_count, 128), lambda h: (0, 0))
@@ -173,7 +183,11 @@
 
 
 def per_head(*shape):
-    return pl.BlockSpec((1,) + shape, lambda h: (h,) + (0,) * len(shape))
+    return pl.BlockSpec((HEADS_A_STEP,) + shape, lambda h: (h,) + (0,) * len(shape))
+
+
+def head_columns(sub):
+    return slice(DK * sub, DK * sub + DK), slice(DV * sub, DV * sub + DV)
 
 
 def mixer_local(local_heads, projected, rim, taps, decay_proj, scalars):
@@ -184,52 +198,57 @@
         pq, pk, pv, rq, rk, rv, tq, tk, tv, decay_ref, scalars_ref,
         solve_ref, fresh_ref, wy_ref, reach_ref, zero_ref, handoff_ref, ext_q, ext_k, ext_v,
     ):
-        head = pl.program_id(0)
-        queries = unit_rows(jax.nn.silu(convolved(ext_q, pq, rq, tq)))[0] * DK ** (-0.5)
-        key_rows = unit_rows(jax.nn.silu(convolved(ext_k, pk, rk, tk)))[0]
-        values = jax.nn.silu(convolved(ext_v, pv, rv, tv))
-        decay_in, rate, logs, beta, sums, within, row_ids, column_ids = decay_terms(
-            head, local_heads, decay_ref, scalars_ref
-        )
-        gram = product(key_rows, key_rows, 1, 1)
-        system = jnp.where(row_ids > column_ids, beta * gram * within, 0.0)
-        solve = jnp.where(row_ids == column_ids, 1.0, 0.0)
-        size = 1
-        while size < row_count:
-            lower = (row_ids // (2 * size) == column_ids // (2 * size)) & (
-                row_ids // size != column_ids // size
+        for sub in range(HEADS_A_STEP):
+            head = pl.program_id(0) * HEADS_A_STEP + sub
+            narrow, wide = head_columns(sub)
+            queries = unit_rows(jax.nn.silu(convolved(ext_q.at[sub], pq, rq, tq, narrow)))[0] * DK ** (-0.5)
+            key_rows = unit_rows(jax.nn.silu(convolved(ext_k.at[sub], pk, rk, tk, narrow)))[0]
+            values = jax.nn.silu(convolved(ext_v.at[sub], pv, rv, tv, wide))
+            decay_in, rate, logs, beta, sums, within, row_ids, column_ids = decay_terms(
+                head, local_heads, decay_ref, scalars_ref
             )
-            part = jnp.where(lower, system, 0.0)
-            if size == 1:
-                solve = solve - part
-            else:
-                solve = solve - product(solve, product(part, solve, 1, 0), 1, 0)
-            size *= 2
-        grown = jnp.exp(sums)
-        fresh = product(solve, beta * values, 1, 0)
-        wy_keys = product(solve, (beta * grown) * key_rows, 1, 0)
-        attention = product(queries, key_rows, 1, 1) * within
-        last = sums[row_count - 1 : row_count, :]
-        tail_keys = jnp.exp(last - sums) * key_rows
-        eye = lax.broadcasted_iota(jnp.int32, (DK, DK), 0) == lax.broadcasted_iota(
-            jnp.int32, (DK, DK), 1
-        )
-        solve_ref[0] = solve
-        fresh_ref[0] = fresh
-        wy_ref[0] = wy_keys
-        reach_ref[0] = grown * queries - product(attention, wy_keys, 1, 0)
-        zero_ref[0] = product(attention, fresh, 1, 0)
-        handoff_ref[0, :, :DK] = (
-            jnp.where(eye, jnp.exp(last), 0.0) - product(tail_keys, wy_keys, 0, 0)
-        ).astype(jnp.bfloat16)
-        handoff_ref[0, :, DK:] = product(tail_keys, fresh, 0, 0).astype(jnp.bfloat16)
+            gram = product(key_rows, key_rows, 1, 1, True)
+            system = jnp.where(row_ids > column_ids, beta * gram * within, 0.0)
+            solve = jnp.where(row_ids == column_ids, 1.0, 0.0)
+            size = 1
+            while size < row_count:
+                lower = (row_ids // (2 * size) == column_ids // (2 * size)) & (
+                    row_ids // size != column_ids // size
+                )
+                part = jnp.where(lower, system, 0.0)
+                if size == 1:
+                    solve = solve - part
+                else:
+                    solve = solve - product(solve, product(part, solve, 1, 0), 1, 0)
+                size *= 2
+            unit = jnp.where(row_ids == column_ids, 1.0, 0.0)
+            remainder = (unit - solve) - product(system, solve, 1, 0, True)
+            solve = solve + product(solve, remainder, 1, 0)
+            grown = jnp.exp(sums)
+            fresh = product(solve, beta * values, 1, 0, True)
+            wy_keys = product(solve, (beta * grown) * key_rows, 1, 0, True)
+            attention = product(queries, key_rows, 1, 1) * within
+            last = sums[row_count - 1 : row_count, :]
+            tail_keys = jnp.exp(last - sums) * key_rows
+            eye = lax.broadcasted_iota(jnp.int32, (DK, DK), 0) == lax.broadcasted_iota(
+                jnp.int32, (DK, DK), 1
+            )
+            solve_ref[sub] = solve
+            fresh_ref[sub] = fresh
+            wy_ref[sub] = wy_keys
+            reach_ref[sub] = grown * queries - product(attention, wy_keys, 1, 0)
+            zero_ref[sub] = product(attention, fresh, 1, 0)
+            handoff_ref[sub, :, :DK] = (
+                jnp.where(eye, jnp.exp(last), 0.0) - product(tail_keys, wy_keys, 0, 0)
+            ).astype(jnp.bfloat16)
+            handoff_ref[sub, :, DK:] = product(tail_keys, fresh, 0, 0).astype(jnp.bfloat16)
 
     def out(*shape, kind=jnp.float32):
         return jax.ShapeDtypeStruct((local_heads,) + shape, kind)
 
     return pl.pallas_call(
         kernel,
-        grid=(local_heads,),
+        grid=(local_heads // HEADS_A_STEP,),
         in_specs=three(row_count) + three(8) + three(8) + [whole, scalar_spec],
         out_specs=[
             per_head(row_count, row_count),
@@ -248,9 +267,9 @@
             out(DK, DK + DV, kind=jnp.bfloat16),
         ],
         scratch_shapes=[
-            pltpu.VMEM((row_count + 8, DK), jnp.float32),
-            pltpu.VMEM((row_count + 8, DK), jnp.float32),
-            pltpu.VMEM((row_count + 8, DV), jnp.float32),
+            pltpu.VMEM((HEADS_A_STEP, row_count + 8, DK), jnp.float32),
+            pltpu.VMEM((HEADS_A_STEP, row_count + 8, DK), jnp.float32),
+            pltpu.VMEM((HEADS_A_STEP, row_count + 8, DV), jnp.float32),
         ],
         compiler_params=params(),
     )(*([projected] * 3), *([rim] * 3), *([taps] * 3), decay_proj, scalars)
@@ -342,9 +361,14 @@
             block,
             pl.BlockSpec((row_count, DV), lambda h: (0, gate_first + h)),
             pl.BlockSpec((1, DV), lambda h: (0, 0)),
-            per_head(row_count, DK),
+            pl.BlockSpec((1, row_count, DK), lambda h: (h, 0, 0)),
         ],
-        out_specs=[block, block, pl.BlockSpec((8, DV), lambda h: (0, 0)), per_head(DK, DV)],
+        out_specs=[
+            block,
+            block,
+            pl.BlockSpec((8, DV), lambda h: (0, 0)),
+            pl.BlockSpec((1, DK, DV), lambda h: (h, 0, 0)),
+        ],
         out_shape=[
             jax.ShapeDtypeStruct((row_count, width), jnp.float32),
             jax.ShapeDtypeStruct((row_count, width), jnp.bfloat16),
@@ -381,24 +405,26 @@
     )(my_index, base, handoffs, d_enterings)
 
 
-def conv_back(d_pre, extended, taps_ref, padded, d_block_ref, d_tail_ref, d_rim_ref, d_taps_ref):
+def conv_back(
+    d_pre, extended, taps_ref, padded, d_block_ref, d_tail_ref, d_rim_ref, d_taps_ref, columns
+):
     row_count = d_pre.shape[0]
     first = 8 - (KCONV - 1)
     padded[0:8, :] = jnp.zeros((8, d_pre.shape[1]), jnp.float32)
     padded[8 : 8 + row_count, :] = d_pre
     padded[8 + row_count : 16 + row_count, :] = jnp.zeros((8, d_pre.shape[1]), jnp.float32)
     total = None
-    d_taps_ref[...] = jnp.zeros_like(d_taps_ref)
+    d_taps_ref[:, columns] = jnp.zeros((8, d_pre.shape[1]), jnp.float32)
     for tap in range(KCONV):
         start = KCONV - 1 - tap
-        term = taps_ref[tap : tap + 1, :] * padded[start : start + row_count + 8, :]
+        term = taps_ref[tap : tap + 1, columns] * padded[start : start + row_count + 8, :]
         total = term if total is None else total + term
-        d_taps_ref[tap : tap + 1, :] = jnp.sum(
+        d_taps_ref[tap : tap + 1, columns] = jnp.sum(
             d_pre * extended[first + tap : first + tap + row_count, :], axis=0, keepdims=True
         )
-    d_rim_ref[...] = total[0:8, :]
-    d_block_ref[...] = total[8:, :].astype(jnp.bfloat16)
-    d_tail_ref[...] = total[row_count:, :]
+    d_rim_ref[:, columns] = total[0:8, :]
+    d_block_ref[:, columns] = total[8:, :].astype(jnp.bfloat16)
+    d_tail_ref[:, columns] = total[row_count:, :]
 
 
 def mixer_back(
@@ -413,105 +439,107 @@
         solve_ref, fresh_ref, wy_ref, enter_ref, d_out_ref, d_leave_ref,
         dq_ref, dk_ref, dv_ref, tail_q, tail_k, tail_v, rim_q, rim_k, rim_v,
         taps_q, taps_k, taps_v, d_decay_ref, d_scalars_ref,
-        ext_q, ext_k, ext_v, pad_k, pad_v,
+        ext_q, ext_k, ext_v, pad_q, pad_k, pad_v,
     ):
-        head = pl.program_id(0)
-
-        @pl.when(head == 0)
+        @pl.when(pl.program_id(0) == 0)
         def _():
             d_decay_ref[...] = jnp.zeros_like(d_decay_ref)
             d_scalars_ref[...] = jnp.zeros_like(d_scalars_ref)
 
-        pre_q = convolved(ext_q, pq, rq, tq)
-        pre_k = convolved(ext_k, pk, rk, tk)
-        pre_v = convolved(ext_v, pv, rv, tv)
-        conv_q, conv_k = jax.nn.silu(pre_q), jax.nn.silu(pre_k)
-        unit_q, scale_q = unit_rows(conv_q)
-        queries = unit_q * DK ** (-0.5)
-        key_rows, scale_k = unit_rows(conv_k)
-        values = jax.nn.silu(pre_v)
-        decay_in, rate, logs, beta, sums, within, row_ids, column_ids = decay_terms(
-            head, local_heads, decay_ref, scalars_ref
-        )
-        strict = row_ids > column_ids
-        grown = jnp.exp(sums)
-        last = sums[row_count - 1 : row_count, :]
-        tail = jnp.exp(last - sums)
-        tail_keys = tail * key_rows
-        gram = product(key_rows, key_rows, 1, 1)
-        scores = jnp.where(strict, gram * within, 0.0)
-        attention = product(queries, key_rows, 1, 1) * within
-        enter, d_out, d_leave = enter_ref[0], d_out_ref[...], d_leave_ref[0]
-        update = fresh_ref[0] - product(wy_ref[0], enter, 1, 0)
-        d_update = product(attention, d_out, 0, 0) + product(tail_keys, d_leave, 1, 0)
-        d_right = product(solve_ref[0], d_update, 0, 0)
-        d_attention = product(d_out, update, 1, 1) * within
-        d_system = -product(d_right, update, 1, 1)
-        out_state = product(d_out, enter, 1, 1)
-        right_state = product(d_right, enter, 1, 1)
-        leave_update = product(update, d_leave, 1, 1)
-        remainder = values - grown * product(key_rows, enter, 1, 0)
-        d_values = beta * d_right
-        d_beta = jnp.sum(d_right * remainder, axis=1, keepdims=True) + jnp.sum(
-            d_system * scores, axis=1, keepdims=True
-        )
-        pair = beta * (d_system * scores)
-        d_gram = jnp.where(strict, beta * d_system * within, 0.0)
-        d_queries = grown * out_state + product(d_attention, key_rows, 1, 0)
-        d_keys = (
-            product(d_attention, queries, 0, 0)
-            + product(d_gram, key_rows, 1, 0)
-            + product(d_gram, key_rows, 0, 0)
-            + tail * leave_update
-            - (beta * grown) * right_state
-        )
-        both = pair + d_attention * product(queries, key_rows, 1, 1)
-        tail_rows = jnp.sum(tail_keys * leave_update, axis=1, keepdims=True)
-        diagonal = row_ids == column_ids
-        columns = jnp.sum(both, axis=0, keepdims=True)
-        d_sums = (
-            jnp.sum(both, axis=1, keepdims=True)
-            - jnp.sum(jnp.where(diagonal, columns, 0.0), axis=1, keepdims=True)
-            + jnp.sum(out_state * (grown * queries), axis=1, keepdims=True)
-            - jnp.sum(right_state * ((beta * grown) * key_rows), axis=1, keepdims=True)
-            - tail_rows
-        )
-        d_last = jnp.exp(last) * jnp.sum(
-            jnp.sum(d_leave * enter, axis=1, keepdims=True), axis=0, keepdims=True
-        ) + jnp.sum(tail_rows, axis=0, keepdims=True)
-        d_logs = d_last + jnp.sum(
-            jnp.where(row_ids <= column_ids, to_row(d_sums, diagonal), 0.0), axis=1, keepdims=True
-        )
-        d_decay_in = d_logs * rate * jax.nn.sigmoid(decay_in)
-        d_beta_in = d_beta * beta * (1.0 - beta)
-        d_decay_ref[...] = (
-            d_decay_ref[...]
-            + put_lane(d_decay_in, head)
-            + put_lane(d_beta_in, head + local_heads)
-        )
-        d_rate = jnp.sum(d_logs * logs, axis=0, keepdims=True)
-        d_bias = jnp.sum(d_decay_in, axis=0, keepdims=True)
-        d_scalars_ref[0:1, :] = d_scalars_ref[0:1, :] + put_lane(d_rate, head)
-        d_scalars_ref[1:2, :] = d_scalars_ref[1:2, :] + put_lane(d_bias, head)
-
-        def unit_back(d_unit, unit, scale):
-            return scale * (d_unit - unit * jnp.sum(unit * d_unit, axis=1, keepdims=True))
-
-        def silu_back(d_act, pre):
-            logistic = jax.nn.sigmoid(pre)
-            return d_act * logistic * (1.0 + pre * (1.0 - logistic))
-
-        d_pre_q = silu_back(unit_back(d_queries * DK ** (-0.5), unit_q, scale_q), pre_q)
-        conv_back(d_pre_q, ext_q, tq, pad_k, dq_ref, tail_q, rim_q, taps_q)
-        d_pre_k = silu_back(unit_back(d_keys, key_rows, scale_k), pre_k)
-        conv_back(d_pre_k, ext_k, tk, pad_k, dk_ref, tail_k, rim_k, taps_k)
-        conv_back(silu_back(d_values, pre_v), ext_v, tv, pad_v, dv_ref, tail_v, rim_v, taps_v)
+        for sub in range(HEADS_A_STEP):
+            head = pl.program_id(0) * HEADS_A_STEP + sub
+            narrow, wide = head_columns(sub)
+            pre_q = convolved(ext_q.at[sub], pq, rq, tq, narrow)
+            pre_k = convolved(ext_k.at[sub], pk, rk, tk, narrow)
+            pre_v = convolved(ext_v.at[sub], pv, rv, tv, wide)
+            conv_q, conv_k = jax.nn.silu(pre_q), jax.nn.silu(pre_k)
+            unit_q, scale_q = unit_rows(conv_q)
+            queries = unit_q * DK ** (-0.5)
+            key_rows, scale_k = unit_rows(conv_k)
+            values = jax.nn.silu(pre_v)
+            decay_in, rate, logs, beta, sums, within, row_ids, column_ids = decay_terms(
+                head, local_heads, decay_ref, scalars_ref
+            )
+            strict = row_ids > column_ids
+            grown = jnp.exp(sums)
+            last = sums[row_count - 1 : row_count, :]
+            tail = jnp.exp(last - sums)
+            tail_keys = tail * key_rows
+            gram = product(key_rows, key_rows, 1, 1, True)
+            scores = jnp.where(strict, gram * within, 0.0)
+            attention = product(queries, key_rows, 1, 1) * within
+            enter, d_out, d_leave = enter_ref[sub], d_out_ref[:, wide], d_leave_ref[sub]
+            update = fresh_ref[sub] - product(wy_ref[sub], enter, 1, 0)
+            d_update = product(attention, d_out, 0, 0) + product(tail_keys, d_leave, 1, 0)
+            d_right = product(solve_ref[sub], d_update, 0, 0, True)
+            d_attention = product(d_out, update, 1, 1) * within
+            d_system = -product(d_right, update, 1, 1)
+            out_state = product(d_out, enter, 1, 1)
+            right_state = product(d_right, enter, 1, 1)
+            leave_update = product(update, d_leave, 1, 1)
+            remainder = values - grown * product(key_rows, enter, 1, 0)
+            d_values = beta * d_right
+            d_beta = jnp.sum(d_right * remainder, axis=1, keepdims=True) + jnp.sum(
+                d_system * scores, axis=1, keepdims=True
+            )
+            pair = beta * (d_system * scores)
+            d_gram = jnp.where(strict, beta * d_system * within, 0.0)
+            d_queries = grown * out_state + product(d_attention, key_rows, 1, 0)
+            d_keys = (
+                product(d_attention, queries, 0, 0)
+                + product(d_gram, key_rows, 1, 0)
+                + product(d_gram, key_rows, 0, 0)
+                + tail * leave_update
+                - (beta * grown) * right_state
+            )
+            both = pair + d_attention * product(queries, key_rows, 1, 1)
+            tail_rows = jnp.sum(tail_keys * leave_update, axis=1, keepdims=True)
+            diagonal = row_ids == column_ids
+            columns = jnp.sum(both, axis=0, keepdims=True)
+            d_sums = (
+                jnp.sum(both, axis=1, keepdims=True)
+                - jnp.sum(jnp.where(diagonal, columns, 0.0), axis=1, keepdims=True)
+                + jnp.sum(out_state * (grown * queries), axis=1, keepdims=True)
+                - jnp.sum(right_state * ((beta * grown) * key_rows), axis=1, keepdims=True)
+                - tail_rows
+            )
+            d_last = jnp.exp(last) * jnp.sum(
+                jnp.sum(d_leave * enter, axis=1, keepdims=True), axis=0, keepdims=True
+            ) + jnp.sum(tail_rows, axis=0, keepdims=True)
+            d_logs = d_last + jnp.sum(
+                jnp.where(row_ids <= column_ids, to_row(d_sums, diagonal), 0.0), axis=1, keepdims=True
+            )
+            d_decay_in = d_logs * rate * jax.nn.sigmoid(decay_in)
+            d_beta_in = d_beta * beta * (1.0 - beta)
+            d_decay_ref[...] = (
+                d_decay_ref[...]
+                + put_lane(d_decay_in, head)
+                + put_lane(d_beta_in, head + local_heads)
+            )
+            d_rate = jnp.sum(d_logs * logs, axis=0, keepdims=True)
+            d_bias = jnp.sum(d_decay_in, axis=0, keepdims=True)
+            d_scalars_ref[0:1, :] = d_scalars_ref[0:1, :] + put_lane(d_rate, head)
+            d_scalars_ref[1:2, :] = d_scalars_ref[1:2, :] + put_lane(d_bias, head)
+
+            def unit_back(d_unit, unit, scale):
+                return scale * (d_unit - unit * jnp.sum(unit * d_unit, axis=1, keepdims=True))
+
+            def silu_back(d_act, pre):
+                logistic = jax.nn.sigmoid(pre)
+                return d_act * logistic * (1.0 + pre * (1.0 - logistic))
+
+            d_pre_q = silu_back(unit_back(d_queries * DK ** (-0.5), unit_q, scale_q), pre_q)
+            conv_back(d_pre_q, ext_q.at[sub], tq, pad_q.at[sub], dq_ref, tail_q, rim_q, taps_q, narrow)
+            d_pre_k = silu_back(unit_back(d_keys, key_rows, scale_k), pre_k)
+            conv_back(d_pre_k, ext_k.at[sub], tk, pad_k.at[sub], dk_ref, tail_k, rim_k, taps_k, narrow)
+            conv_back(
+                silu_back(d_values, pre_v), ext_v.at[sub], tv, pad_v.at[sub],
+                dv_ref, tail_v, rim_v, taps_v, wide,
+            )
 
     def blocks(rows):
         return [
-            pl.BlockSpec((rows, DK), lambda h: (0, h)),
-            pl.BlockSpec((rows, DK), lambda h: (0, h)),
-            pl.BlockSpec((rows, DV), lambda h: (0, h)),
+            pl.BlockSpec((rows, HEADS_A_STEP * width), lambda h: (0, h)) for width in (DK, DK, DV)
         ]
 
     def shapes(rows, kind):
@@ -521,7 +549,7 @@
 
     outs = pl.pallas_call(
         kernel,
-        grid=(local_heads,),
+        grid=(local_heads // HEADS_A_STEP,),
         in_specs=three(row_count)
         + three(8)
         + three(8)
@@ -532,7 +560,7 @@
             per_head(row_count, DV),
             per_head(row_count, DK),
             per_head(DK, DV),
-            pl.BlockSpec((row_count, DV), lambda h: (0, h)),
+            pl.BlockSpec((row_count, HEADS_A_STEP * DV), lambda h: (0, h)),
             per_head(DK, DV),
         ],
         out_specs=blocks(row_count) + blocks(8) * 3 + [whole, scalar_spec],
@@ -543,11 +571,12 @@
             jax.ShapeDtypeStruct((8, 128), jnp.float32),
         ],
         scratch_shapes=[
-            pltpu.VMEM((row_count + 8, DK), jnp.float32),
-            pltpu.VMEM((row_count + 8, DK), jnp.float32),
-            pltpu.VMEM((row_count + 8, DV), jnp.float32),
-            pltpu.VMEM((row_count + 16, DK), jnp.float32),
-            pltpu.VMEM((row_count + 16, DV), jnp.float32),
+            pltpu.VMEM((HEADS_A_STEP, row_count + 8, DK), jnp.float32),
+            pltpu.VMEM((HEADS_A_STEP, row_count + 8, DK), jnp.float32),
+            pltpu.VMEM((HEADS_A_STEP, row_count + 8, DV), jnp.float32),
+            pltpu.VMEM((HEADS_A_STEP, row_count + 16, DK), jnp.float32),
+            pltpu.VMEM((HEADS_A_STEP, row_count + 16, DK), jnp.float32),
+            pltpu.VMEM((HEADS_A_STEP, row_count + 16, DV), jnp.float32),
         ],
         compiler_params=params(),
     )(
@@ -563,8 +592,9 @@
 TILE = 16
 CAPACITY_UNIT = 44
 FIRST_GATHER = 24
-FIRST_REDUCE = 20
+FIRST_REDUCE = 16
 SECOND_REDUCE = 24
+SECOND_GATHER = 16
 TABLE = 1 << 16
 VMEM_LIMIT = 48 * 1024 * 1024
 
@@ -942,27 +972,35 @@
 
 
 def optimizer_update(
-    sources, slot_sources, slot_rows, slot_kinds, kinds_used, slot_masks, small_rates, master, moment_one, moment_two
+    sources, slot_sources, slot_rows, slot_kinds, kinds_used, slot_masks, small_rates,
+    master, moment_one, moment_two, first_block, earlier,
 ):
     capacity, piece_size = master.shape
     chunks = piece_size // CHUNK
     rows = CHUNK // LANES
     slot_blocks = pl.cdiv(capacity, 8)
-
     steps = slot_blocks * chunks
 
-    def kernel(kinds_ref, sources_ref, rows_ref, *refs):
+    def steps_here(first):
+        return (first if earlier else slot_blocks - first) * chunks
+
+    def place(step, first):
+        now = jnp.minimum(step, jnp.maximum(steps_here(first) - 1, 0))
+        block, chunk = now // chunks, lax.rem(now, chunks)
+        return (block if earlier else slot_blocks - 1 - block), chunk
+
+    def kernel(first_ref, kinds_ref, sources_ref, rows_ref, *refs):
         source_refs, refs = refs[: len(sources)], refs[len(sources) :]
-        (
-            masks_ref, small_ref, master_ref, one_ref, two_ref,
-            grad_out, master_out, one_out, two_out, low_out, scratch, buffer, sem,
-        ) = refs
-        first = pl.program_id(0) * 8
-        step = pl.program_id(0) * chunks + pl.program_id(1)
+        masks_ref, small_ref, master_ref, one_ref, two_ref = refs[:5]
+        refs = refs[5 + len(earlier) :]
+        grad_out, master_out, one_out, two_out, low_out, scratch, buffer, sem = refs
+        step = pl.program_id(0)
+        count = jnp.maximum(steps_here(first_ref[0]), 1)
+        first = place(step, first_ref[0])[0] * 8
         slot = lax.rem(step, 2)
 
         def start(step, which):
-            block, chunk = step // chunks, lax.rem(step, chunks)
+            block, chunk = place(step, first_ref[0])
             for s in range(8):
                 for i, source_ref in enumerate(source_refs):
 
@@ -977,63 +1015,75 @@
                             sem.at[which],
                         ).start()
 
+                @pl.when(sources_ref[block * 8 + s] >= len(sources))
+                def _():
+                    pltpu.make_async_copy(
+                        source_refs[0].at[0, pl.ds(0, rows)], buffer.at[which, s], sem.at[which]
+                    ).start()
+
         @pl.when(step == 0)
         def _():
             start(0, 0)
 
-        @pl.when(step + 1 < steps)
+        @pl.when(step + 1 < count)
         def _():
             start(step + 1, 1 - slot)
 
-        pltpu.make_async_copy(buffer.at[slot], buffer.at[slot], sem.at[slot]).wait()
-        for s in range(8):
-            kind_now = kinds_ref[first + s]
-            for kind in kinds_used:
-
-                @pl.when(kind_now == kind)
-                def _():
-                    for tile in range(rows // TILE):
-                        row_tile, column = divmod(tile, kind)
-                        start = (row_tile * TILE * kind + column) * 8 + s
-                        scratch[pl.ds(start, TILE, stride=8 * kind), :] = buffer[
-                            slot, s, TILE * tile : TILE * tile + TILE, :
-                        ].astype(jnp.float32)
-        present = masks_ref[0] > 0.5
-        is_small = masks_ref[1] > 0.5
-        rate_rows = masks_ref[2]
-        for j in range(rows):
-            lanes = slice(LANES * j, LANES * j + LANES)
-            grad = jnp.where(present, scratch[8 * j : 8 * j + 8, :], 0.0)
-            rate = jnp.where(is_small, small_ref[:, lanes], rate_rows)
-            master_now = master_ref[:, lanes]
-            one_new = BETA_ONE * one_ref[:, lanes] + (1.0 - BETA_ONE) * grad
-            two_new = BETA_TWO * two_ref[:, lanes] + (1.0 - BETA_TWO) * grad * grad
-            first_hat = one_new / (1.0 - BETA_ONE**STEP)
-            second_hat = two_new / (1.0 - BETA_TWO**STEP)
-            master_new = master_now - rate * (
-                first_hat / (jnp.sqrt(second_hat) + ADAM_EPSILON) + WEIGHT_DECAY * master_now
-            )
-            grad_out[:, lanes] = grad
-            master_out[:, lanes] = master_new
-            one_out[:, lanes] = one_new
-            two_out[:, lanes] = two_new
-            low_out[:, lanes] = master_new.astype(jnp.bfloat16)
-
-    state_spec = pl.BlockSpec((8, CHUNK), lambda i, j, *tables: (i, j))
+        @pl.when(step < count)
+        def _():
+            pltpu.make_async_copy(buffer.at[slot], buffer.at[slot], sem.at[slot]).wait()
+            for s in range(8):
+                kind_now = kinds_ref[first + s]
+                for kind in kinds_used:
+
+                    @pl.when(kind_now == kind)
+                    def _():
+                        for tile in range(rows // TILE):
+                            row_tile, column = divmod(tile, kind)
+                            start_row = (row_tile * TILE * kind + column) * 8 + s
+                            scratch[pl.ds(start_row, TILE, stride=8 * kind), :] = buffer[
+                                slot, s, TILE * tile : TILE * tile + TILE, :
+                            ].astype(jnp.float32)
+
+            present = masks_ref[0] > 0.5
+            is_small = masks_ref[1] > 0.5
+            rate_rows = masks_ref[2]
+            for j in range(rows):
+                lanes = slice(LANES * j, LANES * j + LANES)
+                grad = jnp.where(present, scratch[8 * j : 8 * j + 8, :], 0.0)
+                rate = jnp.where(is_small, small_ref[:, lanes], rate_rows)
+                master_now = master_ref[:, lanes]
+                one_new = BETA_ONE * one_ref[:, lanes] + (1.0 - BETA_ONE) * grad
+                two_new = BETA_TWO * two_ref[:, lanes] + (1.0 - BETA_TWO) * grad * grad
+                first_hat = one_new / (1.0 - BETA_ONE**STEP)
+                second_hat = two_new / (1.0 - BETA_TWO**STEP)
+                master_new = master_now - rate * (
+                    first_hat / (jnp.sqrt(second_hat) + ADAM_EPSILON) + WEIGHT_DECAY * master_now
+                )
+                grad_out[:, lanes] = grad
+                master_out[:, lanes] = master_new
+                one_out[:, lanes] = one_new
+                two_out[:, lanes] = two_new
+                low_out[:, lanes] = master_new.astype(jnp.bfloat16)
+
+    state_spec = pl.BlockSpec((8, CHUNK), lambda t, first, *tables: place(t, first[0]))
+    anywhere = pl.BlockSpec(memory_space=pl.ANY)
     wide = jax.ShapeDtypeStruct((capacity, piece_size), jnp.float32)
+    operands = [*sources, slot_masks, small_rates, master, moment_one, moment_two, *earlier]
     return pl.pallas_call(
         kernel,
         grid_spec=pltpu.PrefetchScalarGridSpec(
-            num_scalar_prefetch=3,
-            grid=(slot_blocks, chunks),
-            in_specs=[pl.BlockSpec(memory_space=pl.ANY) for source in sources]
+            num_scalar_prefetch=4,
+            grid=(steps,),
+            in_specs=[anywhere for source in sources]
             + [
-                pl.BlockSpec((3, 8, LANES), lambda i, j, *tables: (0, i, 0)),
-                pl.BlockSpec((1, CHUNK), lambda i, j, *tables: (0, j)),
+                pl.BlockSpec((3, 8, LANES), lambda t, first, *tables: (0, place(t, first[0])[0], 0)),
+                pl.BlockSpec((1, CHUNK), lambda t, first, *tables: (0, place(t, first[0])[1])),
                 state_spec,
                 state_spec,
                 state_spec,
-            ],
+            ]
+            + [anywhere for array in earlier],
             out_specs=[state_spec] * 5,
             scratch_shapes=[
                 pltpu.VMEM((8 * rows, LANES), jnp.float32),
@@ -1042,11 +1092,16 @@
             ],
         ),
         out_shape=[wide] * 4 + [jax.ShapeDtypeStruct((capacity, piece_size), jnp.bfloat16)],
-        compiler_params=params(),
-    )(
-        slot_kinds, slot_sources, slot_rows, *sources,
-        slot_masks, small_rates, master, moment_one, moment_two,
-    )
+        input_output_aliases={
+            4 + len(operands) - len(earlier) + i: i for i in range(len(earlier))
+        },
+        cost_estimate=pl.CostEstimate(
+            flops=20 * master.size,
+            bytes_accessed=16 * master.size,
+            transcendentals=2 * master.size,
+        ),
+        compiler_params=pltpu.CompilerParams(vmem_limit_bytes=24 * 1024 * 1024),
+    )(first_block, slot_kinds, slot_sources, slot_rows, *operands)
 
 
 def weight_grad(left, right):
@@ -1079,6 +1134,18 @@
         part = lax.dynamic_slice_in_dim(rest, trip * rows, rows)
         part = lax.psum_scatter(part, "seq", scatter_dimension=0, tiled=True)
         return lax.dynamic_update_slice_in_dim(table, part, trip * extra_step, axis=0)
+
+    return lax.fori_loop(0, trips, more, room)
+
+
+def bring_spilled(reduced, first, trips, most, step):
+    devices = lax.axis_size("seq")
+    room = reserve((most * step,) + reduced.shape[1:], reduced.dtype)
+
+    def more(trip, table):
+        part = lax.dynamic_slice_in_dim(reduced, first + trip * step, step)
+        part = lax.ppermute(part, "seq", [(i, i ^ 1) for i in range(devices)])
+        return lax.dynamic_update_slice_in_dim(table, part, trip * step, axis=0)
 
     return lax.fori_loop(0, trips, more, room)
 
@@ -1108,38 +1175,70 @@
     padded = capacity + -capacity % 8
     small_rank = ranks[big_count]
     big_owners, big_ranks = owners[:big_count], ranks[:big_count]
-    is_mixer = np.arange(big_count) < mixer_count
-    held_there = jnp.sum(onehot[:big_count] * mixer_held[None, :], axis=1)
 
     def rest_row(over, owner):
         return over // extra_step * (seq_parts * extra_step) + owner * extra_step + over % extra_step
 
     early = -(-capacity * FIRST_GATHER // (8 * CAPACITY_UNIT)) * 8
     late = capacity - early
-    extra_step = min(4, late)
+    late_room = min(late, -(-capacity * SECOND_GATHER // CAPACITY_UNIT))
+    extra_step = 2 if late % 2 == 0 else 1
     most_gather = -(-late // extra_step)
     trips_gather = jnp.maximum(-(-(jnp.max(mixer_held) - early) // extra_step), 0)
     early_row = big_owners * early + big_ranks
     mixer_fetch = jnp.where(
         big_ranks < early, early_row, TABLE + rest_row(big_ranks - early, big_owners)
     )
+    neighbours = np.arange(seq_parts) ^ 1
+    late_held = jnp.maximum(mixer_held + mlp_held - early, 0)
+    late_spare = jnp.maximum(late_room - late_held[neighbours], 0)
+    late_over = jnp.maximum(late_held - late_room, 0)
+    trips_late = -(-jnp.max(jnp.maximum(late_over - late_spare, 0)) // extra_step)
+    spare_there = jnp.sum(onehot[:big_count] * late_spare[None, :], axis=1)
+    past = big_ranks - early - late_room
+    rest_trip = (past - spare_there) // extra_step
+    rest_start = late_room + spare_there + rest_trip * extra_step
+    rest_start = jnp.minimum(rest_start, late - extra_step)
     mlp_fetch = jnp.where(
-        big_ranks < early, TABLE + early_row, big_owners * late + big_ranks - early
+        big_ranks < early,
+        TABLE + early_row,
+        jnp.where(
+            past < 0,
+            big_owners * late_room + big_ranks - early,
+            jnp.where(
+                past < spare_there,
+                (big_owners ^ 1) * late_room + late_room - spare_there + past,
+                2 * TABLE
+                + rest_trip * (seq_parts * extra_step)
+                + big_owners * extra_step
+                + big_ranks - early - rest_start,
+            ),
+        ),
     )
     first_room = -(-capacity * FIRST_REDUCE // CAPACITY_UNIT)
     second_room = -(-capacity * SECOND_REDUCE // CAPACITY_UNIT)
     most_reduce = -(-(capacity - second_room) // extra_step)
     second_held = mixer_held + jnp.maximum(mlp_held - first_room, 0)
-    trips_reduce = jnp.maximum(-(-(jnp.max(second_held) - second_room) // extra_step), 0)
-    mlp_ranks = big_ranks - held_there
-    second_index = jnp.where(is_mixer, big_ranks, big_ranks - first_room)
+    second_there = jnp.sum(onehot[:big_count] * second_held[None, :], axis=1)
+    room_there = jnp.maximum(second_room - second_held[neighbours], 0)
+    over_held = jnp.maximum(second_held - second_room, 0)
+    spill_step = min(4, second_room)
+    most_spill = -(-min(second_room, capacity - second_room) // spill_step)
+    trips_spill = -(-jnp.max(jnp.minimum(over_held, room_there)) // spill_step)
+    trips_reduce = -(-jnp.max(jnp.maximum(over_held - room_there, 0)) // extra_step)
+    second_over = big_ranks - second_room
+    spare = jnp.sum(onehot[:big_count] * room_there[None, :], axis=1)
     store = jnp.where(
-        ~is_mixer & (mlp_ranks < first_room),
-        big_owners * first_room + mlp_ranks,
+        big_ranks >= second_there,
+        big_owners * first_room + big_ranks - second_there,
         jnp.where(
-            second_index < second_room,
-            TABLE + big_owners * second_room + second_index,
-            2 * TABLE + rest_row(second_index - second_room, big_owners),
+            second_over < 0,
+            TABLE + big_owners * second_room + big_ranks,
+            jnp.where(
+                second_over < spare,
+                TABLE + (big_owners ^ 1) * second_room + (second_room - spare) + second_over,
+                2 * TABLE + rest_row(second_over - spare, big_owners),
+            ),
         ),
     )
     small_owner = owners[big_count]
@@ -1147,6 +1246,7 @@
     def spots(table, name):
         return table[firsts[name] : firsts[name] + counts[name]]
 
+    my_spare_here = room_there[my_index ^ 1]
     my_mixer = mixer_held[my_index]
     my_mlp = mlp_held[my_index]
     my_count = my_mixer + my_mlp
@@ -1182,16 +1282,24 @@
     rows_of_piece = piece_size // LANES
     small_width = small_rows * LANES
     small_part = jnp.concatenate([my_small, gains], axis=1).reshape(-1, LANES)
-    small_table = lax.all_gather(small_part, "seq", axis=0, tiled=False)
+    small_table, small_base = gather_states(small_part)
     input_blocks = exchange([inputs] * head_parts, "head")
     early_part = pack_blocks(master, slot_kinds, kinds_used, 0, early)
     early_table = lax.all_gather(early_part, "seq", axis=0, tiled=True)
     late_part = pack_blocks(master, slot_kinds, kinds_used, early, late)
+    late_send = late_part[:late_room]
+    if late_room < late:
+        guests = lax.ppermute(
+            late_part[late_room:], "seq", [(i, i ^ 1) for i in range(seq_parts)]
+        )
+        late_send = lax.dynamic_update_slice_in_dim(
+            late_part, guests, late_held[my_index], axis=0
+        )[:late_room]
     back_blocks = exchange([cotangent] * head_parts, "head")
     rows_full = in_order(input_blocks, my_head, 1)
     back_full = in_order(back_blocks, my_head, 1)
     small_flat = lax.dynamic_index_in_dim(
-        small_table, small_owner, axis=0, keepdims=False
+        small_table, small_owner ^ small_base[0], axis=0, keepdims=False
     ).reshape(-1)
     by_name, small_used = unpack(small_flat, segments_list[8:])
     gains = small_flat[small_width:].astype(jnp.float32)[None, :]
@@ -1213,16 +1321,16 @@
     )
 
     beside = (
-        trips_gather, late_part, normed, scale_one, decay_proj, decay_weight, taps, scalars,
+        trips_gather, late_part, late_send, normed, scale_one, decay_proj, decay_weight, taps, scalars,
         back_full, mixer_fetch, mlp_fetch, store, gain_two, norm_row,
     )
     early_table, beside = lax.optimization_barrier((early_table, beside))
     (
-        trips_now, late_part, normed, scale_one, decay_proj, decay_weight, taps, scalars,
+        trips_now, late_part, late_send, normed, scale_one, decay_proj, decay_weight, taps, scalars,
         back_full, mixer_fetch, mlp_fetch, store, gain_two, norm_row,
     ) = beside
     mixer_rest = gather_rest(late_part, 0, trips_now, most_gather, extra_step)
-    late_table = lax.all_gather(late_part, "seq", axis=0, tiled=True)
+    late_table = lax.all_gather(late_send, "seq", axis=0, tiled=True)
 
     mixer_names = ("wq", "wk", "wv", "wg")
     mixer_weights, projected = assemble(
@@ -1247,23 +1355,28 @@
     mixed_parts = exchange(
         spread_products(my_head_row, head_parts, [(gated_low, out_weights, False)]), "head"
     )
-    (down_weights,) = assemble(
-        [late_table, early_table], [(spots(mlp_fetch, "wdown"), columns["wdown"])], 352
-    )
-    (mlp_weights,) = assemble(
-        [late_table, early_table],
-        [(spots(mlp_fetch, name), columns[name]) for name in ("wgate", "wup")],
-        512,
-    )
-    mixed_parts, down_weights, mlp_weights = lax.optimization_barrier(
-        (mixed_parts, down_weights, mlp_weights)
-    )
     mixed = total_of(mixed_parts)
     inputs_wide = inputs.astype(jnp.float32)
     residual = inputs_wide + mixed
     resid_low = residual.astype(jnp.bfloat16)
 
     resid_blocks = exchange([resid_low] * head_parts, "head")
+    trips_now, late_table = lax.optimization_barrier((trips_late, late_table))
+    late_rest = gather_rest(
+        late_part, late_room + late_spare[my_index], trips_now, most_gather, extra_step
+    )
+    mlp_tables = [late_table, early_table, late_rest]
+    (down_weights,) = assemble(
+        mlp_tables, [(spots(mlp_fetch, "wdown"), columns["wdown"])], 352
+    )
+    (mlp_weights,) = assemble(
+        mlp_tables,
+        [(spots(mlp_fetch, name), columns[name]) for name in ("wgate", "wup")],
+        512,
+    )
+    resid_blocks, down_weights, mlp_weights = lax.optimization_barrier(
+        (resid_blocks, down_weights, mlp_weights)
+    )
     resid_full = in_order(resid_blocks, my_head, 1).astype(jnp.float32)
     scale_two = lax.rsqrt(jnp.mean(resid_full * resid_full, axis=-1, keepdims=True) + NORM_EPSILON)
     hidden_in = (resid_full * scale_two * gain_two).astype(jnp.bfloat16)
@@ -1418,29 +1531,54 @@
         (trips_reduce, second_reduced, grad_tables[1])
     )
     rest_reduced = reduce_rest(rest_grads, trips_now, most_reduce, extra_step)
-    my_first = slot_ids - my_mixer
-    in_first = (my_first >= 0) & (my_first < first_room)
-    my_second = jnp.where(my_first >= 0, slot_ids - first_room, slot_ids)
-    slot_sources = jnp.where(in_first, 0, jnp.where(my_second < second_room, 1, 2))
+    spilled = bring_spilled(
+        second_reduced, second_room - my_spare_here, trips_spill, most_spill, spill_step
+    )
+    my_held = second_held[my_index]
+    in_first = slot_ids >= my_held
+    my_over = slot_ids - second_room
+    my_spare = room_there[my_index]
+    spill_trip = my_over // spill_step
+    there = second_room - my_spare + spill_trip * spill_step
+    spill_shift = there - jnp.minimum(there, second_room - spill_step)
+    slot_sources = jnp.where(
+        in_first, 0, jnp.where(my_over < 0, 2, jnp.where(my_over < my_spare, 3, 4))
+    )
     slot_rows = jnp.where(
-        in_first, my_first, jnp.where(my_second < second_room, my_second, my_second - second_room)
-    )
-    slot_sources = jnp.where(present > 0, jnp.where(is_small > 0, 3, slot_sources), 0)
+        in_first,
+        slot_ids - my_held,
+        jnp.where(
+            my_over < 0,
+            slot_ids,
+            jnp.where(my_over < my_spare, my_over + spill_shift, my_over - my_spare),
+        ),
+    )
+    slot_sources = jnp.where(present > 0, jnp.where(is_small > 0, 1, slot_sources), 0)
     slot_rows = jnp.where(is_small > 0, 0, slot_rows)
     slot_rows = jnp.where(present > 0, slot_rows, 0)
     slot_masks = jnp.stack([present.astype(jnp.float32), is_small.astype(jnp.float32), slot_rates])
     slot_masks = jnp.broadcast_to(slot_masks[:, :, None], slot_masks.shape + (LANES,))
-    grad_slots, master_new, moment_new, second_new, weights_low = optimizer_update(
-        [first_reduced, second_reduced, rest_reduced, small_block],
-        slot_sources,
-        slot_rows,
-        slot_kinds,
-        kinds_used,
-        slot_masks,
-        jnp.asarray(small_rates)[None, :],
-        master,
-        moment_one,
-        moment_two,
+    first_block = jnp.minimum((my_held + 7) // 8, padded // 8).astype(jnp.int32).reshape(1)
+
+    def update(sources, earlier):
+        return optimizer_update(
+            sources,
+            slot_sources,
+            slot_rows,
+            slot_kinds,
+            kinds_used,
+            slot_masks,
+            jnp.asarray(small_rates)[None, :],
+            master,
+            moment_one,
+            moment_two,
+            first_block,
+            earlier,
+        )
+
+    partly = update([first_reduced, small_block], [])
+    grad_slots, master_new, moment_new, second_new, weights_low = update(
+        [first_reduced, small_block, second_reduced, spilled, rest_reduced], partly
     )
     return (
         block_out,

time: 721 us -> 674 us (0.935)
  waiting for transfers between devices: 330 us -> 273 us
  Pallas kernels: 223 us -> 182 us
  local copies, waits for them, and re-layouts: 21.6 us -> 61.1 us
  blocking collectives: 12 us -> 0 us
  starting transfers between devices: 71.6 us -> 82.6 us
    reduce_scatter x1, waiting for transfers between devices: 80.8 us -> 47.8 us  [on_device(): lax.psum_scatter(second_table, 'seq', scatter_dimension=0, tiled=True)]
    pallas_call x2, Pallas kernels: 62.9 us -> 30.1 us  [the longest x1 18.9 us: mixer_local(): pl.pallas_call(kernel, grid=(local_heads // HEADS_A_STEP,), in_specs=thre...]
    unnamed x186 -> x253, local copies, waits for them, and re-layouts: 8.54 us -> 36.4 us
    all_gather x1, waiting for transfers between devices: 66.1 us -> 50.8 us  [on_device(): early_table = lax.all_gather(early_part, 'seq', axis=0, tiled=True)]
    all_gather x1, waiting for transfers between devices: 12.8 us -> 0.01 us  [on_device(): late_table = lax.all_gather(late_send, 'seq', axis=0, tiled=True)]
    all_gather x1 -> x0, blocking collectives: 12 us -> none  [on_device(): small_table = lax.all_gather(small_part, 'seq', axis=0, tiled=False)]
    reduce_scatter x1, waiting for transfers between devices: 13.3 us -> 3.95 us  [on_device(): lax.psum_scatter(grad_tables[0], 'seq', scatter_dimension=0, tiled=True)]
    ppermute x14 -> x21, waiting for transfers between devices: 46.5 us -> 52.3 us  [moved(): return lax.ppermute(array, 'seq', [(i, i ^ mask) for i in range(devices)])]
  transfers between devices with their start and end apart: 56 -> 65, of which waited for: 28 -> 33; matrix products, arithmetic and copies ran while one was open for 3% -> 7% of each run, Pallas kernels for 23% -> 20%
where the time goes in v3:
time: 674 us; the launch traced here: 664 us
  waiting for transfers between devices  273 us (41%)
  Pallas kernels  182 us (27%)
  starting transfers between devices  82.6 us (12%)
  local copies, waits for them, and re-layouts  61.1 us (9%)
  between operations  27.9 us (4%)
  other arithmetic  25.5 us (4%)
  matrix products  12 us (2%)
    ppermute x33, waiting for transfers between devices, exchange(): lax.ppermute(blocks[m], axis, [(i, i ^ m) for i in range(devices)])  102 us
    ppermute x33, starting transfers between devices, exchange(): lax.ppermute(blocks[m], axis, [(i, i ^ m) for i in range(devices)])  61 us
    ppermute x21, waiting for transfers between devices, moved(): return lax.ppermute(array, 'seq', [(i, i ^ mask) for i in range(devices)])  52.3 us
    all_gather x1, waiting for transfers between devices, on_device(): early_table = lax.all_gather(early_part, 'seq', axis=0, tiled=True)  50.8 us
    reduce_scatter x1, waiting for transfers between devices, on_device(): lax.psum_scatter(second_table, 'seq', scatter_dimension=0, tiled=True)  47.8 us
    pallas_call x2, Pallas kernels, optimizer_update(): pl.pallas_call(kernel, grid_spec=pltpu.PrefetchScalarGridSpec(num_scalar_...  38.8 us
    unnamed x253, local copies, waits for them, and re-layouts  36.4 us
    pallas_call x8, Pallas kernels, weight_grad_blocks(): pl.pallas_call(kernel, grid_spec=pltpu.PrefetchScalarGridSpec(num_scalar_...  32.5 us
  transfers between devices with their start and end apart: 65, of which 33 were waited for; matrix products, arithmetic and copies ran while one was open for 7% of the time, Pallas kernels for 20%

profile of v3, /device:TPU:0, one launch (start us, length us, event | category | flops | bytes accessed | tf_op | source)
XLA Modules:
  0.0 664.0 jit_solution(14181392623073887044)
XLA Ops:
  11.9 8.9 %shard_map.171 = bf16[24,512,128]{2,1,0:T(8,128)(2,1)} custom-call(s32[48]{0:T(128)S(1)} %broadcast_add_fusion.1.kinds_ref, f32[44,65536]{1,0:T(8,128)} %refs_7_.1), custom_call_target="tpu_custom_call" | custom-call | tf_op jit(solution)/shard_map/pallas_call | solution.py:644
  24.7 3.0 collective-permute-start.5
  27.7 2.6 collective-permute-start.6
  36.2 7.4 %shard_map.172 = bf16[20,512,128]{2,1,0:T(8,128)(2,1)S(1)} custom-call(s32[48]{0:T(128)S(1)} %broadcast_add_fusion.1.kinds_ref, f32[44,65536]{1,0:T(8,128)} %refs_7_.1), custom_call_target="tpu_custom_call" | custom-call | tf_op jit(solution)/shard_map/pallas_call | solution.py:644
  48.5 3.4 collective-permute-start.3
  55.5 3.3 collective-permute-done.9
  61.8 4.0 collective-permute-done.13
  69.1 3.2 collective-permute-start.17
  73.5 6.3 collective-permute-done.15
  79.8 13.0 %collective-permute-done.16 = bf16[256,512]{1,0:T(8,128)(2,1)} collective-permute-done((bf16[256,512]{1,0:T(8,128)(2,1)}, bf16[256,512]{1,0:T(8,128)(2,1)}, u32[]{:S(2)}, u32[]{:S(2)}) %collective-permute-start.16) | collective-permute-done | bytes 262176 | tf_op jit(solution)/shard_map/ppermute | solution.py:838
  100.6 50.8 %all-gather.5.cloned.1.call-done.refs_1_.refs_0_ = bf16[192,512,128]{2,1,0:T(8,128)(2,1)} async-done(((bf16[24,512,128]{2,1,0:T(8,128)(2,1)}), bf16[192,512,128]{2,1,0:T(8,128)(2,1)}) %all-gather.5.cloned.1.call-update) | async-done | bytes 25165840 | tf_op jit(solution)/shard_map/all_gather | solution.py:1288
  155.5 12.9 %shard_map.174 = (bf16[2048,3072]{1,0:T(8,128)(2,1)}, f32[256,3072]{1,0:T(8,128)S(1)}) custom-call(s32[96]{0:T(128)S(1)} %reshape.276.order_ref, bf16[256,2048]{1,0:T(8,128)(2,1)S(1)} %copy-done.14, bf16[192,512,128]{2,1,0:T(8,128)(2,1)} %all-gather.5.cloned.1.call-done.refs_1_.refs_0_, bf16[160,512,128]{2,1,0:T(8,128)(2,1)} %get-tuple-element.221.refs_2_.refs_1_), custom_call_target="tpu_custom_call" | custom-call | flops 3221225472 | bytes 25165824 | tf_op jit(solution)/shard_map/pallas_call | solution.py:772
  173.2 18.9 %shard_map.175 = (f32[4,256,256]{2,1,0:T(8,128)S(1)}, f32[4,256,256]{2,1,0:T(8,128)S(1)}, f32[4,256,128]{2,1,0:T(8,128)S(1)}, f32[4,256,128]{2,1,0:T(8,128)S(1)}...) custom-call(f32[256,3072]{1,0:T(8,128)} %copy-done.2, f32[256,3072]{1,0:T(8,128)} %copy-done.2, ...), custom_call_target="tpu_custom_call" | custom-call | tf_op jit(solution)/shard_map/pallas_call | solution.py:249
  198.2 3.8 shard_map.177.refs_1_
  203.4 11.6 %collective-permute-done.20 = bf16[4,128,384]{2,1,0:T(8,128)(2,1)} collective-permute-done((bf16[4,128,384]{2,1,0:T(8,128)(2,1)}, bf16[4,128,384]{2,1,0:T(8,128)(2,1)}, u32[]{:S(2)}, u32[]{:S(2)}) %collective-permute-start.20) | collective-permute-done | bytes 393248 | tf_op jit(solution)/shard_map/ppermute | solution.py:871
  215.0 2.5 collective-permute-done.22
  217.5 14.6 %collective-permute-done.24 = bf16[4,128,384]{2,1,0:T(8,128)(2,1)} collective-permute-done((bf16[4,128,384]{2,1,0:T(8,128)(2,1)}, bf16[4,128,384]{2,1,0:T(8,128)(2,1)}, u32[]{:S(2)}, u32[]{:S(2)}) %collective-permute-start.24) | collective-permute-done | bytes 393248 | tf_op jit(solution)/shard_map/ppermute | solution.py:871
  238.4 2.8 shard_map.176
  249.0 9.9 %collective-permute-done.26 = bf16[256,512]{1,0:T(8,128)(2,1)S(1)} collective-permute-done((bf16[256,512]{1,0:T(8,128)(2,1)S(1)}, bf16[256,512]{1,0:T(8,128)(2,1)S(1)}, u32[]{:S(2)}, u32[]{:S(2)}) %collective-permute-start.26) | collective-permute-done | bytes 262176 | tf_op jit(solution)/shard_map/ppermute | solution.py:838
  258.9 8.6 %collective-permute-done.27 = bf16[256,512]{1,0:T(8,128)(2,1)S(1)} collective-permute-done((bf16[256,512]{1,0:T(8,128)(2,1)S(1)}, bf16[256,512]{1,0:T(8,128)(2,1)S(1)}, u32[]{:S(2)}, u32[]{:S(2)}) %collective-permute-start.27) | collective-permute-done | bytes 262176 | tf_op jit(solution)/shard_map/ppermute | solution.py:838
  267.7 5.9 collective-permute-start.29
  276.5 10.6 %shard_map.181.refs_1_ = bf16[2048,2816]{1,0:T(8,128)(2,1)} custom-call(s32[88]{0:T(128)S(1)} %reshape.279.order_ref, bf16[128,512,128]{2,1,0:T(8,128)(2,1)} %all-gather.7.cloned.1.call-done.refs_0_, bf16[192,512,128]{2,1,0:T(8,128)(2,1)} %all-gather.5.cloned.1.call-done.refs_1_.refs_0_, bf16[160,512,128]{2,1,0:T(8,128)(2,1)} %get-tuple-element.239.refs_2_), custom_call_target="tpu_custom_call" | custom-call | bytes 23068672 | tf_op jit(solution)/shard_map/pallas_call | solution.py:772
  287.1 4.4 shard_map.180.refs_1_
  291.5 3.4 collective-permute-done.30
  297.5 6.5 fusion.22
  304.1 3.4 multiply_convert_fusion.1
  311.6 4.4 shard_map.186
  316.1 4.9 shard_map.187
  321.0 5.0 shard_map.188
  327.7 7.5 %shard_map.189 = (bf16[256,512]{1,0:T(8,128)(2,1)S(1)}, bf16[256,512]{1,0:T(8,128)(2,1)S(1)}, bf16[256,512]{1,0:T(8,128)(2,1)S(1)}, bf16[256,512]{1,0:T(8,128)(2,1)S(1)}) custom-call(s32[1]{0:T(128)} %bitcast.part_ref, bf16[256,2816]{1,0:T(8,128)(2,1)S(1)} %pad_maximum_fusion.1.right_ref.refs_0_, bf16[2048,2816]{1,0:T(8,128)(2,1)} %shard_map.181.refs_1_), custom_call_target="tpu_custom_call" | custom-call | flops 2952790016 | bytes 11534336 | tf_op jit(solution)/shard_map/pallas_call | solution.py:821
  335.2 4.8 collective-permute-start.35
  343.0 6.1 collective-permute-done.35
  349.1 12.2 %collective-permute-done.36 = bf16[256,512]{1,0:T(8,128)(2,1)S(1)} collective-permute-done((bf16[256,512]{1,0:T(8,128)(2,1)S(1)}, bf16[256,512]{1,0:T(8,128)(2,1)S(1)}, u32[]{:S(2)}, u32[]{:S(2)}) %collective-permute-start.36) | collective-permute-done | bytes 262176 | tf_op jit(solution)/shard_map/ppermute | solution.py:838
  362.2 3.6 collective-permute-start.38
  374.5 6.2 collective-permute-done.41
  380.7 10.0 %collective-permute-done.42 = bf16[256,512]{1,0:T(8,128)(2,1)S(1)} collective-permute-done((bf16[256,512]{1,0:T(8,128)(2,1)S(1)}, bf16[256,512]{1,0:T(8,128)(2,1)S(1)}, u32[]{:S(2)}, u32[]{:S(2)}) %collective-permute-start.42) | collective-permute-done | bytes 262176 | tf_op jit(solution)/shard_map/ppermute | solution.py:838
  395.7 3.7 shard_map.190
  400.2 2.6 collective-permute-start.47
  403.0 4.0 shard_map.194
  407.0 3.9 shard_map.195
  411.0 3.3 collective-permute-done.45
  415.8 9.3 %collective-permute-done.49 = bf16[4,128,256]{2,1,0:T(8,128)(2,1)S(1)} collective-permute-done((bf16[4,128,256]{2,1,0:T(8,128)(2,1)S(1)}, bf16[4,128,256]{2,1,0:T(8,128)(2,1)S(1)}, u32[]{:S(2)}, u32[]{:S(2)}) %collective-permute-start.49) | collective-permute-done | bytes 262176 | tf_op jit(solution)/shard_map/ppermute | solution.py:871
  428.6 11.2 %shard_map.192 = (bf16[256,512]{1,0:T(8,128)(2,1)S(1)}, bf16[256,512]{1,0:T(8,128)(2,1)S(1)}, bf16[256,1024]{1,0:T(8,128)(2,1)S(1)}, f32[8,512]{1,0:T(8,128)S(1)...) custom-call(f32[256,3072]{1,0:T(8,128)} %copy-done.2, ...), custom_call_target="tpu_custom_call" | custom-call | tf_op jit(solution)/shard_map/pallas_call | solution.py:550
  443.0 4.0 shard_map.196
  447.0 3.1 shard_map.197
  450.1 3.2 shard_map.198
  453.3 4.0 reduce-scatter.4.cloned.1.call-done.refs_0_
  466.4 4.7 shard_map.182
  476.6 11.1 %shard_map.193 = (bf16[256,512]{1,0:T(8,128)(2,1)S(1)}, bf16[256,512]{1,0:T(8,128)(2,1)S(1)}, bf16[256,512]{1,0:T(8,128)(2,1)S(1)}, bf16[256,512]{1,0:T(8,128)(2,1)S(1)}) custom-call(s32[1]{0:T(128)} %bitcast.part_ref, bf16[256,3072]{1,0:T(8,128)(2,1)S(1)} %pad_maximum_fusion.refs_0_, bf16[2048,3072]{1,0:T(8,128)(2,1)} %get-tuple-element.285.refs_1_, ...), custom_call_target="tpu_custom_call" | custom-call | flops 3355443200 | bytes 13107200 | tf_op jit(solution)/shard_map/pallas_call | solution.py:821
  488.5 3.3 collective-permute-start.53
  494.1 5.4 collective-permute-done.52
  499.4 17.1 %collective-permute-done.53 = bf16[256,512]{1,0:T(8,128)(2,1)S(1)} collective-permute-done((bf16[256,512]{1,0:T(8,128)(2,1)S(1)}, bf16[256,512]{1,0:T(8,128)(2,1)S(1)}, u32[]{:S(2)}, u32[]{:S(2)}) %collective-permute-start.53) | collective-permute-done | bytes 262176 | tf_op jit(solution)/shard_map/ppermute | solution.py:838
  518.0 5.2 collective-permute-start.55
  532.6 6.4 collective-permute-done.59
  540.6 2.6 fusion.13
  543.1 3.5 collective-permute-done.60
  546.8 4.9 copy-done
  551.7 4.8 copy-done.5
  556.5 15.6 %shard_map.201 = (f32[44,65536]{1,0:T(8,128)}, f32[44,65536]{1,0:T(8,128)}, f32[44,65536]{1,0:T(8,128)}, f32[44,65536]{1,0:T(8,128)}, bf16[44,65536]{1,0:T(8,128)(2,1)}) custom-call(s32[1]{0:T(128)} %bitcast.88.first_ref, s32[48]{0:T(128)S(1)} %copy-done.47, s32[48]{0:T(128)S(1)} %get-tuple-element.400.sources_ref, s32[48]{0:T(128)S(1)} %get-tuple-element.399.rows_ref, ...), custom_call_target="tpu_custom_call" | custom-call | flops 57671680 | bytes 46137344 | tf_op jit(solution)/shard_map/pallas_call | solution.py:1073
  572.1 47.8 %reduce-scatter.6.cloned.1.call-done.refs_2_ = bf16[24,512,128]{2,1,0:T(8,128)(2,1)} async-done(((bf16[192,512,128]{2,1,0:T(8,128)(2,1)}), bf16[24,512,128]{2,1,0:T(8,128)(2,1)}) %reduce-scatter.6.cloned.1.call-update) | async-done | bytes 3145744 | tf_op jit(solution)/shard_map/reduce_scatter | solution.py:1476
  619.9 4.8 while.42
  624.7 4.6 copy-done.1
  629.3 4.6 copy-done.6
  633.9 23.2 %shard_map.202 = (f32[44,65536]{1,0:T(8,128)}, f32[44,65536]{1,0:T(8,128)}, f32[44,65536]{1,0:T(8,128)}, f32[44,65536]{1,0:T(8,128)}, bf16[44,65536]{1,0:T(8,128)(2,1)}) custom-call(s32[1]{0:T(128)} %bitcast.88.first_ref, s32[48]{0:T(128)S(1)} %copy-done.47, ...), custom_call_target="tpu_custom_call", output_to_operand_aliasing={{0}: (14, {}), {1}: (15, {}), {2}: (16, {}), {3}: (17, {}),... | custom-call | flops 57671680 | bytes 46137344 | tf_op jit(solution)/shard_map/pallas_call | solution.py:1073
  (500 shorter events, 129.0 us)
Async XLA Ops:
  7.2 144.3 %all-gather.5.cloned.1.call-start = ((), (), s32[]{:S(2)}) async-start(), calls=%async_computation.3 | async-start | bytes 28311552 | tf_op jit(solution)/shard_map/all_gather | solution.py:1288
  24.7 27.2 %collective-permute-start.5 = (bf16[1,1088]{1,0:T(2,128)(2,1)S(1)}, bf16[1,1088]{1,0:T(2,128)(2,1)S(1)}, u32[]{:S(2)}, u32[]{:S(2)}) collective-permute-start(bf16[1,1088]{1,0:T(2,128)(2,1)S(1)} %get-tuple-element.402), channel_id=1, source_target_pairs={{0,8},{8,0},{16,24},{24,16},{1,9},{9,1},{17,25},{25,17},{2,10},{10... | collective-permute-start | bytes 6536 | tf_op jit(solution)/shard_map/ppermute | solution.py:838
  27.7 24.2 %collective-permute-start.6 = (bf16[1,1088]{1,0:T(2,128)(2,1)S(1)}, bf16[1,1088]{1,0:T(2,128)(2,1)S(1)}, u32[]{:S(2)}, u32[]{:S(2)}) collective-permute-start(bf16[1,1088]{1,0:T(2,128)(2,1)S(1)} %get-tuple-element.402), channel_id=1, source_target_pairs={{0,16},{8,24},{16,0},{24,8},{1,17},{9,25},{17,1},{25,9},{2,18},{10... | collective-permute-start | bytes 6536 | tf_op jit(solution)/shard_map/ppermute | solution.py:838
  30.3 21.6 %collective-permute-start.7 = (bf16[1,1088]{1,0:T(2,128)(2,1)S(1)}, bf16[1,1088]{1,0:T(2,128)(2,1)S(1)}, u32[]{:S(2)}, u32[]{:S(2)}) collective-permute-start(bf16[1,1088]{1,0:T(2,128)(2,1)S(1)} %get-tuple-element.402), channel_id=1, source_target_pairs={{0,24},{8,16},{16,8},{24,0},{1,25},{9,17},{17,9},{25,1},{2,26},{10... | collective-permute-start | bytes 6536 | tf_op jit(solution)/shard_map/ppermute | solution.py:838
  30.3 38.8 %collective-permute-start.2 = (bf16[256,512]{1,0:T(8,128)(2,1)S(1)}, bf16[256,512]{1,0:T(8,128)(2,1)S(1)}, u32[]{:S(2)}, u32[]{:S(2)}) collective-permute-start(bf16[256,512]{1,0:T(8,128)(2,1)S(1)} %copy-done.68), channel_id=1, source_target_pairs={{0,8},{8,0},{16,24},{24,16},{1,9},{9,1},{17,25},{25,17},{2,10},{10... | collective-permute-start | bytes 786440 | tf_op jit(solution)/shard_map/ppermute | solution.py:838
  48.5 23.8 %collective-permute-start.3 = (bf16[256,512]{1,0:T(8,128)(2,1)S(1)}, bf16[256,512]{1,0:T(8,128)(2,1)S(1)}, u32[]{:S(2)}, u32[]{:S(2)}) collective-permute-start(bf16[256,512]{1,0:T(8,128)(2,1)S(1)} %copy-done.68), channel_id=1, source_target_pairs={{0,16},{8,24},{16,0},{24,8},{1,17},{9,25},{17,1},{25,9},{2,18},{10... | collective-permute-start | bytes 786440 | tf_op jit(solution)/shard_map/ppermute | solution.py:838
  52.5 6.2 collective-permute-start.8
  52.6 6.1 collective-permute-start.9
  53.7 7.4 %collective-permute-start.11 = (bf16[242,128]{1,0:T(8,128)(2,1)S(1)}, bf16[242,128]{1,0:T(8,128)(2,1)S(1)}, u32[]{:S(2)}, u32[]{:S(2)}) collective-permute-start(bf16[242,128]{1,0:T(8,128)(2,1)S(1)} %bitcast.232), channel_id=1, source_target_pairs={{0,4},{1,5},{2,6},{3,7},{4,0},{5,1},{6,2},{7,3},{8,12},{9,13},{10,... | collective-permute-start | bytes 185864 | tf_op jit(solution)/shard_map/ppermute | solution.py:871
  58.8 2.5 collective-permute-start.10
  58.8 7.1 %collective-permute-start.13 = (bf16[242,128]{1,0:T(8,128)(2,1)S(1)}, bf16[242,128]{1,0:T(8,128)(2,1)S(1)}, u32[]{:S(2)}, u32[]{:S(2)}) collective-permute-start(bf16[242,128]{1,0:T(8,128)(2,1)S(1)} %bitcast.233), channel_id=1, source_target_pairs={{0,6},{1,7},{2,4},{3,5},{4,2},{5,3},{6,0},{7,1},{8,14},{9,15},{10,... | collective-permute-start | bytes 185864 | tf_op jit(solution)/shard_map/ppermute | solution.py:871
  61.1 4.8 collective-permute-start.12
  61.3 11.0 %collective-permute-start.4 = (bf16[256,512]{1,0:T(8,128)(2,1)S(1)}, bf16[256,512]{1,0:T(8,128)(2,1)S(1)}, u32[]{:S(2)}, u32[]{:S(2)}) collective-permute-start(bf16[256,512]{1,0:T(8,128)(2,1)S(1)} %copy-done.68), channel_id=1, source_target_pairs={{0,24},{8,16},{16,8},{24,0},{1,25},{9,17},{17,9},{25,1},{2,26},{10... | collective-permute-start | bytes 786440 | tf_op jit(solution)/shard_map/ppermute | solution.py:838
  65.9 13.9 %collective-permute-start.15 = (bf16[256,512]{1,0:T(8,128)(2,1)}, bf16[256,512]{1,0:T(8,128)(2,1)}, u32[]{:S(2)}, u32[]{:S(2)}) collective-permute-start(bf16[256,512]{1,0:T(8,128)(2,1)} %param.21), channel_id=1, source_target_pairs={{0,8},{8,0},{16,24},{24,16},{1,9},{9,1},{17,25},{25,17},{2,10},{10... | collective-permute-start | bytes 786440 | tf_op jit(solution)/shard_map/ppermute | solution.py:838
  69.0 23.8 %collective-permute-start.16 = (bf16[256,512]{1,0:T(8,128)(2,1)}, bf16[256,512]{1,0:T(8,128)(2,1)}, u32[]{:S(2)}, u32[]{:S(2)}) collective-permute-start(bf16[256,512]{1,0:T(8,128)(2,1)} %param.21), channel_id=1, source_target_pairs={{0,16},{8,24},{16,0},{24,8},{1,17},{9,25},{17,1},{25,9},{2,18},{10... | collective-permute-start | bytes 786440 | tf_op jit(solution)/shard_map/ppermute | solution.py:838
  69.1 23.7 %collective-permute-start.17 = (bf16[256,512]{1,0:T(8,128)(2,1)}, bf16[256,512]{1,0:T(8,128)(2,1)}, u32[]{:S(2)}, u32[]{:S(2)}) collective-permute-start(bf16[256,512]{1,0:T(8,128)(2,1)} %param.21), channel_id=1, source_target_pairs={{0,24},{8,16},{16,8},{24,0},{1,25},{9,17},{17,9},{25,1},{2,26},{10... | collective-permute-start | bytes 786440 | tf_op jit(solution)/shard_map/ppermute | solution.py:838
  72.3 25.0 %collective-permute-start.1 = (bf16[4,512,128]{2,1,0:T(8,128)(2,1)}, bf16[4,512,128]{2,1,0:T(8,128)(2,1)}, u32[]{:S(2)}, u32[]{:S(2)}) collective-permute-start(bf16[4,512,128]{2,1,0:T(8,128)(2,1)} %slice.263), channel_id=1, source_target_pairs={{0,1},{1,0},{2,3},{3,2},{4,5},{5,4},{6,7},{7,6},{8,9},{9,8},{10,11... | collective-permute-start | bytes 1572872 | tf_op jit(solution)/shard_map/ppermute | solution.py:1292
  151.4 124.6 %all-gather.7.cloned.1.call-start = ((), (), s32[]{:S(2)}) async-start(), calls=%async_computation.4 | async-start | bytes 18874368 | tf_op jit(solution)/shard_map/all_gather | solution.py:1333
  168.5 4.7 collective-permute-start.18
  193.1 39.0 %collective-permute-start.19 = (bf16[4,128,384]{2,1,0:T(8,128)(2,1)}, bf16[4,128,384]{2,1,0:T(8,128)(2,1)}, u32[]{:S(2)}, u32[]{:S(2)}) collective-permute-start(bf16[4,128,384]{2,1,0:T(8,128)(2,1)} %get-tuple-element.226), channel_id=1, source_target_pairs={{0,1},{1,0},{2,3},{3,2},{4,5},{5,4},{6,7},{7,6},{8,9},{9,8},{10,11... | collective-permute-start | bytes 1179656 | tf_op jit(solution)/shard_map/ppermute | solution.py:871
  194.5 20.5 %collective-permute-start.20 = (bf16[4,128,384]{2,1,0:T(8,128)(2,1)}, bf16[4,128,384]{2,1,0:T(8,128)(2,1)}, u32[]{:S(2)}, u32[]{:S(2)}) collective-permute-start(bf16[4,128,384]{2,1,0:T(8,128)(2,1)} %get-tuple-element.226), channel_id=1, source_target_pairs={{0,2},{1,3},{2,0},{3,1},{4,6},{5,7},{6,4},{7,5},{8,10},{9,11},{10,... | collective-permute-start | bytes 1179656 | tf_op jit(solution)/shard_map/ppermute | solution.py:871
  195.9 21.7 %collective-permute-start.22 = (bf16[4,128,384]{2,1,0:T(8,128)(2,1)}, bf16[4,128,384]{2,1,0:T(8,128)(2,1)}, u32[]{:S(2)}, u32[]{:S(2)}) collective-permute-start(bf16[4,128,384]{2,1,0:T(8,128)(2,1)} %get-tuple-element.226), channel_id=1, source_target_pairs={{0,4},{1,5},{2,6},{3,7},{4,0},{5,1},{6,2},{7,3},{8,12},{9,13},{10,... | collective-permute-start | bytes 1179656 | tf_op jit(solution)/shard_map/ppermute | solution.py:871
  196.4 35.7 %collective-permute-start.24 = (bf16[4,128,384]{2,1,0:T(8,128)(2,1)}, bf16[4,128,384]{2,1,0:T(8,128)(2,1)}, u32[]{:S(2)}, u32[]{:S(2)}) collective-permute-start(bf16[4,128,384]{2,1,0:T(8,128)(2,1)} %get-tuple-element.226), channel_id=1, source_target_pairs={{0,6},{1,7},{2,4},{3,5},{4,2},{5,3},{6,0},{7,1},{8,14},{9,15},{10,... | collective-permute-start | bytes 1179656 | tf_op jit(solution)/shard_map/ppermute | solution.py:871
  215.0 19.2 %collective-permute-start.21 = (bf16[4,128,384]{2,1,0:T(8,128)(2,1)}, bf16[4,128,384]{2,1,0:T(8,128)(2,1)S(1)}, u32[]{:S(2)}, u32[]{:S(2)}) collective-permute-start(bf16[4,128,384]{2,1,0:T(8,128)(2,1)} %collective-permute-done.20), channel_id=1, source_target_pairs={{0,1},{1,0},{2,3},{3,2},{4,5},{5,4},{6,7},{7,6},{8,9},{9,8},{10,11... | collective-permute-start | bytes 1179656 | tf_op jit(solution)/shard_map/ppermute | solution.py:871
  217.5 17.8 %collective-permute-start.23 = (bf16[4,128,384]{2,1,0:T(8,128)(2,1)}, bf16[4,128,384]{2,1,0:T(8,128)(2,1)S(1)}, u32[]{:S(2)}, u32[]{:S(2)}) collective-permute-start(bf16[4,128,384]{2,1,0:T(8,128)(2,1)} %collective-permute-done.22), channel_id=1, source_target_pairs={{0,1},{1,0},{2,3},{3,2},{4,5},{5,4},{6,7},{7,6},{8,9},{9,8},{10,11... | collective-permute-start | bytes 1179656 | tf_op jit(solution)/shard_map/ppermute | solution.py:871
  232.1 4.4 collective-permute-start.25
  244.3 14.5 %collective-permute-start.26 = (bf16[256,512]{1,0:T(8,128)(2,1)S(1)}, bf16[256,512]{1,0:T(8,128)(2,1)S(1)}, u32[]{:S(2)}, u32[]{:S(2)}) collective-permute-start(bf16[256,512]{1,0:T(8,128)(2,1)S(1)} %get-tuple-element.232), channel_id=1, source_target_pairs={{0,8},{8,0},{16,24},{24,16},{1,9},{9,1},{17,25},{25,17},{2,10},{10... | collective-permute-start | bytes 786440 | tf_op jit(solution)/shard_map/ppermute | solution.py:838
  246.2 21.3 %collective-permute-start.27 = (bf16[256,512]{1,0:T(8,128)(2,1)S(1)}, bf16[256,512]{1,0:T(8,128)(2,1)S(1)}, u32[]{:S(2)}, u32[]{:S(2)}) collective-permute-start(bf16[256,512]{1,0:T(8,128)(2,1)S(1)} %get-tuple-element.233), channel_id=1, source_target_pairs={{0,16},{8,24},{16,0},{24,8},{1,17},{9,25},{17,1},{25,9},{2,18},{10... | collective-permute-start | bytes 786440 | tf_op jit(solution)/shard_map/ppermute | solution.py:838
  248.6 18.9 %collective-permute-start.28 = (bf16[256,512]{1,0:T(8,128)(2,1)S(1)}, bf16[256,512]{1,0:T(8,128)(2,1)S(1)}, u32[]{:S(2)}, u32[]{:S(2)}) collective-permute-start(bf16[256,512]{1,0:T(8,128)(2,1)S(1)} %get-tuple-element.234), channel_id=1, source_target_pairs={{0,24},{8,16},{16,8},{24,0},{1,25},{9,17},{17,9},{25,1},{2,26},{10... | collective-permute-start | bytes 786440 | tf_op jit(solution)/shard_map/ppermute | solution.py:838
  267.7 23.9 %collective-permute-start.29 = (bf16[256,512]{1,0:T(8,128)(2,1)S(1)}, bf16[256,512]{1,0:T(8,128)(2,1)S(1)}, u32[]{:S(2)}, u32[]{:S(2)}) collective-permute-start(bf16[256,512]{1,0:T(8,128)(2,1)S(1)} %fusion.40), channel_id=1, source_target_pairs={{0,8},{8,0},{16,24},{24,16},{1,9},{9,1},{17,25},{25,17},{2,10},{10... | collective-permute-start | bytes 786440 | tf_op jit(solution)/shard_map/ppermute | solution.py:838
  273.6 21.4 %collective-permute-start.30 = (bf16[256,512]{1,0:T(8,128)(2,1)S(1)}, bf16[256,512]{1,0:T(8,128)(2,1)S(1)}, u32[]{:S(2)}, u32[]{:S(2)}) collective-permute-start(bf16[256,512]{1,0:T(8,128)(2,1)S(1)} %fusion.40), channel_id=1, source_target_pairs={{0,16},{8,24},{16,0},{24,8},{1,17},{9,25},{17,1},{25,9},{2,18},{10... | collective-permute-start | bytes 786440 | tf_op jit(solution)/shard_map/ppermute | solution.py:838
  274.6 20.4 %collective-permute-start.31 = (bf16[256,512]{1,0:T(8,128)(2,1)S(1)}, bf16[256,512]{1,0:T(8,128)(2,1)S(1)}, u32[]{:S(2)}, u32[]{:S(2)}) collective-permute-start(bf16[256,512]{1,0:T(8,128)(2,1)S(1)} %fusion.40), channel_id=1, source_target_pairs={{0,24},{8,16},{16,8},{24,0},{1,25},{9,17},{17,9},{25,1},{2,26},{10... | collective-permute-start | bytes 786440 | tf_op jit(solution)/shard_map/ppermute | solution.py:838
  276.1 181.2 %reduce-scatter.4.cloned.1.call-start = ((), (), s32[]{:S(2)}) async-start(), calls=%async_computation.5 | async-start | bytes 18874368 | tf_op jit(solution)/shard_map/reduce_scatter | solution.py:1420
  326.1 293.9 %reduce-scatter.6.cloned.1.call-start = ((), (), s32[]{:S(2)}) async-start(), calls=%async_computation.6 | async-start | bytes 28311552 | tf_op jit(solution)/shard_map/reduce_scatter | solution.py:1476
  335.2 13.9 %collective-permute-start.35 = (bf16[256,512]{1,0:T(8,128)(2,1)S(1)}, bf16[256,512]{1,0:T(8,128)(2,1)S(1)}, u32[]{:S(2)}, u32[]{:S(2)}) collective-permute-start(bf16[256,512]{1,0:T(8,128)(2,1)S(1)} %get-tuple-element.264), channel_id=1, source_target_pairs={{0,8},{8,0},{16,24},{24,16},{1,9},{9,1},{17,25},{25,17},{2,10},{10... | collective-permute-start | bytes 786440 | tf_op jit(solution)/shard_map/ppermute | solution.py:838
  340.0 21.4 %collective-permute-start.36 = (bf16[256,512]{1,0:T(8,128)(2,1)S(1)}, bf16[256,512]{1,0:T(8,128)(2,1)S(1)}, u32[]{:S(2)}, u32[]{:S(2)}) collective-permute-start(bf16[256,512]{1,0:T(8,128)(2,1)S(1)} %get-tuple-element.265), channel_id=1, source_target_pairs={{0,16},{8,24},{16,0},{24,8},{1,17},{9,25},{17,1},{25,9},{2,18},{10... | collective-permute-start | bytes 786440 | tf_op jit(solution)/shard_map/ppermute | solution.py:838
  340.9 20.4 %collective-permute-start.37 = (bf16[256,512]{1,0:T(8,128)(2,1)S(1)}, bf16[256,512]{1,0:T(8,128)(2,1)S(1)}, u32[]{:S(2)}, u32[]{:S(2)}) collective-permute-start(bf16[256,512]{1,0:T(8,128)(2,1)S(1)} %get-tuple-element.266), channel_id=1, source_target_pairs={{0,24},{8,16},{16,8},{24,0},{1,25},{9,17},{17,9},{25,1},{2,26},{10... | collective-permute-start | bytes 786440 | tf_op jit(solution)/shard_map/ppermute | solution.py:838
  362.2 10.7 %collective-permute-start.38 = (f32[2,128]{1,0:T(2,128)S(1)}, f32[2,128]{1,0:T(2,128)S(1)}, u32[]{:S(2)}, u32[]{:S(2)}) collective-permute-start(f32[2,128]{1,0:T(2,128)S(1)} %bitcast.255), channel_id=1, source_target_pairs={{0,8},{8,0},{16,24},{24,16},{1,9},{9,1},{17,25},{25,17},{2,10},{10... | collective-permute-start | bytes 3080 | tf_op jit(solution)/shard_map/ppermute | solution.py:838
  367.4 7.0 %collective-permute-start.39 = (f32[2,128]{1,0:T(2,128)S(1)}, f32[2,128]{1,0:T(2,128)S(1)}, u32[]{:S(2)}, u32[]{:S(2)}) collective-permute-start(f32[2,128]{1,0:T(2,128)S(1)} %bitcast.256), channel_id=1, source_target_pairs={{0,16},{8,24},{16,0},{24,8},{1,17},{9,25},{17,1},{25,9},{2,18},{10... | collective-permute-start | bytes 3080 | tf_op jit(solution)/shard_map/ppermute | solution.py:838
  368.4 6.0 collective-permute-start.40
  369.9 10.7 %collective-permute-start.41 = (bf16[256,512]{1,0:T(8,128)(2,1)S(1)}, bf16[256,512]{1,0:T(8,128)(2,1)S(1)}, u32[]{:S(2)}, u32[]{:S(2)}) collective-permute-start(bf16[256,512]{1,0:T(8,128)(2,1)S(1)} %convert_element_type.208), channel_id=1, source_target_pairs={{0,8},{8,0},{16,24},{24,16},{1,9},{9,1},{17,25},{25,17},{2,10},{10... | collective-permute-start | bytes 786440 | tf_op jit(solution)/shard_map/ppermute | solution.py:838
  371.0 19.6 %collective-permute-start.42 = (bf16[256,512]{1,0:T(8,128)(2,1)S(1)}, bf16[256,512]{1,0:T(8,128)(2,1)S(1)}, u32[]{:S(2)}, u32[]{:S(2)}) collective-permute-start(bf16[256,512]{1,0:T(8,128)(2,1)S(1)} %convert_element_type.208), channel_id=1, source_target_pairs={{0,16},{8,24},{16,0},{24,8},{1,17},{9,25},{17,1},{25,9},{2,18},{10... | collective-permute-start | bytes 786440 | tf_op jit(solution)/shard_map/ppermute | solution.py:838
  372.9 17.7 %collective-permute-start.43 = (bf16[256,512]{1,0:T(8,128)(2,1)S(1)}, bf16[256,512]{1,0:T(8,128)(2,1)S(1)}, u32[]{:S(2)}, u32[]{:S(2)}) collective-permute-start(bf16[256,512]{1,0:T(8,128)(2,1)S(1)} %convert_element_type.208), channel_id=1, source_target_pairs={{0,24},{8,16},{16,8},{24,0},{1,25},{9,17},{17,9},{25,1},{2,26},{10... | collective-permute-start | bytes 786440 | tf_op jit(solution)/shard_map/ppermute | solution.py:838
  399.4 25.6 %collective-permute-start.44 = (bf16[4,128,256]{2,1,0:T(8,128)(2,1)S(1)}, bf16[4,128,256]{2,1,0:T(8,128)(2,1)S(1)}, u32[]{:S(2)}, u32[]{:S(2)}) collective-permute-start(bf16[4,128,256]{2,1,0:T(8,128)(2,1)S(1)} %get-tuple-element.274), channel_id=1, source_target_pairs={{0,1},{1,0},{2,3},{3,2},{4,5},{5,4},{6,7},{7,6},{8,9},{9,8},{10,11... | collective-permute-start | bytes 786440 | tf_op jit(solution)/shard_map/ppermute | solution.py:871
  399.5 14.8 %collective-permute-start.45 = (bf16[4,128,256]{2,1,0:T(8,128)(2,1)S(1)}, bf16[4,128,256]{2,1,0:T(8,128)(2,1)S(1)}, u32[]{:S(2)}, u32[]{:S(2)}) collective-permute-start(bf16[4,128,256]{2,1,0:T(8,128)(2,1)S(1)} %get-tuple-element.274), channel_id=1, source_target_pairs={{0,2},{1,3},{2,0},{3,1},{4,6},{5,7},{6,4},{7,5},{8,10},{9,11},{10,... | collective-permute-start | bytes 786440 | tf_op jit(solution)/shard_map/ppermute | solution.py:871
  400.2 15.6 %collective-permute-start.47 = (bf16[4,128,256]{2,1,0:T(8,128)(2,1)S(1)}, bf16[4,128,256]{2,1,0:T(8,128)(2,1)S(1)}, u32[]{:S(2)}, u32[]{:S(2)}) collective-permute-start(bf16[4,128,256]{2,1,0:T(8,128)(2,1)S(1)} %get-tuple-element.274), channel_id=1, source_target_pairs={{0,4},{1,5},{2,6},{3,7},{4,0},{5,1},{6,2},{7,3},{8,12},{9,13},{10,... | collective-permute-start | bytes 786440 | tf_op jit(solution)/shard_map/ppermute | solution.py:871
  402.7 22.3 %collective-permute-start.49 = (bf16[4,128,256]{2,1,0:T(8,128)(2,1)S(1)}, bf16[4,128,256]{2,1,0:T(8,128)(2,1)S(1)}, u32[]{:S(2)}, u32[]{:S(2)}) collective-permute-start(bf16[4,128,256]{2,1,0:T(8,128)(2,1)S(1)} %get-tuple-element.274), channel_id=1, source_target_pairs={{0,6},{1,7},{2,4},{3,5},{4,2},{5,3},{6,0},{7,1},{8,14},{9,15},{10,... | collective-permute-start | bytes 786440 | tf_op jit(solution)/shard_map/ppermute | solution.py:871
  414.3 10.8 %collective-permute-start.46 = (bf16[4,128,256]{2,1,0:T(8,128)(2,1)S(1)}, bf16[4,128,256]{2,1,0:T(8,128)(2,1)S(1)}, u32[]{:S(2)}, u32[]{:S(2)}) collective-permute-start(bf16[4,128,256]{2,1,0:T(8,128)(2,1)S(1)} %collective-permute-done.45), channel_id=1, source_target_pairs={{0,1},{1,0},{2,3},{3,2},{4,5},{5,4},{6,7},{7,6},{8,9},{9,8},{10,11... | collective-permute-start | bytes 786440 | tf_op jit(solution)/shard_map/ppermute | solution.py:871
  415.8 9.4 %collective-permute-start.48 = (bf16[4,128,256]{2,1,0:T(8,128)(2,1)S(1)}, bf16[4,128,256]{2,1,0:T(8,128)(2,1)S(1)}, u32[]{:S(2)}, u32[]{:S(2)}) collective-permute-start(bf16[4,128,256]{2,1,0:T(8,128)(2,1)S(1)} %collective-permute-done.47), channel_id=1, source_target_pairs={{0,1},{1,0},{2,3},{3,2},{4,5},{5,4},{6,7},{7,6},{8,9},{9,8},{10,11... | collective-permute-start | bytes 786440 | tf_op jit(solution)/shard_map/ppermute | solution.py:871
  425.0 1.5 collective-permute-start.50
  439.9 3.1 collective-permute-start.51
  471.2 20.5 %collective-permute-start.32 = (bf16[256,512]{1,0:T(8,128)(2,1)S(1)}, bf16[256,512]{1,0:T(8,128)(2,1)S(1)}, u32[]{:S(2)}, u32[]{:S(2)}) collective-permute-start(bf16[256,512]{1,0:T(8,128)(2,1)S(1)} %get-tuple-element.248), channel_id=1, source_target_pairs={{0,8},{8,0},{16,24},{24,16},{1,9},{9,1},{17,25},{25,17},{2,10},{10... | collective-permute-start | bytes 786440 | tf_op jit(solution)/shard_map/ppermute | solution.py:838
  472.7 21.4 %collective-permute-start.33 = (bf16[256,512]{1,0:T(8,128)(2,1)S(1)}, bf16[256,512]{1,0:T(8,128)(2,1)S(1)}, u32[]{:S(2)}, u32[]{:S(2)}) collective-permute-start(bf16[256,512]{1,0:T(8,128)(2,1)S(1)} %get-tuple-element.249), channel_id=1, source_target_pairs={{0,16},{8,24},{16,0},{24,8},{1,17},{9,25},{17,1},{25,9},{2,18},{10... | collective-permute-start | bytes 786440 | tf_op jit(solution)/shard_map/ppermute | solution.py:838
  475.1 18.9 %collective-permute-start.34 = (bf16[256,512]{1,0:T(8,128)(2,1)S(1)}, bf16[256,512]{1,0:T(8,128)(2,1)S(1)}, u32[]{:S(2)}, u32[]{:S(2)}) collective-permute-start(bf16[256,512]{1,0:T(8,128)(2,1)S(1)} %get-tuple-element.250), channel_id=1, source_target_pairs={{0,24},{8,16},{16,8},{24,0},{1,25},{9,17},{17,9},{25,1},{2,26},{10... | collective-permute-start | bytes 786440 | tf_op jit(solution)/shard_map/ppermute | solution.py:838
  487.8 11.7 %collective-permute-start.52 = (bf16[256,512]{1,0:T(8,128)(2,1)S(1)}, bf16[256,512]{1,0:T(8,128)(2,1)S(1)}, u32[]{:S(2)}, u32[]{:S(2)}) collective-permute-start(bf16[256,512]{1,0:T(8,128)(2,1)S(1)} %get-tuple-element.289), channel_id=1, source_target_pairs={{0,8},{8,0},{16,24},{24,16},{1,9},{9,1},{17,25},{25,17},{2,10},{10... | collective-permute-start | bytes 786440 | tf_op jit(solution)/shard_map/ppermute | solution.py:838
  488.5 28.1 %collective-permute-start.53 = (bf16[256,512]{1,0:T(8,128)(2,1)S(1)}, bf16[256,512]{1,0:T(8,128)(2,1)S(1)}, u32[]{:S(2)}, u32[]{:S(2)}) collective-permute-start(bf16[256,512]{1,0:T(8,128)(2,1)S(1)} %get-tuple-element.290), channel_id=1, source_target_pairs={{0,16},{8,24},{16,0},{24,8},{1,17},{9,25},{17,1},{25,9},{2,18},{10... | collective-permute-start | bytes 786440 | tf_op jit(solution)/shard_map/ppermute | solution.py:838
  491.7 24.8 %collective-permute-start.54 = (bf16[256,512]{1,0:T(8,128)(2,1)S(1)}, bf16[256,512]{1,0:T(8,128)(2,1)S(1)}, u32[]{:S(2)}, u32[]{:S(2)}) collective-permute-start(bf16[256,512]{1,0:T(8,128)(2,1)S(1)} %get-tuple-element.291), channel_id=1, source_target_pairs={{0,24},{8,16},{16,8},{24,0},{1,25},{9,17},{17,9},{25,1},{2,26},{10... | collective-permute-start | bytes 786440 | tf_op jit(solution)/shard_map/ppermute | solution.py:838
  518.0 8.9 %collective-permute-start.55 = (f32[4,128]{1,0:T(4,128)S(1)}, f32[4,128]{1,0:T(4,128)S(1)}, u32[]{:S(2)}, u32[]{:S(2)}) collective-permute-start(f32[4,128]{1,0:T(4,128)S(1)} %pad_maximum_fusion.14), channel_id=1, source_target_pairs={{0,8},{8,0},{16,24},{24,16},{1,9},{9,1},{17,25},{25,17},{2,10},{10... | collective-permute-start | bytes 6152 | tf_op jit(solution)/shard_map/ppermute | solution.py:838
  523.2 4.5 collective-permute-start.56
  524.1 5.4 collective-permute-start.57
  529.7 1.4 collective-permute-start.58
  531.1 7.9 %collective-permute-start.59 = (f32[208,128]{1,0:T(8,128)S(1)}, f32[208,128]{1,0:T(8,128)S(1)}, u32[]{:S(2)}, u32[]{:S(2)}) collective-permute-start(f32[208,128]{1,0:T(8,128)S(1)} %bitcast_add_fusion), channel_id=1, source_target_pairs={{0,2},{1,3},{2,0},{3,1},{4,6},{5,7},{6,4},{7,5},{8,10},{9,11},{10,... | collective-permute-start | bytes 319496 | tf_op jit(solution)/shard_map/ppermute | solution.py:1522
  539.0 7.6 %collective-permute-start.60 = (f32[208,128]{1,0:T(8,128)S(1)}, f32[208,128]{1,0:T(8,128)S(1)}, u32[]{:S(2)}, u32[]{:S(2)}) collective-permute-start(f32[208,128]{1,0:T(8,128)S(1)} %fusion.93), channel_id=1, source_target_pairs={{0,4},{1,5},{2,6},{3,7},{4,0},{5,1},{6,2},{7,3},{8,12},{9,13},{10,... | collective-permute-start | bytes 319496 | tf_op jit(solution)/shard_map/ppermute | solution.py:1522
  621.8 2.1 collective-permute-start
  (112 other events, 1997.8 us)
Sparse Core Ops, SparseCore 0:
  20.9 130.4 all-gather.4
  154.2 106.7 all-gather.6
  326.2 131.0 reduce-scatter.3
  460.7 159.1 reduce-scatter.5
